TPU v7x, 256 devices: a whole 4x4x8 slice. The times are simulated.
256 devices in a mesh: rows: 16 (over x, y), leaf: 16 (over z, core).
Axes of the slice: x: 4, y: 4, z: 8, core: 2. Of those that a mesh axis runs over, the one named last changes fastest.
Arguments:
- right_side: float32 [131072, 128], P(('rows', 'leaf')), may hold values from -6 to 6
- reflectors: float32 [131072, 2048], P(('rows', 'leaf')), may hold values from -0.0625 to 0.0625
- leaf_factor: float32 [16, 2048, 2048], P('rows', None, 'leaf'), may hold values from -1 to 1, as said below
- node_reflect: float32 [16, 2048, 2048], P('rows', 'leaf'), may hold values from -0.125 to 0.125
- node_factor: float32 [16, 2048, 2048], P('rows', None, 'leaf'), may hold values from -1 to 1, as said below
- upper_blocks: float32 [2048, 2048], P('leaf'), may hold values from -1 to 1, as said below
- block_inverse: float32 [2048, 128], P('leaf'), may hold values from -2 to 2, as said below
Outputs:
- rotated: float32 [131072, 128], P(('rows', 'leaf'))
- solution: float32 [2048, 128], P('leaf', 'rows')
Inputs may be any that keep to these rules, and one draw needn't show every extreme that they name: `leaf_factor`: each [2048, 2048] slot is upper triangular, with diagonal between 0.5 and 1. `node_factor`: each [2048, 2048] slot is upper triangular, with diagonal between 0.5 and 1. `upper_blocks`: zero in every 128 x 128 block on or below the block diagonal. `block_inverse`: each stacked 128 x 128 block is upper triangular, with positive diagonal.
All inputs are finite; a program needn't handle non-finite values.
Results may differ from a plain program's by a relative error of at most 0.0003.
Values sent between devices are 32-bit elements; how exact they have to be, the bound alone decides.
No kernel may reach another device: no remote copies, remote signals or barrier semaphores. Data moves between devices by JAX's collectives and lax.ppermute only.
A program may use at most 128 MiB of HBM per device.

v0:
```python
import functools

import jax
import jax.numpy as jnp
from jax import lax
from jax.experimental import pallas as pl
from jax.experimental.pallas import tpu as pltpu
from jax.sharding import PartitionSpec as P

SIDE = 128
SPLIT = (((1,), (0,)), ((), ()))
LIMIT = 56 * 1024 * 1024


def halves(value):
    high = value.astype(jnp.bfloat16)
    low = (value - high.astype(jnp.float32)).astype(jnp.bfloat16)
    return high, low


def once(left, right):
    return lax.dot_general(left, right, SPLIT, preferred_element_type=jnp.float32)


def thrice(left, right):
    return once(left[0], right[0]) + (once(left[0], right[1]) + once(left[1], right[0]))


def full(left, right):
    return lax.dot_general(
        left, right, SPLIT, precision=lax.Precision.HIGHEST, preferred_element_type=jnp.float32
    )


def pick(parity, own, other):
    first = parity == 0
    return jnp.where(first, own, other), jnp.where(first, other, own)


smem = pl.BlockSpec(memory_space=pltpu.SMEM)


def params():
    return pltpu.CompilerParams(vmem_limit_bytes=LIMIT)


def shaped(*shape, dtype=jnp.float32):
    return jax.ShapeDtypeStruct(shape, dtype)


def weights_kernel(where_ref, side_ref, vectors_ref, keep_ref, give_ref, high_ref, low_ref):
    @pl.when(pl.program_id(0) == 0)
    def _():
        high, low = halves(side_ref[...].T)
        high_ref[...] = high
        low_ref[...] = low

    out = thrice((high_ref[...], low_ref[...]), halves(vectors_ref[...]))
    first = where_ref[0] == 0
    even, odd = out[:, :SIDE], out[:, SIDE:]
    keep_ref[0] = jnp.where(first, even, odd)
    give_ref[0] = jnp.where(first, odd, even)


def weights_of(where, side, vectors):
    tall, order = vectors.shape
    columns = side.shape[1]
    steps = order // (2 * SIDE)
    block = pl.BlockSpec((1, columns, SIDE), lambda n: (n, 0, 0))
    return pl.pallas_call(
        weights_kernel,
        grid=(steps,),
        in_specs=[
            smem,
            pl.BlockSpec((tall, columns), lambda n: (0, 0)),
            pl.BlockSpec((tall, 2 * SIDE), lambda n: (0, n)),
        ],
        out_specs=[block, block],
        out_shape=[shaped(steps, columns, SIDE)] * 2,
        scratch_shapes=[pltpu.VMEM((columns, tall), jnp.bfloat16)] * 2,
        compiler_params=params(),
        name="weights",
    )(where, side, vectors)


def coeffs_kernel(where_ref, own_ref, other_ref, factor_ref, out_ref):
    parity = where_ref[0]
    steps = own_ref.shape[0]
    total = jnp.zeros(own_ref.shape[1:], jnp.float32)
    for n in range(steps):
        left = jnp.concatenate(pick(parity, own_ref[n], other_ref[n]), axis=1)
        right = factor_ref[2 * n * SIDE:(2 * n + 2) * SIDE, :]
        total = total + thrice(halves(left), halves(right))
    total = total.T
    for n in range(steps):
        out_ref[n] = total


def coeffs_of(where, own, other, factor):
    return pl.pallas_call(
        coeffs_kernel,
        in_specs=[smem] + [pl.BlockSpec(memory_space=pltpu.VMEM)] * 3,
        out_shape=shaped(own.shape[0], SIDE, own.shape[1]),
        compiler_params=params(),
        name="coeffs",
    )(where, own, other, factor)


def lowered_kernel(where_ref, own_ref, other_ref, vectors_ref, side_ref, out_ref, top_ref):
    step = pl.program_id(0)

    @pl.when(step == 0)
    def _():
        out_ref[...] = side_ref[...]

    right = jnp.concatenate(pick(where_ref[0], own_ref[0], other_ref[0]), axis=0)
    out_ref[...] -= thrice(halves(vectors_ref[...]), halves(right))

    @pl.when(step == pl.num_programs(0) - 1)
    def _():
        top_ref[...] = out_ref[:SIDE, :].T


def lowered_of(where, own, other, vectors, side):
    tall, order = vectors.shape
    columns = side.shape[1]
    steps = order // (2 * SIDE)
    block = pl.BlockSpec((1, SIDE, columns), lambda n: (n, 0, 0))
    whole = pl.BlockSpec((tall, columns), lambda n: (0, 0))
    return pl.pallas_call(
        lowered_kernel,
        grid=(steps,),
        in_specs=[smem, block, block, pl.BlockSpec((tall, 2 * SIDE), lambda n: (0, n)), whole],
        out_specs=[whole, pl.BlockSpec((columns, SIDE), lambda n: (0, 0))],
        out_shape=[shaped(tall, columns), shaped(columns, SIDE)],
        compiler_params=params(),
        name="lowered",
    )(where, own, other, vectors, side)


def joint_kernel(where_ref, reflect_ref, short_ref, long_ref, *refs):
    out_refs, scratch = refs[:4], refs[4:]
    reflect_high, reflect_low, panel_high, panel_low, panel = scratch
    step = pl.program_id(0)
    kept = short_ref.shape[1]
    order = reflect_ref.shape[1]

    @pl.when(step == 0)
    def _():
        high, low = halves(reflect_ref[...])
        reflect_high[...] = high
        reflect_low[...] = low

    edge = (step + 1) * SIDE
    row = lax.broadcasted_iota(jnp.int32, (kept, SIDE), 0)
    panel[:, :SIDE] = jnp.zeros((order, SIDE), jnp.float32)
    panel[0:kept, :SIDE] = jnp.where(row < edge, short_ref[0], 0.0)
    panel[0:kept, SIDE:] = long_ref[0]
    rest = order - kept
    start = pl.multiple_of(edge, SIDE)
    tail = short_ref[0, pl.ds(jnp.minimum(start, kept - SIDE), SIDE), :]
    for n in range(rest // SIDE):
        at = pl.multiple_of(jnp.minimum(edge + n * SIDE, kept - SIDE), SIDE)
        piece = short_ref[0, pl.ds(at, SIDE), :]
        inside = edge + n * SIDE < kept - SIDE
        panel[kept + n * SIDE:kept + (n + 1) * SIDE, SIDE:] = jnp.where(inside, piece, 0.0)
    high, low = halves(panel[...])
    panel_high[...] = high
    panel_low[...] = low
    out = thrice((reflect_high[...], reflect_low[...]), (panel_high[...], panel_low[...]))
    own = pl.ds(pl.multiple_of(where_ref[1] * SIDE, SIDE), SIDE)
    mine_high, mine_low = panel_high[own, :], panel_low[own, :]
    out_high, out_low = halves(out)
    for position, ref in enumerate(out_refs):
        side = pl.ds(0, SIDE) if position < 2 else pl.ds(SIDE, SIDE)
        top, bottom = (out_high, mine_high) if position % 2 == 0 else (out_low, mine_low)
        cut = slice(0, SIDE) if position < 2 else slice(SIDE, 2 * SIDE)
        ref[0, 0:SIDE, :] = top[:, cut]
        ref[0, SIDE:2 * SIDE, :] = bottom[:, cut]


def joint_of(where, reflect, packed):
    count, kept, _ = packed.shape
    block, order = reflect.shape
    steps = count // 2
    low_half = pl.BlockSpec((1, 2 * SIDE, SIDE), lambda n: (n, 0, 0))
    high_half = pl.BlockSpec((1, 2 * SIDE, SIDE), lambda n: (steps - 1 - n, 0, 0))
    return pl.pallas_call(
        joint_kernel,
        grid=(steps,),
        in_specs=[
            smem,
            pl.BlockSpec((block, order), lambda n: (0, 0)),
            pl.BlockSpec((1, kept, SIDE), lambda n: (n, 0, 0)),
            pl.BlockSpec((1, kept, SIDE), lambda n: (count - 1 - n, 0, 0)),
        ],
        out_specs=[low_half, low_half, high_half, high_half],
        out_shape=[shaped(steps, 2 * SIDE, SIDE, dtype=jnp.bfloat16)] * 4,
        scratch_shapes=[pltpu.VMEM((block, order), jnp.bfloat16)] * 2
        + [pltpu.VMEM((order, 2 * SIDE), jnp.bfloat16)] * 2
        + [pltpu.VMEM((order, 2 * SIDE), jnp.float32)],
        compiler_params=params(),
        cost_estimate=pl.CostEstimate(
            flops=6 * block * order * order, bytes_accessed=4 * packed.size, transcendentals=0
        ),
        name="joint",
    )(where, reflect, packed, packed)


def level_kernel(where_ref, upper_ref, lower_ref, *refs):
    joint_refs, (keep_ref, give_ref) = refs[:4], refs[4:]
    steps = keep_ref.shape[0]
    first = where_ref[0] == 0
    left = halves(jnp.concatenate([upper_ref[...], lower_ref[...]], axis=1))
    for n in range(steps):
        at = 2 * n
        high_ref, low_ref = joint_refs[:2] if at < steps else joint_refs[2:]
        at = at % steps
        high = jnp.concatenate([high_ref[at], high_ref[at + 1]], axis=1)
        low = jnp.concatenate([low_ref[at], low_ref[at + 1]], axis=1)
        out = thrice(left, (high, low))
        even, odd = out[:, :SIDE], out[:, SIDE:]
        keep_ref[n] = jnp.where(first, even, odd)
        give_ref[n] = jnp.where(first, odd, even)


def level_of(where, upper, lower, joint):
    columns = upper.shape[0]
    steps = joint[0].shape[0]
    return pl.pallas_call(
        level_kernel,
        in_specs=[smem] + [pl.BlockSpec(memory_space=pltpu.VMEM)] * 6,
        out_shape=[shaped(steps, columns, SIDE)] * 2,
        compiler_params=params(),
        name="level",
    )(where, upper, lower, *joint)


def inverse_kernel(packed_ref, out_ref):
    count = packed_ref.shape[0]
    for q in range(count // 2):
        a, b = 2 * q, 2 * q + 1
        left, right = packed_ref[a, 0], packed_ref[b, 0]
        cross = full(full(left, packed_ref[a, 1]), right)
        out_ref[q, 0:SIDE, 0:SIDE] = left
        out_ref[q, 0:SIDE, SIDE:2 * SIDE] = -cross
        out_ref[q, SIDE:2 * SIDE, 0:SIDE] = jnp.zeros((SIDE, SIDE), jnp.float32)
        out_ref[q, SIDE:2 * SIDE, SIDE:2 * SIDE] = right


def inverse_of(packed):
    count = packed.shape[0]
    return pl.pallas_call(
        inverse_kernel,
        grid=(1,),
        in_specs=[pl.BlockSpec((count, 2, SIDE, SIDE), lambda n: (0, 0, 0, 0))],
        out_specs=pl.BlockSpec((count // 2, 2 * SIDE, 2 * SIDE), lambda n: (0, 0, 0)),
        out_shape=shaped(count // 2, 2 * SIDE, 2 * SIDE),
        compiler_params=params(),
        name="inverse",
    )(packed)


def band_block(packed_ref, row, column):
    kept = packed_ref.shape[1]
    count = packed_ref.shape[0]
    if column - row < kept:
        return packed_ref[row, column - row]
    return packed_ref[count - 1 - row, column - count // 2]


def final_kernel(
    where_ref, own_ref, other_ref, summit_ref, lower_ref, reflect_ref, packed_ref, inverse_ref,
    out_ref, solved_ref, whole_ref,
):
    parity = where_ref[0]
    count = packed_ref.shape[0]
    steps = own_ref.shape[0]
    for n in range(steps):
        even, odd = pick(parity, own_ref[n], other_ref[n])
        whole_ref[2 * n * SIDE:(2 * n + 1) * SIDE, :] = even
        whole_ref[(2 * n + 1) * SIDE:(2 * n + 2) * SIDE, :] = odd
    out_ref[...] = summit_ref[...] - thrice(halves(reflect_ref[...]), halves(whole_ref[...]))
    whole_ref[...] = lower_ref[...] - whole_ref[...]
    for q in reversed(range(count // 2)):
        rows = pl.ds(2 * q * SIDE, 2 * SIDE)
        value = whole_ref[rows, :]
        if q < count // 2 - 1:
            band = jnp.concatenate(
                [
                    jnp.concatenate(
                        [band_block(packed_ref, k, j) for j in range(2 * q + 2, count)], axis=1
                    )
                    for k in (2 * q, 2 * q + 1)
                ],
                axis=0,
            )
            value = value - full(band, whole_ref[(2 * q + 2) * SIDE:, :])
        whole_ref[rows, :] = full(inverse_ref[q], value)
    mine = pl.ds(pl.multiple_of(where_ref[1] * SIDE, SIDE), SIDE)
    solved_ref[...] = whole_ref[mine, :].T


def final_of(where, own, other, summit, lower, reflect, packed, inverse):
    columns = summit.shape[1]
    return pl.pallas_call(
        final_kernel,
        in_specs=[smem] + [pl.BlockSpec(memory_space=pltpu.VMEM)] * 7,
        out_shape=[shaped(SIDE, columns), shaped(columns, SIDE)],
        scratch_shapes=[pltpu.VMEM(lower.shape, jnp.float32)],
        compiler_params=params(),
        name="final",
    )(where, own, other, summit, lower, reflect, packed, inverse)


def moved(value, axis, pairs):
    return lax.ppermute(value, axis, pairs)


def per_device(
    right_side, reflectors, leaf_factor, node_reflect, node_factor, upper_blocks, block_inverse
):
    block = upper_blocks.shape[0]
    columns = right_side.shape[1]
    count = lax.axis_size("leaf")
    rows = lax.axis_size("rows")
    half = count // 2
    kept = half + 1
    row_index = lax.axis_index("rows")
    leaf_index = lax.axis_index("leaf")
    where = jnp.stack([leaf_index % 2, leaf_index]).astype(jnp.int32)
    swap = [(i, i ^ 1) for i in range(count)]
    same = [list(range(k, count, 2)) for k in range(2)]

    def scatter_sum(parts):
        keep, give = parts
        pair = keep + moved(give, "leaf", swap)
        got = lax.all_to_all(pair, "leaf", 0, 0, axis_index_groups=same)
        return jnp.sum(got, axis=0)

    def copies(mine):
        return jnp.broadcast_to(mine[None], (half,) + mine.shape)

    def collect(spread):
        own = lax.all_to_all(spread, "leaf", 0, 0, axis_index_groups=same)
        return own, moved(own, "leaf", swap)

    def packed_whole(blocks, pairs, shift):
        given = moved(blocks[kept:], "leaf", pairs)
        padded = jnp.pad(given, ((kept, 2), (0, 0), (0, 0)))
        placed = lax.dynamic_slice_in_dim(padded, jnp.maximum(kept - shift, 0), kept, 0)
        return lax.all_gather(blocks[:kept] + placed, "leaf", axis=0)

    factor_blocks = node_factor[0].reshape(count, block, block)
    factor_packed = packed_whole(
        factor_blocks, [(d, count - 1 - d) for d in range(half, count)], leaf_index + 1
    )
    upper_list = upper_blocks.reshape(block, count, block).transpose(1, 0, 2)
    upper_list = lax.dynamic_slice_in_dim(
        jnp.pad(upper_list, ((0, count), (0, 0), (0, 0))), leaf_index, count, 0
    )
    upper_list = jnp.concatenate([block_inverse[None], upper_list[1:]], axis=0)
    upper_packed = packed_whole(
        upper_list, [(d, count - 1 - d) for d in range(half)], count - leaf_index
    )

    weights = collect(copies(scatter_sum(weights_of(where, right_side, reflectors))))
    coeffs = collect(coeffs_of(where, *weights, leaf_factor[0]))
    rotated, top = lowered_of(where, *coeffs, reflectors, right_side)

    joint = joint_of(where, node_reflect[0], factor_packed.reshape(count, kept * block, block))

    stride = 1
    upper = top
    lower = moved(top, "rows", [(i, i + 1) for i in range(0, rows, 2)])
    own_coeffs = jnp.zeros_like(top)
    own_top = top
    while stride < rows:
        if stride > 1:
            nodes = list(range(stride, rows, 2 * stride))
            upper = moved(lower, "rows", [(j + stride // 2, j) for j in nodes])
            lower = moved(lower, "rows", [(j - stride // 2, j) for j in nodes])
        if 2 * stride == rows:
            lower_whole = lax.all_gather(lower.T, "leaf", axis=0, tiled=True)
        share = scatter_sum(level_of(where, upper, lower, joint))
        lower = lower - share
        mine = row_index % (2 * stride) == stride
        own_coeffs = jnp.where(mine, share, own_coeffs)
        own_top = jnp.where(mine, upper, own_top)
        stride *= 2
    root = rows // 2

    back = moved(lower, "rows", [(root, 0)])
    own, other = collect(copies(own_coeffs.T))
    inverse = inverse_of(upper_packed)
    lowered, solved = final_of(
        where, own, other, own_top.T, lower_whole, node_reflect[0], upper_packed, inverse
    )
    final_top = jnp.where(row_index == 0, back.T, lowered)
    rotated = lax.dynamic_update_slice_in_dim(rotated, final_top, 0, 0)
    arrived = lax.all_to_all(solved.reshape(rows, columns // rows, block), "rows", 0, 0)[root]
    return (rotated, arrived.T)


def solution(mesh):
    in_specs = (
        P(("rows", "leaf"), None),
        P(("rows", "leaf"), None),
        P("rows", None, "leaf"),
        P("rows", "leaf", None),
        P("rows", None, "leaf"),
        P("leaf", None),
        P("leaf", None),
    )
    out_specs = (P(("rows", "leaf"), None), P("leaf", "rows"))
    return jax.shard_map(
        per_device, mesh=mesh, in_specs=in_specs, out_specs=out_specs, check_vma=False
    )
```

profile of v0, /device:TPU:1, one launch (start us, length us, event | category | flops | bytes accessed | tf_op | source)
XLA Modules:
  0.0 385.9 jit_solution(7279973714408216616)
XLA Ops:
  7.2 1.2 slice.27
  8.4 1.3 collective-permute-start.4
  9.7 27.0 %collective-permute-done.4 = f32[7,128,128]{2,1,0:T(8,128)S(1)} collective-permute-done((f32[7,128,128]{2,1,0:T(8,128)S(1)}, f32[7,128,128]{2,1,0:T(8,128)S(1)}, u32[]{:S(2)}, u32[]{:S(2)}) %collective-permute-start.4) | collective-permute-done | bytes 458784 | tf_op jit(solution)/shard_map/ppermute | solution.py:317
  36.7 0.9 fusion
  38.1 1.8 collective-permute-start.17
  40.1 14.7 %collective-permute-done.17 = f32[7,128,128]{1,2,0:T(8,128)S(1)} collective-permute-done((f32[7,128,128]{1,2,0:T(8,128)S(1)}, f32[7,128,128]{1,2,0:T(8,128)S(1)}, u32[]{:S(2)}, u32[]{:S(2)}) %collective-permute-start.17) | collective-permute-done | bytes 458784 | tf_op jit(solution)/shard_map/ppermute | solution.py:317
  55.0 1.1 copy.55
  56.6 7.2 %weights.1 = (f32[8,128,128]{2,1,0:T(8,128)}, f32[8,128,128]{2,1,0:T(8,128)}) custom-call(s32[2]{0:T(128)} %pad_add_fusion.where_ref, f32[512,128]{1,0:T(8,128)} %side_ref.3, f32[512,2048]{1,0:T(8,128)} %vectors_ref.3), custom_call_target="tpu_custom_call" | custom-call | tf_op jit(solution)/shard_map/weights/pallas_call | solution.py:70
  64.2 1.7 collective-permute-done
  65.9 1.2 add.52
  67.1 29.0 %all_to_all.45 = f32[8,128,128]{2,1,0:T(8,128)S(1)} all-to-all(f32[8,128,128]{2,1,0:T(8,128)S(1)} %add.52), channel_id=1, replica_groups={{0,2,4,6,8,10,12,14},{1,3,5,7,9,11,13,15},{16,18,20,22,24,26,28,30},{17..., dimensions={0} | all-to-all | bytes 1048576 | tf_op jit(solution)/shard_map/all_to_all | solution.py:338
  96.2 23.1 %all_to_all.46.own_ref = f32[8,128,128]{2,1,0:T(8,128)S(1)} all-to-all(f32[8,128,128]{2,1,0:T(8,128)S(1)} %broadcast_in_dim.8), channel_id=1, replica_groups={{0,2,4,6,8,10,12,14},{1,3,5,7,9,11,13,15},{16,18,20,22,24,26,28,30},{17..., dimensions={0} | all-to-all | bytes 1048576 | tf_op jit(solution)/shard_map/all_to_all | solution.py:345
  119.4 1.9 collective-permute-start.1
  121.3 1.5 collective-permute-done.1.other_ref
  122.8 0.8 copy-done.6
  123.6 3.0 coeffs.1
  126.6 24.2 %all_to_all.47.own_ref = f32[8,128,128]{2,1,0:T(8,128)S(1)} all-to-all(f32[8,128,128]{2,1,0:T(8,128)} %coeffs.1), channel_id=1, replica_groups={{0,2,4,6,8,10,12,14},{1,3,5,7,9,11,13,15},{16,18,20,22,24,26,28,30},{17..., dimensions={0} | all-to-all | bytes 1048576 | tf_op jit(solution)/shard_map/all_to_all | solution.py:345
  150.8 0.7 collective-permute-start.2
  151.6 1.5 collective-permute-done.2.other_ref
  153.1 0.8 copy-done.7
  153.9 7.5 %lowered.1 = (f32[512,128]{1,0:T(8,128)}, f32[128,128]{1,0:T(8,128)}) custom-call(s32[2]{0:T(128)} %pad_add_fusion.where_ref, f32[8,128,128]{2,1,0:T(8,128)} %copy-done.2, f32[8,128,128]{2,1,0:T(8,128)} %copy-done.7, f32[512,2048]{1,0:T(8,128)} %vectors_ref.3, f32[512,128]{1,0:T(8,128)} %side_ref.3), custom_call_target="tpu_custom_call" | custom-call | tf_op jit(solution)/shard_map/lowered/pallas_call | solution.py:130
  161.4 0.9 copy.36
  162.3 3.4 collective-permute-start.3
  165.7 1.3 collective-permute-done.3
  167.0 0.7 copy.37.lower_ref
  167.8 11.2 %joint.1 = (bf16[8,256,128]{2,1,0:T(8,128)(2,1)}, bf16[8,256,128]{2,1,0:T(8,128)(2,1)}, bf16[8,256,128]{2,1,0:T(8,128)(2,1)}, bf16[8,256,128]{2,1,0:T(8,128)(2,1)}) custom-call(s32[2]{0:T(128)} %pad_add_fusion.where_ref, f32[128,2048]{1,0:T(8,128)} %bitcast.32, f32[16,1152,128]{2,1,0:T(8,128)} %bitcast.28, f32[16,1152,128]{2,1,0:T(8,128)} %bitcast.29), custom_call_target="tpu_custom_call" | custom-call | flops 3221225472 | bytes 9437184 | tf_op jit(solution)/shard_map/joint/pallas_call | solution.py:188
  179.0 3.3 level.4
  182.3 1.0 collective-permute-start.5
  183.3 1.7 collective-permute-done.5
  185.0 1.1 add.55
  186.2 19.4 %all_to_all.48 = f32[8,128,128]{2,1,0:T(8,128)S(1)} all-to-all(f32[8,128,128]{2,1,0:T(8,128)S(1)} %add.55), channel_id=1, replica_groups={{0,2,4,6,8,10,12,14},{1,3,5,7,9,11,13,15},{16,18,20,22,24,26,28,30},{17..., dimensions={0} | all-to-all | bytes 1048576 | tf_op jit(solution)/shard_map/all_to_all | solution.py:338
  205.7 0.7 collective-permute-start.7
  206.4 0.7 collective-permute-start.6
  207.1 0.7 copy.39.upper_ref
  207.8 0.7 copy.40.lower_ref
  208.6 3.2 level.5
  211.7 1.7 collective-permute-start.8
  213.5 1.7 collective-permute-done.8
  215.2 1.1 add.56
  216.3 20.4 %all_to_all.49 = f32[8,128,128]{2,1,0:T(8,128)S(1)} all-to-all(f32[8,128,128]{2,1,0:T(8,128)S(1)} %add.56), channel_id=1, replica_groups={{0,2,4,6,8,10,12,14},{1,3,5,7,9,11,13,15},{16,18,20,22,24,26,28,30},{17..., dimensions={0} | all-to-all | bytes 1048576 | tf_op jit(solution)/shard_map/all_to_all | solution.py:338
  238.2 0.7 copy.42.upper_ref
  239.0 0.7 copy.43.lower_ref
  239.7 3.2 level.6
  243.3 1.7 collective-permute-done.11
  245.1 1.1 add.57
  246.2 20.4 %all_to_all.50 = f32[8,128,128]{2,1,0:T(8,128)S(1)} all-to-all(f32[8,128,128]{2,1,0:T(8,128)S(1)} %add.57), channel_id=1, replica_groups={{0,2,4,6,8,10,12,14},{1,3,5,7,9,11,13,15},{16,18,20,22,24,26,28,30},{17..., dimensions={0} | all-to-all | bytes 1048576 | tf_op jit(solution)/shard_map/all_to_all | solution.py:338
  268.1 0.7 copy.45.upper_ref
  268.8 0.7 copy.46.lower_ref
  269.5 3.2 level.7
  273.2 1.7 collective-permute-done.14
  274.9 1.9 add.58
  276.9 3.5 all-to-all-start.6
  280.4 0.7 all-gather.6.cloned.1.call-update
  281.1 17.1 %all-to-all-done.6 = f32[8,128,128]{2,1,0:T(8,128)S(1)} async-done(((f32[8,128,128]{2,1,0:T(8,128)}), f32[8,128,128]{2,1,0:T(8,128)S(1)}, u32[]{:S(2)}, u32[]{:S(2)}) %all-to-all-start.6) | async-done | bytes 524320 | tf_op jit(solution)/shard_map/all_to_all | solution.py:338
  298.4 0.9 fusion.3
  299.3 20.9 %all_to_all.51.own_ref = f32[8,128,128]{2,1,0:T(8,128)S(1)} all-to-all(f32[8,128,128]{2,1,0:T(8,128)S(1)} %broadcast_in_dim.20), channel_id=1, replica_groups={{0,2,4,6,8,10,12,14},{1,3,5,7,9,11,13,15},{16,18,20,22,24,26,28,30},{17..., dimensions={0} | all-to-all | bytes 1048576 | tf_op jit(solution)/shard_map/all_to_all | solution.py:345
  320.2 1.4 collective-permute-start.16
  321.7 4.1 %inverse.1.inverse_ref = f32[8,256,256]{2,1,0:T(8,128)} custom-call(f32[16,9,128,128]{3,2,1,0:T(8,128)} %bitcast.26), custom_call_target="tpu_custom_call" | custom-call | tf_op jit(solution)/shard_map/inverse/pallas_call | solution.py:253
  325.8 1.5 collective-permute-start.15
  327.9 9.5 %all-gather.6.cloned.1.call-done.lower_ref = f32[2048,128]{1,0:T(8,128)} async-done(((f32[128,128]{1,0:T(8,128)}), f32[2048,128]{1,0:T(8,128)}) %all-gather.6.cloned.1.call-update) | async-done | bytes 1048592 | tf_op jit(solution)/shard_map/all_gather | solution.py:384
  337.4 0.8 copy-done.5
  338.2 23.0 %final.1 = (f32[128,128]{1,0:T(8,128)}, f32[128,128]{1,0:T(8,128)}) custom-call(s32[2]{0:T(128)} %pad_add_fusion.where_ref, f32[8,128,128]{2,1,0:T(8,128)} %copy-done, f32[8,128,128]{2,1,0:T(8,128)} %copy-done.5, f32[128,128]{1,0:T(8,128)} %select_bitcast_fusion.summit_ref, f32[2048,128]{1,0:T(8,128)} %all-gather.6.cloned.1.call-done.lower_ref, ...), custom_call_target="tpu_custom_call" | custom-call | tf_op jit(solution)/shard_map/final/pallas_call | solution.py:306
  361.2 11.1 %all-to-all-start.8 = ((f32[16,8,128]{2,1,0:T(8,128)}), f32[16,8,128]{2,1,0:T(8,128)S(1)}, u32[]{:S(2)}, u32[]{:S(2)}) async-start(f32[16,8,128]{2,1,0:T(8,128)} %bitcast.39), calls=%async_computation.8 | async-start | bytes 131072 | tf_op jit(solution)/shard_map/all_to_all | solution.py:401
  372.9 5.9 %all-to-all-done.8 = f32[16,8,128]{2,1,0:T(8,128)S(1)} async-done(((f32[16,8,128]{2,1,0:T(8,128)}), f32[16,8,128]{2,1,0:T(8,128)S(1)}, u32[]{:S(2)}, u32[]{:S(2)}) %all-to-all-start.8) | async-done | bytes 65568 | tf_op jit(solution)/shard_map/all_to_all | solution.py:401
  (62 shorter events, 7.9 us)
Async XLA Ops:
  7.2 29.5 %slice-start = ((f32[1,2048,128]{2,1,0:T(8,128)}), f32[1,1152,128]{2,1,0:T(8,128)S(1)}, s32[]{:S(2)}) async-start(f32[1,2048,128]{2,1,0:T(8,128)} %param.11), calls=%async_computation.12 | async-start | bytes 1179648 | tf_op jit(solution)/shard_map/slice | solution.py:352
  7.2 30.5 %copy-start.3 = (f32[128,2048]{1,0:T(8,128)S(1)}, f32[128,2048]{1,0:T(8,128)}, u32[]{:S(2)}) copy-start(f32[128,2048]{1,0:T(8,128)} %param.12) | copy-start | bytes 3145732
  7.2 160.6 %all-gather.8.cloned.1.call-start = ((), (), s32[]{:S(2)}) async-start(), calls=%async_computation.10 | async-start | bytes 10027008 | tf_op jit(solution)/shard_map/all_gather | solution.py:352
  8.4 28.3 %collective-permute-start.4 = (f32[7,128,128]{2,1,0:T(8,128)S(1)}, f32[7,128,128]{2,1,0:T(8,128)S(1)}, u32[]{:S(2)}, u32[]{:S(2)}) collective-permute-start(f32[7,128,128]{2,1,0:T(8,128)S(1)} %bitcast.37), channel_id=1, source_target_pairs={{8,7},{9,6},{10,5},{11,4},{12,3},{13,2},{14,1},{15,0},{24,23},{25,... | collective-permute-start | bytes 1376264 | tf_op jit(solution)/shard_map/ppermute | solution.py:317
  37.6 2.3 copy-start.8
  37.6 284.0 %all-gather.10.cloned.1.call-start = ((), (), s32[]{:S(2)}) async-start(), calls=%async_computation.11 | async-start | bytes 10027008 | tf_op jit(solution)/shard_map/all_gather | solution.py:352
  38.1 16.8 %collective-permute-start.17 = (f32[7,128,128]{1,2,0:T(8,128)S(1)}, f32[7,128,128]{1,2,0:T(8,128)S(1)}, u32[]{:S(2)}, u32[]{:S(2)}) collective-permute-start(f32[7,128,128]{1,2,0:T(8,128)S(1)} %pad_dynamic-slice_fusion.1), channel_id=1, source_target_pairs={{0,15},{1,14},{2,13},{3,12},{4,11},{5,10},{6,9},{7,8},{16,31},{17,... | collective-permute-start | bytes 1376264 | tf_op jit(solution)/shard_map/ppermute | solution.py:317
  63.8 2.1 collective-permute-start
  119.4 3.5 copy-start.1
  119.4 3.5 collective-permute-start.1
  122.8 0.8 copy-start.6
  150.8 2.3 copy-start.2
  150.8 2.3 collective-permute-start.2
  153.1 0.8 copy-start.7
  162.3 4.7 %collective-permute-start.3 = (f32[128,128]{0,1:T(8,128)S(1)}, f32[128,128]{0,1:T(8,128)S(1)}, u32[]{:S(2)}, u32[]{:S(2)}) collective-permute-start(f32[128,128]{0,1:T(8,128)S(1)} %copy.36), channel_id=1, source_target_pairs={{0,16},{32,48},{64,80},{96,112},{128,144},{160,176},{192,208},{224... | collective-permute-start | bytes 196616 | tf_op jit(solution)/shard_map/ppermute | solution.py:317
  182.3 2.8 collective-permute-start.5
  205.7 1.3 collective-permute-start.7
  206.4 1.4 collective-permute-start.6
  211.7 3.5 collective-permute-start.8
  236.9 1.3 collective-permute-start.10
  237.5 1.4 collective-permute-start.9
  242.9 2.2 collective-permute-start.11
  266.7 1.3 collective-permute-start.13
  267.4 1.4 collective-permute-start.12
  268.8 8.0 %copy-start.4 = (f32[128,128]{0,1:T(8,128)}, f32[128,128]{0,1:T(8,128)S(1)}, u32[]{:S(2)}) copy-start(f32[128,128]{0,1:T(8,128)S(1)} %collective-permute-done.12) | copy-start | bytes 196612
  272.7 2.2 collective-permute-start.14
  276.9 21.4 %all-to-all-start.6 = ((f32[8,128,128]{2,1,0:T(8,128)}), f32[8,128,128]{2,1,0:T(8,128)S(1)}, u32[]{:S(2)}, u32[]{:S(2)}) async-start(f32[8,128,128]{2,1,0:T(8,128)} %add.58), calls=%async_computation.6 | async-start | bytes 1048576 | tf_op jit(solution)/shard_map/all_to_all | solution.py:338
  280.4 57.0 %all-gather.6.cloned.1.call-start = ((), (), s32[]{:S(2)}) async-start(), calls=%async_computation.9 | async-start | bytes 1114112 | tf_op jit(solution)/shard_map/all_gather | solution.py:384
  320.2 5.5 %copy-start = (f32[8,128,128]{2,1,0:T(8,128)}, f32[8,128,128]{2,1,0:T(8,128)S(1)}, u32[]{:S(2)}) copy-start(f32[8,128,128]{2,1,0:T(8,128)S(1)} %all_to_all.51.own_ref) | copy-start | bytes 1572868
  320.2 17.1 %collective-permute-start.16 = (f32[8,128,128]{2,1,0:T(8,128)S(1)}, f32[8,128,128]{2,1,0:T(8,128)S(1)}, u32[]{:S(2)}, u32[]{:S(2)}) collective-permute-start(f32[8,128,128]{2,1,0:T(8,128)S(1)} %all_to_all.51.own_ref), channel_id=1, source_target_pairs={{0,1},{1,0},{2,3},{3,2},{4,5},{5,4},{6,7},{7,6},{8,9},{9,8},{10,11... | collective-permute-start | bytes 1572872 | tf_op jit(solution)/shard_map/ppermute | solution.py:317
  325.8 46.4 %collective-permute-start.15 = (f32[128,128]{0,1:T(8,128)S(1)}, f32[128,128]{0,1:T(8,128)S(1)}, u32[]{:S(2)}, u32[]{:S(2)}) collective-permute-start(f32[128,128]{0,1:T(8,128)S(1)} %get-tuple-element.38), channel_id=1, source_target_pairs={{128,0},{129,1},{130,2},{131,3},{132,4},{133,5},{134,6},{135,7},{1... | collective-permute-start | bytes 196616 | tf_op jit(solution)/shard_map/ppermute | solution.py:317
  337.4 0.8 copy-start.5
  361.2 17.6 %all-to-all-start.8 = ((f32[16,8,128]{2,1,0:T(8,128)}), f32[16,8,128]{2,1,0:T(8,128)S(1)}, u32[]{:S(2)}, u32[]{:S(2)}) async-start(f32[16,8,128]{2,1,0:T(8,128)} %bitcast.39), calls=%async_computation.8 | async-start | bytes 131072 | tf_op jit(solution)/shard_map/all_to_all | solution.py:401
Sparse Core Ops, SparseCore 0:
  37.8 80.2 all-gather.7
  119.8 71.6 all-gather.9
  283.0 54.3 all-gather.5
where the time goes:
time: 388 us; the launch traced here: 386 us
  blocking collectives  157 us (40%)
  waiting for transfers between devices  88.1 us (23%)
  Pallas kernels  68.7 us (18%)
  starting transfers between devices  34.8 us (9%)
  between operations  14.1 us (4%)
  local copies, waits for them, and re-layouts  12.3 us (3%)
  other arithmetic  10.4 us (3%)
    all_to_all x4, blocking collectives, scatter_sum(): got = lax.all_to_all(pair, 'leaf', 0, 0, axis_index_groups=same)  89.2 us
    all_to_all x3, blocking collectives, collect(): own = lax.all_to_all(spread, 'leaf', 0, 0, axis_index_groups=same)  68.2 us
    ppermute x18, waiting for transfers between devices, moved(): return lax.ppermute(value, axis, pairs)  54.9 us
    pallas_call x1, Pallas kernels, final_of(): pl.pallas_call(final_kernel, in_specs=[smem] + [pl.BlockSpec(memory_space...  23 us
    ppermute x18, starting transfers between devices, moved(): return lax.ppermute(value, axis, pairs)  20.1 us
    all_to_all x1, waiting for transfers between devices, scatter_sum(): got = lax.all_to_all(pair, 'leaf', 0, 0, axis_index_groups=same)  17.1 us
    pallas_call x4, Pallas kernels, level_of(): pl.pallas_call(level_kernel, in_specs=[smem] + [pl.BlockSpec(memory_space...  12.7 us
    pallas_call x1, Pallas kernels, joint_of(): pl.pallas_call(joint_kernel, grid=(steps,), in_specs=[smem, pl.BlockSpec(...  11.2 us
  transfers between devices with their start and end apart: 23, of which 13 were waited for; matrix products, arithmetic and copies ran while one was open for 5% of the time, Pallas kernels for 18%

commit v1 on v0

v1 whole, which is shorter than its diff:
```python
import functools

import jax
import jax.numpy as jnp
from jax import lax
from jax.experimental import pallas as pl
from jax.experimental.pallas import tpu as pltpu
from jax.sharding import PartitionSpec as P

SIDE = 128
GROUP = 2
SPLIT = (((1,), (0,)), ((), ()))
LIMIT = 28 * 1024 * 1024


def halves(value):
    high = value.astype(jnp.bfloat16)
    low = (value - high.astype(jnp.float32)).astype(jnp.bfloat16)
    return high, low


def once(left, right):
    return lax.dot_general(left, right, SPLIT, preferred_element_type=jnp.float32)


def thrice(left, right):
    return once(left[0], right[0]) + (once(left[0], right[1]) + once(left[1], right[0]))


def full(left, right):
    return lax.dot_general(
        left, right, SPLIT, precision=lax.Precision.HIGHEST, preferred_element_type=jnp.float32
    )


def pick(parity, own, other):
    first = parity == 0
    return jnp.where(first, own, other), jnp.where(first, other, own)


smem = pl.BlockSpec(memory_space=pltpu.SMEM)


vmem = pl.BlockSpec(memory_space=pltpu.VMEM)


def params():
    return pltpu.CompilerParams(vmem_limit_bytes=LIMIT)


def cost(flops, size):
    return pl.CostEstimate(flops=flops, bytes_accessed=size, transcendentals=0)


def shaped(*shape, dtype=jnp.float32):
    return jax.ShapeDtypeStruct(shape, dtype)


def weights_kernel(where_ref, side_ref, vectors_ref, keep_ref, give_ref, high_ref, low_ref):
    @pl.when(pl.program_id(0) == 0)
    def _():
        high, low = halves(side_ref[...].T)
        high_ref[...] = high
        low_ref[...] = low

    first = where_ref[0] == 0
    for n in range(keep_ref.shape[0]):
        vectors = vectors_ref[:, 2 * n * SIDE:(2 * n + 2) * SIDE]
        out = thrice((high_ref[...], low_ref[...]), halves(vectors))
        even, odd = out[:, :SIDE], out[:, SIDE:]
        keep_ref[n] = jnp.where(first, even, odd)
        give_ref[n] = jnp.where(first, odd, even)


def weights_of(where, side, vectors):
    tall, order = vectors.shape
    columns = side.shape[1]
    steps = order // (2 * SIDE)
    block = pl.BlockSpec((GROUP, columns, SIDE), lambda n: (n, 0, 0))
    return pl.pallas_call(
        weights_kernel,
        grid=(steps // GROUP,),
        in_specs=[
            smem,
            pl.BlockSpec((tall, columns), lambda n: (0, 0)),
            pl.BlockSpec((tall, 2 * GROUP * SIDE), lambda n: (0, n)),
        ],
        out_specs=[block, block],
        out_shape=[shaped(steps, columns, SIDE)] * 2,
        scratch_shapes=[pltpu.VMEM((columns, tall), jnp.bfloat16)] * 2,
        compiler_params=params(),
        cost_estimate=cost(6 * tall * columns * order, 4 * vectors.size),
        name="weights",
    )(where, side, vectors)


def coeffs_kernel(where_ref, own_ref, other_ref, factor_ref, out_ref):
    parity = where_ref[0]
    steps = own_ref.shape[0]
    total = jnp.zeros(own_ref.shape[1:], jnp.float32)
    for n in range(steps):
        left = jnp.concatenate(pick(parity, own_ref[n], other_ref[n]), axis=1)
        right = factor_ref[2 * n * SIDE:(2 * n + 2) * SIDE, :]
        total = total + thrice(halves(left), halves(right))
    total = total.T
    for n in range(steps):
        out_ref[n] = total


def coeffs_of(where, own, other, factor):
    return pl.pallas_call(
        coeffs_kernel,
        in_specs=[smem] + [pl.BlockSpec(memory_space=pltpu.VMEM)] * 3,
        out_shape=shaped(own.shape[0], SIDE, own.shape[1]),
        compiler_params=params(),
        cost_estimate=cost(6 * own.shape[1] * factor.size, 4 * factor.size),
        name="coeffs",
    )(where, own, other, factor)


def lowered_kernel(where_ref, own_ref, other_ref, vectors_ref, side_ref, out_ref, top_ref):
    step = pl.program_id(0)

    @pl.when(step == 0)
    def _():
        out_ref[...] = side_ref[...]

    total = out_ref[...]
    for n in range(own_ref.shape[0]):
        right = jnp.concatenate(pick(where_ref[0], own_ref[n], other_ref[n]), axis=0)
        vectors = vectors_ref[:, 2 * n * SIDE:(2 * n + 2) * SIDE]
        total = total - thrice(halves(vectors), halves(right))
    out_ref[...] = total

    @pl.when(step == pl.num_programs(0) - 1)
    def _():
        top_ref[...] = out_ref[:SIDE, :].T


def lowered_of(where, own, other, vectors, side):
    tall, order = vectors.shape
    columns = side.shape[1]
    steps = order // (2 * SIDE)
    block = pl.BlockSpec((GROUP, SIDE, columns), lambda n: (n, 0, 0))
    whole = pl.BlockSpec((tall, columns), lambda n: (0, 0))
    return pl.pallas_call(
        lowered_kernel,
        grid=(steps // GROUP,),
        in_specs=[
            smem, block, block, pl.BlockSpec((tall, 2 * GROUP * SIDE), lambda n: (0, n)), whole,
        ],
        out_specs=[whole, pl.BlockSpec((columns, SIDE), lambda n: (0, 0))],
        out_shape=[shaped(tall, columns), shaped(columns, SIDE)],
        compiler_params=params(),
        cost_estimate=cost(6 * tall * columns * order, 4 * vectors.size),
        name="lowered",
    )(where, own, other, vectors, side)


def joint_kernel(where_ref, reflect_ref, packed_ref, high_ref, low_ref, panel_ref, sems):
    count, kept, _ = packed_ref.shape
    order = reflect_ref.shape[1]
    steps = count // 2
    copies = []
    for n in range(steps):
        pair = []
        for k in (n, count - 1 - n):
            copy = pltpu.make_async_copy(packed_ref.at[k], panel_ref.at[k], sems.at[k])
            copy.start()
            pair.append(copy)
        copies.append(pair)
    reflect = halves(reflect_ref[...])
    own = where_ref[1]
    spare = kept // SIDE - 1
    for n in range(steps):
        for copy in copies[n]:
            copy.wait()
        far = count - 1 - n
        edge = (n + 1) * SIDE
        stop = order - n * SIDE
        short, long = halves(panel_ref[n]), halves(panel_ref[far])
        shared = [jnp.concatenate([s[:edge], t[:edge]], axis=1) for s, t in zip(short, long)]
        rest = [
            jnp.concatenate([t[edge:], s[edge:kept - SIDE]], axis=0)
            if stop > kept else t[edge:stop]
            for s, t in zip(short, long)
        ]
        both = thrice([r[:, :edge] for r in reflect], shared)
        left = both[:, :SIDE]
        right = both[:, SIDE:] + thrice([r[:, edge:stop] for r in reflect], rest)

        def rows(k, at):
            return panel_ref[k, pl.ds(pl.multiple_of(at * SIDE, SIDE), SIDE), :]

        zero = jnp.zeros((SIDE, SIDE), jnp.float32)
        own_left = jnp.where(own <= n, rows(n, jnp.minimum(own, spare)), zero)
        moved_on = jnp.clip(own + n - spare, 0, spare)
        own_right = jnp.where(
            own <= spare,
            rows(far, jnp.minimum(own, spare)),
            jnp.where(own <= far, rows(n, moved_on), zero),
        )
        for k, top, bottom in ((n, left, own_left), (far, right, own_right)):
            at = pl.ds(k * SIDE, SIDE)
            for ref, part in zip((high_ref, low_ref), zip(halves(top), halves(bottom))):
                ref[0:SIDE, at] = part[0]
                ref[SIDE:2 * SIDE, at] = part[1]


def joint_of(where, reflect, packed):
    block, order = reflect.shape
    return pl.pallas_call(
        joint_kernel,
        in_specs=[smem, vmem, pl.BlockSpec(memory_space=pl.ANY)],
        out_specs=[vmem] * 2,
        out_shape=[shaped(2 * block, order, dtype=jnp.bfloat16)] * 2,
        scratch_shapes=[
            pltpu.VMEM(packed.shape, jnp.float32),
            pltpu.SemaphoreType.DMA((packed.shape[0],)),
        ],
        compiler_params=params(),
        cost_estimate=cost(3 * block * order * order, 4 * packed.size),
        name="joint",
    )(where, reflect, packed)


def level_kernel(where_ref, upper_ref, lower_ref, high_ref, low_ref, keep_ref, give_ref):
    first = where_ref[0] == 0
    left = halves(jnp.concatenate([upper_ref[...], lower_ref[...]], axis=1))
    for n in range(keep_ref.shape[0]):
        at = pl.ds(2 * n * SIDE, 2 * SIDE)
        out = thrice(left, (high_ref[:, at], low_ref[:, at]))
        even, odd = out[:, :SIDE], out[:, SIDE:]
        keep_ref[n] = jnp.where(first, even, odd)
        give_ref[n] = jnp.where(first, odd, even)


def level_of(where, upper, lower, joint):
    columns = upper.shape[0]
    wide, order = joint[0].shape
    steps = order // (2 * SIDE)
    return pl.pallas_call(
        level_kernel,
        in_specs=[smem] + [vmem] * 4,
        out_specs=[vmem] * 2,
        out_shape=[shaped(steps, columns, SIDE)] * 2,
        compiler_params=params(),
        cost_estimate=cost(6 * columns * wide * order, 4 * wide * order),
        name="level",
    )(where, upper, lower, *joint)


def fold_kernel(pieces_ref, out_ref):
    count = pieces_ref.shape[0]
    for n in range(count // 2):
        far = count - 1 - n
        out_ref[n, 0:far] = pieces_ref[n, n + 1:count]
        out_ref[n, far] = pieces_ref[n, count]
        for k in range(far + 1, count):
            out_ref[n, k] = pieces_ref[far, k]
        out_ref[n, count] = pieces_ref[far, count]


def fold_of(pieces):
    count = pieces.shape[0]
    return pl.pallas_call(
        fold_kernel,
        in_specs=[vmem],
        out_specs=vmem,
        out_shape=shaped(count // 2, *pieces.shape[1:]),
        compiler_params=params(),
        name="fold",
    )(pieces)


def final_kernel(
    where_ref, own_ref, other_ref, summit_ref, reflect_ref, folded_ref,
    out_ref, solved_ref, coeffs_ref, whole_ref, panel_ref, sems,
):
    parity = where_ref[0]
    steps = own_ref.shape[0]
    count = 2 * steps
    copies = []
    for p in range(count // 4):
        copy = pltpu.make_async_copy(
            folded_ref.at[:, 2 * p:2 * p + 2], panel_ref.at[p], sems.at[p]
        )
        copy.start()
        copies.append(copy)
    for n in range(steps):
        for part, ref in enumerate((coeffs_ref, whole_ref)):
            even, odd = pick(parity, own_ref[n, part], other_ref[n, part])
            ref[2 * n * SIDE:(2 * n + 1) * SIDE, :] = even
            ref[(2 * n + 1) * SIDE:(2 * n + 2) * SIDE, :] = odd
    out_ref[...] = summit_ref[...] - thrice(halves(reflect_ref[...]), halves(coeffs_ref[...]))

    def block_at(row, column):
        near = min(row, count - 1 - row)
        if row >= count // 2:
            at = column
        else:
            at = count - 1 - row if column == count else column - row - 1
        return panel_ref[near // 2, :, near % 2, at].reshape(SIDE, SIDE)

    zero = jnp.zeros((SIDE, SIDE), jnp.float32)
    for q in reversed(range(count // 2)):
        if q >= count // 4:
            copies[count // 2 - 1 - q].wait()
        a, b = 2 * q, 2 * q + 1
        rows = pl.ds(a * SIDE, 2 * SIDE)
        value = whole_ref[rows, :]
        if b < count - 1:
            band = jnp.concatenate(
                [
                    jnp.concatenate([block_at(k, j) for j in range(b + 1, count)], axis=1)
                    for k in (a, b)
                ],
                axis=0,
            )
            value = value - full(band, whole_ref[(b + 1) * SIDE:, :])
        inverse = jnp.concatenate(
            [
                jnp.concatenate([block_at(a, count), -block_at(a, b)], axis=1),
                jnp.concatenate([zero, block_at(b, count)], axis=1),
            ],
            axis=0,
        )
        whole_ref[rows, :] = full(inverse, value)
    mine = pl.ds(pl.multiple_of(where_ref[1] * SIDE, SIDE), SIDE)
    solved_ref[...] = whole_ref[mine, :].T


def final_of(where, own, other, summit, reflect, folded):
    columns = summit.shape[1]
    order = reflect.shape[1]
    rows, near, long = folded.shape[:3]
    return pl.pallas_call(
        final_kernel,
        in_specs=[smem] + [vmem] * 4 + [pl.BlockSpec(memory_space=pl.ANY)],
        out_specs=[vmem] * 2,
        out_shape=[shaped(SIDE, columns), shaped(columns, SIDE)],
        scratch_shapes=[pltpu.VMEM((order, columns), jnp.float32)] * 2
        + [
            pltpu.VMEM((near // 2, rows, 2, long) + folded.shape[3:], jnp.float32),
            pltpu.SemaphoreType.DMA((near // 2,)),
        ],
        compiler_params=params(),
        cost_estimate=cost(8 * columns * order * order, 4 * folded.size),
        name="final",
    )(where, own, other, summit, reflect, folded)


def dot(left, right):
    return jnp.dot(left, right, precision=lax.Precision.HIGHEST, preferred_element_type=jnp.float32)


def moved(value, axis, pairs):
    return lax.ppermute(value, axis, pairs)


def per_device(
    right_side, reflectors, leaf_factor, node_reflect, node_factor, upper_blocks, block_inverse
):
    block = upper_blocks.shape[0]
    columns = right_side.shape[1]
    count = lax.axis_size("leaf")
    rows = lax.axis_size("rows")
    half = count // 2
    kept = half + 1
    row_index = lax.axis_index("rows")
    leaf_index = lax.axis_index("leaf")
    where = jnp.stack([leaf_index % 2, leaf_index]).astype(jnp.int32)
    swap = [(i, i ^ 1) for i in range(count)]
    same = [list(range(k, count, 2)) for k in range(2)]

    def scatter_sum(parts):
        keep, give = parts
        pair = keep + moved(give, "leaf", swap)
        got = lax.all_to_all(pair, "leaf", 0, 0, axis_index_groups=same)
        return jnp.sum(got, axis=0)

    def copies(mine):
        return jnp.broadcast_to(mine[None], (half,) + mine.shape)

    def collect(spread):
        own = lax.all_to_all(spread, "leaf", 0, 0, axis_index_groups=same)
        return own, moved(own, "leaf", swap)

    factor_blocks = node_factor[0].reshape(count, block, block)
    given = moved(
        factor_blocks[kept:], "leaf", [(d, count - 1 - d) for d in range(half, count)]
    )
    weights_part = scatter_sum(weights_of(where, right_side, reflectors))

    given, _ = lax.optimization_barrier((given, weights_part))
    padded = jnp.pad(given, ((kept, 2), (0, 0), (0, 0)))
    placed = lax.dynamic_slice_in_dim(padded, jnp.maximum(half - leaf_index, 0), kept, 0)
    factor_packed = lax.all_gather(factor_blocks[:kept] + placed, "leaf", axis=0)

    weights = collect(copies(weights_part))
    coeffs = collect(coeffs_of(where, *weights, leaf_factor[0]))
    rotated, top = lowered_of(where, *coeffs, reflectors, right_side)

    upper_own, inverse_own, _ = lax.optimization_barrier((upper_blocks, block_inverse, top))
    inverse_next = moved(inverse_own, "leaf", [(i + 1, i) for i in range(0, count, 2)])
    eighth = block // rows
    upper_slice = lax.dynamic_slice_in_dim(upper_own, row_index * eighth, eighth, 0)
    inverse_slice = lax.dynamic_slice_in_dim(inverse_own, row_index * eighth, eighth, 0)
    upper_slice = upper_slice.reshape(eighth, count, block).transpose(1, 0, 2)
    beside = lax.dynamic_slice_in_dim(
        upper_own, jnp.minimum(leaf_index + 1, count - 1) * block, block, 1
    )
    cross = dot(dot(inverse_slice, beside), inverse_next)
    at_cross = jnp.arange(count)[:, None, None] == leaf_index + 1
    at_cross = jnp.logical_and(at_cross, leaf_index % 2 == 0)
    upper_slice = jnp.where(at_cross, cross[None], upper_slice)
    upper_slice = jnp.concatenate([upper_slice, inverse_slice[None]], axis=0)
    folded = fold_of(lax.all_gather(upper_slice, "leaf", axis=0))
    folded = lax.all_gather(folded, "rows", axis=0)

    joint = joint_of(where, node_reflect[0], factor_packed.reshape(count, kept * block, block))

    stride = 1
    upper = top
    lower = moved(top, "rows", [(i, i + 1) for i in range(0, rows, 2)])
    own_coeffs = jnp.zeros_like(top)
    own_top = top
    while stride < rows:
        if stride > 1:
            nodes = list(range(stride, rows, 2 * stride))
            upper = moved(lower, "rows", [(j + stride // 2, j) for j in nodes])
            lower = moved(lower, "rows", [(j - stride // 2, j) for j in nodes])
        share = scatter_sum(level_of(where, upper, lower, joint))
        lower = lower - share
        mine = row_index % (2 * stride) == stride
        own_coeffs = jnp.where(mine, share, own_coeffs)
        own_top = jnp.where(mine, upper, own_top)
        stride *= 2
    root = rows // 2

    back = moved(lower, "rows", [(root, 0)])
    own, other = collect(copies(jnp.stack([own_coeffs.T, lower.T])))
    lowered, solved = final_of(where, own, other, own_top.T, node_reflect[0], folded)
    final_top = jnp.where(row_index == 0, back.T, lowered)
    rotated = lax.dynamic_update_slice_in_dim(rotated, final_top, 0, 0)
    arrived = lax.all_to_all(solved.reshape(rows, columns // rows, block), "rows", 0, 0)[root]
    return (rotated, arrived.T)


def solution(mesh):
    in_specs = (
        P(("rows", "leaf"), None),
        P(("rows", "leaf"), None),
        P("rows", None, "leaf"),
        P("rows", "leaf", None),
        P("rows", None, "leaf"),
        P("leaf", None),
        P("leaf", None),
    )
    out_specs = (P(("rows", "leaf"), None), P("leaf", "rows"))
    return jax.shard_map(
        per_device, mesh=mesh, in_specs=in_specs, out_specs=out_specs, check_vma=False
    )
```

time: 388 us -> 416 us (1.072)
  waiting for transfers between devices: 88.1 us -> 126 us
  Pallas kernels: 68.7 us -> 40.6 us
  starting transfers between devices: 34.8 us -> 48.4 us
  local copies, waits for them, and re-layouts: 12.3 us -> 18.1 us
    all_gather x3, waiting for transfers between devices: 9.49 us -> 61.1 us  [the longest x1 55.1 us: per_device(): lax.all_gather(factor_blocks[:kept] + placed, 'leaf', axis=0)]
    pallas_call x9, Pallas kernels: 65.7 us -> 39.4 us  [the longest x1 19.9 us: final_of(): pl.pallas_call(final_kernel, in_specs=[smem] + [vmem] * 4 + [pl.BlockSpec...]
    ppermute x18, waiting for transfers between devices: 54.9 us -> 41.1 us  [moved(): return lax.ppermute(value, axis, pairs)]
    unnamed x20 -> x34, local copies, waits for them, and re-layouts: 2.81 us -> 15.4 us
    all_to_all x1, starting transfers between devices: 11.1 us -> 21.3 us  [per_device(): lax.all_to_all(solved.reshape(rows, columns // rows, block), 'rows', 0, 0)]
    add x5, other arithmetic: 6.48 us -> 1.21 us  [scatter_sum(): pair = keep + moved(give, 'leaf', swap)]
  transfers between devices with their start and end apart: 23 -> 23, of which waited for: 13 -> 14; matrix products, arithmetic and copies ran while one was open for 5% -> 3% of each run, Pallas kernels for 18% -> 8%
where the time goes in v1:
time: 416 us; the launch traced here: 415 us
  blocking collectives  156 us (38%)
  waiting for transfers between devices  126 us (30%)
  starting transfers between devices  48.4 us (12%)
  Pallas kernels  40.6 us (10%)
  local copies, waits for them, and re-layouts  18.1 us (4%)
  between operations  14.3 us (3%)
  other arithmetic  11 us (3%)
    all_to_all x4, blocking collectives, scatter_sum(): got = lax.all_to_all(pair, 'leaf', 0, 0, axis_index_groups=same)  86.4 us
    all_to_all x3, blocking collectives, collect(): own = lax.all_to_all(spread, 'leaf', 0, 0, axis_index_groups=same)  69.3 us
    all_gather x1, waiting for transfers between devices, per_device(): lax.all_gather(factor_blocks[:kept] + placed, 'leaf', axis=0)  55.1 us
    ppermute x18, waiting for transfers between devices, moved(): return lax.ppermute(value, axis, pairs)  41.1 us
    ppermute x18, starting transfers between devices, moved(): return lax.ppermute(value, axis, pairs)  23.5 us
    all_to_all x1, starting transfers between devices, per_device(): lax.all_to_all(solved.reshape(rows, columns // rows, block), 'rows', 0, 0)  21.3 us
    pallas_call x1, Pallas kernels, final_of(): pl.pallas_call(final_kernel, in_specs=[smem] + [vmem] * 4 + [pl.BlockSpec...  19.9 us
    all_to_all x1, waiting for transfers between devices, scatter_sum(): got = lax.all_to_all(pair, 'leaf', 0, 0, axis_index_groups=same)  17.9 us
  transfers between devices with their start and end apart: 23, of which 14 were waited for; matrix products, arithmetic and copies ran while one was open for 3% of the time, Pallas kernels for 8%

profile of v1, /device:TPU:1, one launch (start us, length us, event | category | flops | bytes accessed | tf_op | source)
XLA Modules:
  0.0 415.2 jit_solution(3324821823808069618)
XLA Ops:
  7.3 2.2 copy-done
  9.5 0.9 copy-done.4
  10.4 2.6 weights.1
  13.0 3.3 collective-permute-start
  16.3 1.5 collective-permute-done
  17.9 23.0 %all_to_all.45 = f32[8,128,128]{2,1,0:T(8,128)S(1)} all-to-all(f32[8,128,128]{2,1,0:T(8,128)S(1)} %add.50), channel_id=1, replica_groups={{0,2,4,6,8,10,12,14},{1,3,5,7,9,11,13,15},{16,18,20,22,24,26,28,30},{17..., dimensions={0} | all-to-all | bytes 1048576 | tf_op jit(solution)/shard_map/all_to_all | solution.py:379
  41.0 17.3 %all_to_all.46.own_ref = f32[8,128,128]{2,1,0:T(8,128)S(1)} all-to-all(f32[8,128,128]{2,1,0:T(8,128)S(1)} %broadcast_in_dim.36), channel_id=1, replica_groups={{0,2,4,6,8,10,12,14},{1,3,5,7,9,11,13,15},{16,18,20,22,24,26,28,30},{17..., dimensions={0} | all-to-all | bytes 1048576 | tf_op jit(solution)/shard_map/all_to_all | solution.py:386
  58.3 3.6 collective-permute-start.1
  61.8 1.5 collective-permute-done.1.other_ref
  63.4 1.2 coeffs.1
  64.6 20.5 %all_to_all.47.own_ref = f32[8,128,128]{2,1,0:T(8,128)S(1)} all-to-all(f32[8,128,128]{2,1,0:T(8,128)S(1)} %coeffs.1), channel_id=1, replica_groups={{0,2,4,6,8,10,12,14},{1,3,5,7,9,11,13,15},{16,18,20,22,24,26,28,30},{17..., dimensions={0} | all-to-all | bytes 1048576 | tf_op jit(solution)/shard_map/all_to_all | solution.py:386
  85.6 1.5 collective-permute-done.2.other_ref
  87.1 2.2 copy-done.1
  89.3 4.0 lowered.1
  93.3 2.4 collective-permute-start.17
  95.8 1.0 fusion.3
  96.9 0.9 fusion.1
  98.6 1.3 collective-permute-start.4
  100.0 27.8 %collective-permute-done.4 = f32[7,128,128]{2,1,0:T(8,128)} collective-permute-done((f32[7,128,128]{2,1,0:T(8,128)S(1)}, f32[7,128,128]{2,1,0:T(8,128)}, u32[]{:S(2)}, u32[]{:S(2)}) %collective-permute-start.4) | collective-permute-done | bytes 458784 | tf_op jit(solution)/shard_map/ppermute | solution.py:358
  127.8 1.9 fusion
  129.8 6.0 %all-gather.9.cloned.1.call-done = f32[272,8,128]{2,1,0:T(8,128)} async-done(((f32[17,8,128]{2,1,0:T(8,128)}), f32[272,8,128]{2,1,0:T(8,128)}) %all-gather.9.cloned.1.call-update) | async-done | bytes 1114128 | tf_op jit(solution)/shard_map/all_gather | solution.py:418
  135.9 1.2 copy-done.3
  137.1 0.9 fold.1
  138.1 3.2 collective-permute-start.3
  141.3 1.3 collective-permute-done.3
  142.7 55.1 %all-gather.7.cloned.1.call-done = f32[144,128,128]{2,1,0:T(8,128)} async-done(((f32[9,128,128]{2,1,0:T(8,128)}), f32[144,128,128]{2,1,0:T(8,128)}) %all-gather.7.cloned.1.call-update) | async-done | bytes 9437200 | tf_op jit(solution)/shard_map/all_gather | solution.py:398
  197.8 3.7 copy-done.2
  201.5 7.6 %joint.1 = (bf16[256,2048]{1,0:T(8,128)(2,1)S(1)}, bf16[256,2048]{1,0:T(8,128)(2,1)S(1)}) custom-call(s32[2]{0:T(128)S(1)} %pad_add_fusion.where_ref, f32[128,2048]{1,0:T(8,128)S(1)} %bitcast.40, f32[16,1152,128]{2,1,0:T(8,128)S(1)} %bitcast.37), custom_call_target="tpu_custom_call" | custom-call | flops 1610612736 | bytes 9437184 | tf_op jit(solution)/shard_map/joint/pallas_call | solution.py:212
  209.1 1.1 level.4
  210.6 1.7 collective-permute-done.5
  212.3 21.3 %all_to_all.48 = f32[8,128,128]{2,1,0:T(8,128)} all-to-all(f32[8,128,128]{2,1,0:T(8,128)S(1)} %add.52), channel_id=1, replica_groups={{0,2,4,6,8,10,12,14},{1,3,5,7,9,11,13,15},{16,18,20,22,24,26,28,30},{17..., dimensions={0} | all-to-all | bytes 1048576 | tf_op jit(solution)/shard_map/all_to_all | solution.py:379
  233.6 1.1 reduce_sum.46
  234.8 0.7 collective-permute-start.7
  235.5 0.7 collective-permute-start.6
  236.9 1.1 level.5
  238.0 1.3 collective-permute-start.8
  239.3 1.5 collective-permute-done.8
  240.9 21.1 %all_to_all.49 = f32[8,128,128]{2,1,0:T(8,128)} all-to-all(f32[8,128,128]{2,1,0:T(8,128)S(1)} %add.53), channel_id=1, replica_groups={{0,2,4,6,8,10,12,14},{1,3,5,7,9,11,13,15},{16,18,20,22,24,26,28,30},{17..., dimensions={0} | all-to-all | bytes 1048576 | tf_op jit(solution)/shard_map/all_to_all | solution.py:379
  262.0 1.1 reduce_sum.47
  263.2 0.6 sub.17
  263.8 0.7 collective-permute-start.10
  264.5 0.7 collective-permute-start.9
  265.9 1.1 level.6
  267.6 1.5 collective-permute-done.11
  269.2 21.1 %all_to_all.50 = f32[8,128,128]{2,1,0:T(8,128)} all-to-all(f32[8,128,128]{2,1,0:T(8,128)S(1)} %add.54), channel_id=1, replica_groups={{0,2,4,6,8,10,12,14},{1,3,5,7,9,11,13,15},{16,18,20,22,24,26,28,30},{17..., dimensions={0} | all-to-all | bytes 1048576 | tf_op jit(solution)/shard_map/all_to_all | solution.py:379
  290.3 1.1 reduce_sum.48
  291.5 0.6 sub.18
  292.1 0.7 collective-permute-start.13
  292.8 1.3 collective-permute-start.12
  294.7 0.9 copy.28.lower_ref
  295.6 1.1 level.7
  297.4 1.5 collective-permute-done.14
  298.9 0.9 add.55
  299.8 3.5 all-to-all-start.6
  303.3 17.9 %all-to-all-done.6 = f32[8,128,128]{2,1,0:T(8,128)S(1)} async-done(((f32[8,128,128]{2,1,0:T(8,128)}), f32[8,128,128]{2,1,0:T(8,128)S(1)}, u32[]{:S(2)}, u32[]{:S(2)}) %all-to-all-start.6) | async-done | bytes 524320 | tf_op jit(solution)/shard_map/all_to_all | solution.py:379
  321.3 0.9 select_bitcast_fusion.1
  322.3 31.5 %all_to_all.51.own_ref = f32[8,2,128,128]{3,2,1,0:T(8,128)S(1)} all-to-all(f32[8,2,128,128]{3,2,1,0:T(8,128)S(1)} %broadcast_in_dim.38), channel_id=1, replica_groups={{0,2,4,6,8,10,12,14},{1,3,5,7,9,11,13,15},{16,18,20,22,24,26,28,30},{17..., dimensions={0} | all-to-all | bytes 2097152 | tf_op jit(solution)/shard_map/all_to_all | solution.py:386
  354.5 1.3 collective-permute-start.15
  355.8 1.1 collective-permute-done.16.other_ref
  356.8 3.5 copy-done.8
  360.4 19.9 %final.1 = (f32[128,128]{1,0:T(8,128)S(1)}, f32[128,128]{1,0:T(8,128)}) custom-call(s32[2]{0:T(128)S(1)} %pad_add_fusion.where_ref, f32[8,2,128,128]{3,2,1,0:T(8,128)S(1)} %all_to_all.51.own_ref, f32[8,2,128,128]{3,2,1,0:T(8,128)} %collective-permute-done.16.other_ref, f32[128,128]{1,0:T(8,128)S(1)} %select_bitcast_fusion.summit_ref, ...), custom_call_target="tpu_custom_call" | custom-call | flops 4294967296 | bytes 8912896 | tf_op jit(solution)/shard_map/final/pallas_call | solution.py:337
  380.2 21.3 %all-to-all-start.8 = ((f32[16,8,128]{2,1,0:T(8,128)}), f32[16,8,128]{2,1,0:T(8,128)S(1)}, u32[]{:S(2)}, u32[]{:S(2)}) async-start(f32[16,8,128]{2,1,0:T(8,128)} %bitcast.18), calls=%async_computation.8 | async-start | bytes 131072 | tf_op jit(solution)/shard_map/all_to_all | solution.py:446
  401.5 0.6 fusion.2
  402.2 5.9 %all-to-all-done.8 = f32[16,8,128]{2,1,0:T(8,128)S(1)} async-done(((f32[16,8,128]{2,1,0:T(8,128)}), f32[16,8,128]{2,1,0:T(8,128)S(1)}, u32[]{:S(2)}, u32[]{:S(2)}) %all-to-all-start.8) | async-done | bytes 65568 | tf_op jit(solution)/shard_map/all_to_all | solution.py:446
  (78 shorter events, 7.4 us)
Async XLA Ops:
  7.2 128.7 %all-gather.9.cloned.1.call-start = ((), (), s32[]{:S(2)}) async-start(), calls=%async_computation.10 | async-start | bytes 1183744 | tf_op jit(solution)/shard_map/all_gather | solution.py:418
  7.3 2.2 copy-start
  9.5 0.9 copy-start.4
  10.4 52.9 %copy-start.6 = (f32[1,2048,128]{2,1,0:T(8,128)S(1)}, f32[1,2048,128]{2,1,0:T(8,128)}, u32[]{:S(2)}) copy-start(f32[1,2048,128]{2,1,0:T(8,128)} %param.9) | copy-start | bytes 3145732
  13.0 4.9 %collective-permute-start = (f32[8,128,128]{2,1,0:T(8,128)S(1)}, f32[8,128,128]{2,1,0:T(8,128)S(1)}, u32[]{:S(2)}, u32[]{:S(2)}) collective-permute-start(f32[8,128,128]{2,1,0:T(8,128)S(1)} %get-tuple-element.22), channel_id=1, source_target_pairs={{0,1},{1,0},{2,3},{3,2},{4,5},{5,4},{6,7},{7,6},{8,9},{9,8},{10,11... | collective-permute-start | bytes 1572872 | tf_op jit(solution)/shard_map/ppermute | solution.py:358
  17.9 69.3 %copy-start.5 = (f32[512,128]{1,0:T(8,128)S(1)}, f32[512,128]{1,0:T(8,128)}, u32[]{:S(2)}) copy-start(f32[512,128]{1,0:T(8,128)} %side_ref.3) | copy-start | bytes 786436
  58.3 5.1 %collective-permute-start.1 = (f32[8,128,128]{2,1,0:T(8,128)S(1)}, f32[8,128,128]{2,1,0:T(8,128)S(1)}, u32[]{:S(2)}, u32[]{:S(2)}) collective-permute-start(f32[8,128,128]{2,1,0:T(8,128)S(1)} %all_to_all.46.own_ref), channel_id=1, source_target_pairs={{0,1},{1,0},{2,3},{3,2},{4,5},{5,4},{6,7},{7,6},{8,9},{9,8},{10,11... | collective-permute-start | bytes 1572872 | tf_op jit(solution)/shard_map/ppermute | solution.py:358
  63.4 30.0 %copy-start.16 = (f32[128,128]{1,0:T(8,128)S(1)}, f32[128,128]{1,0:T(8,128)}, u32[]{:S(2)}) copy-start(f32[128,128]{1,0:T(8,128)} %param.13) | copy-start | bytes 196612
  64.6 34.0 %copy-start.9 = (f32[1,2048,128]{2,1,0:T(8,128)S(1)}, f32[1,2048,128]{2,1,0:T(8,128)}, u32[]{:S(2)}) copy-start(f32[1,2048,128]{2,1,0:T(8,128)} %param.11) | copy-start | bytes 3145732
  85.1 2.0 collective-permute-start.2
  87.1 2.2 copy-start.1
  93.3 104.5 %copy-start.7 = (f32[1,128,2048]{2,1,0:T(8,128)S(1)}, f32[1,128,2048]{2,1,0:T(8,128)}, u32[]{:S(2)}) copy-start(f32[1,128,2048]{2,1,0:T(8,128)} %param.10) | copy-start | bytes 3145732
  93.3 3.4 collective-permute-start.17
  98.5 99.3 %all-gather.7.cloned.1.call-start = ((), (), s32[]{:S(2)}) async-start(), calls=%async_computation.9 | async-start | bytes 10027008 | tf_op jit(solution)/shard_map/all_gather | solution.py:398
  98.6 29.2 %collective-permute-start.4 = (f32[7,128,128]{2,1,0:T(8,128)S(1)}, f32[7,128,128]{2,1,0:T(8,128)}, u32[]{:S(2)}, u32[]{:S(2)}) collective-permute-start(f32[7,128,128]{2,1,0:T(8,128)S(1)} %bitcast.44), channel_id=1, source_target_pairs={{8,7},{9,6},{10,5},{11,4},{12,3},{13,2},{14,1},{15,0},{24,23},{25,... | collective-permute-start | bytes 1376264 | tf_op jit(solution)/shard_map/ppermute | solution.py:358
  129.8 226.0 %all-gather.11.cloned.1.call-start = ((), (), s32[]{:S(2)}) async-start(), calls=%async_computation.11 | async-start | bytes 9469952 | tf_op jit(solution)/shard_map/all_gather | solution.py:419
  135.9 1.2 copy-start.3
  138.1 4.6 %collective-permute-start.3 = (f32[128,128]{0,1:T(8,128)S(1)}, f32[128,128]{0,1:T(8,128)S(1)}, u32[]{:S(2)}, u32[]{:S(2)}) collective-permute-start(f32[128,128]{0,1:T(8,128)S(1)} %copy.18), channel_id=1, source_target_pairs={{0,16},{32,48},{64,80},{96,112},{128,144},{160,176},{192,208},{224... | collective-permute-start | bytes 196616 | tf_op jit(solution)/shard_map/ppermute | solution.py:358
  197.8 3.7 copy-start.2
  210.2 2.0 collective-permute-start.5
  234.8 1.3 collective-permute-start.7
  235.5 1.3 collective-permute-start.6
  236.1 0.6 copy-start.10
  238.0 2.8 collective-permute-start.8
  263.8 1.3 collective-permute-start.10
  264.5 1.3 collective-permute-start.9
  265.2 0.6 copy-start.12
  267.0 2.1 collective-permute-start.11
  292.1 2.0 collective-permute-start.13
  292.8 1.9 collective-permute-start.12
  294.1 0.6 copy-start.14
  296.8 57.7 %copy-start.11 = (f32[128,128]{0,1:T(8,128)S(1)}, f32[128,128]{0,1:T(8,128)}, u32[]{:S(2)}) copy-start(f32[128,128]{0,1:T(8,128)} %copy-done.10) | copy-start | bytes 196612
  296.8 57.7 %copy-start.13 = (f32[128,128]{0,1:T(8,128)S(1)}, f32[128,128]{0,1:T(8,128)}, u32[]{:S(2)}) copy-start(f32[128,128]{0,1:T(8,128)} %copy-done.12) | copy-start | bytes 196612
  296.8 57.7 %copy-start.15 = (f32[128,128]{0,1:T(8,128)S(1)}, f32[128,128]{0,1:T(8,128)}, u32[]{:S(2)}) copy-start(f32[128,128]{0,1:T(8,128)} %copy-done.14) | copy-start | bytes 196612
  296.8 2.1 collective-permute-start.14
  299.8 21.4 %all-to-all-start.6 = ((f32[8,128,128]{2,1,0:T(8,128)}), f32[8,128,128]{2,1,0:T(8,128)S(1)}, u32[]{:S(2)}, u32[]{:S(2)}) async-start(f32[8,128,128]{2,1,0:T(8,128)} %add.55), calls=%async_computation.6 | async-start | bytes 1048576 | tf_op jit(solution)/shard_map/all_to_all | solution.py:379
  353.8 3.0 collective-permute-start.16
  354.5 47.1 %collective-permute-start.15 = (f32[128,128]{0,1:T(8,128)S(1)}, f32[128,128]{0,1:T(8,128)S(1)}, u32[]{:S(2)}, u32[]{:S(2)}) collective-permute-start(f32[128,128]{0,1:T(8,128)S(1)} %get-tuple-element.41), channel_id=1, source_target_pairs={{128,0},{129,1},{130,2},{131,3},{132,4},{133,5},{134,6},{135,7},{1... | collective-permute-start | bytes 196616 | tf_op jit(solution)/shard_map/ppermute | solution.py:358
  356.8 3.5 copy-start.8
  380.2 27.8 %all-to-all-start.8 = ((f32[16,8,128]{2,1,0:T(8,128)}), f32[16,8,128]{2,1,0:T(8,128)S(1)}, u32[]{:S(2)}, u32[]{:S(2)}) async-start(f32[16,8,128]{2,1,0:T(8,128)} %bitcast.18), calls=%async_computation.8 | async-start | bytes 131072 | tf_op jit(solution)/shard_map/all_to_all | solution.py:446
Sparse Core Ops, SparseCore 0:
  98.7 37.1 all-gather.8
  137.7 60.0 all-gather.6
  200.3 76.2 all-gather.10

commit v2 on v1

v2 whole, which is shorter than its diff:
```python
import functools

import jax
import jax.numpy as jnp
from jax import lax
from jax.experimental import pallas as pl
from jax.experimental.pallas import tpu as pltpu
from jax.sharding import PartitionSpec as P

SIDE = 128
GROUP = 4
SPLIT = (((1,), (0,)), ((), ()))
SMALL = 24 * 1024 * 1024
LARGE = 56 * 1024 * 1024


def halves(value):
    high = value.astype(jnp.bfloat16)
    low = (value - high.astype(jnp.float32)).astype(jnp.bfloat16)
    return high, low


def once(left, right):
    return lax.dot_general(left, right, SPLIT, preferred_element_type=jnp.float32)


def thrice(left, right):
    return once(left[0], right[0]) + (once(left[0], right[1]) + once(left[1], right[0]))


def stacked(left, right):
    size = left[0].shape[0]
    both = once(jnp.concatenate(left, axis=0), right[0])
    return both[:size] + (both[size:] + once(left[0], right[1]))


def pick(parity, own, other):
    first = parity == 0
    return jnp.where(first, own, other), jnp.where(first, other, own)


smem = pl.BlockSpec(memory_space=pltpu.SMEM)


vmem = pl.BlockSpec(memory_space=pltpu.VMEM)


def params(limit=SMALL):
    return pltpu.CompilerParams(vmem_limit_bytes=limit)


def cost(flops, size):
    return pl.CostEstimate(flops=flops, bytes_accessed=size, transcendentals=0)


def shaped(*shape, dtype=jnp.float32):
    return jax.ShapeDtypeStruct(shape, dtype)


def weights_kernel(where_ref, side_ref, vectors_ref, keep_ref, give_ref, high_ref, low_ref):
    @pl.when(pl.program_id(0) == 0)
    def _():
        high, low = halves(side_ref[...].T)
        high_ref[...] = high
        low_ref[...] = low

    first = where_ref[0] == 0
    for n in range(keep_ref.shape[0]):
        vectors = vectors_ref[:, 2 * n * SIDE:(2 * n + 2) * SIDE]
        out = stacked((high_ref[...], low_ref[...]), halves(vectors))
        even, odd = out[:, :SIDE], out[:, SIDE:]
        keep_ref[n] = jnp.where(first, even, odd)
        give_ref[n] = jnp.where(first, odd, even)


def weights_of(where, side, vectors):
    tall, order = vectors.shape
    columns = side.shape[1]
    steps = order // (2 * SIDE)
    block = pl.BlockSpec((GROUP, columns, SIDE), lambda n: (n, 0, 0))
    return pl.pallas_call(
        weights_kernel,
        grid=(steps // GROUP,),
        in_specs=[
            smem,
            pl.BlockSpec((tall, columns), lambda n: (0, 0)),
            pl.BlockSpec((tall, 2 * GROUP * SIDE), lambda n: (0, n)),
        ],
        out_specs=[block, block],
        out_shape=[shaped(steps, columns, SIDE)] * 2,
        scratch_shapes=[pltpu.VMEM((columns, tall), jnp.bfloat16)] * 2,
        compiler_params=params(LARGE),
        cost_estimate=cost(6 * tall * columns * order, 4 * vectors.size),
        name="weights",
    )(where, side, vectors)


def coeffs_kernel(where_ref, own_ref, other_ref, factor_ref, out_ref):
    parity = where_ref[0]
    steps = own_ref.shape[0]
    total = jnp.zeros(own_ref.shape[1:], jnp.float32)
    for n in range(steps):
        left = jnp.concatenate(pick(parity, own_ref[n], other_ref[n]), axis=1)
        right = factor_ref[2 * n * SIDE:(2 * n + 2) * SIDE, :]
        total = total + stacked(halves(left), halves(right))
    total = total.T
    for n in range(steps):
        out_ref[n] = total


def coeffs_of(where, own, other, factor):
    return pl.pallas_call(
        coeffs_kernel,
        in_specs=[smem] + [pl.BlockSpec(memory_space=pltpu.VMEM)] * 3,
        out_shape=shaped(own.shape[0], SIDE, own.shape[1]),
        compiler_params=params(),
        cost_estimate=cost(6 * own.shape[1] * factor.size, 4 * factor.size),
        name="coeffs",
    )(where, own, other, factor)


def lowered_kernel(where_ref, own_ref, other_ref, vectors_ref, side_ref, out_ref, top_ref):
    step = pl.program_id(0)

    @pl.when(step == 0)
    def _():
        out_ref[...] = side_ref[...]

    total = out_ref[...]
    for n in range(own_ref.shape[0]):
        right = jnp.concatenate(pick(where_ref[0], own_ref[n], other_ref[n]), axis=0)
        vectors = vectors_ref[:, 2 * n * SIDE:(2 * n + 2) * SIDE]
        total = total - thrice(halves(vectors), halves(right))
    out_ref[...] = total

    @pl.when(step == pl.num_programs(0) - 1)
    def _():
        top_ref[...] = out_ref[:SIDE, :].T


def lowered_of(where, own, other, vectors, side):
    tall, order = vectors.shape
    columns = side.shape[1]
    steps = order // (2 * SIDE)
    block = pl.BlockSpec((GROUP, SIDE, columns), lambda n: (n, 0, 0))
    whole = pl.BlockSpec((tall, columns), lambda n: (0, 0))
    return pl.pallas_call(
        lowered_kernel,
        grid=(steps // GROUP,),
        in_specs=[
            smem, block, block, pl.BlockSpec((tall, 2 * GROUP * SIDE), lambda n: (0, n)), whole,
        ],
        out_specs=[whole, pl.BlockSpec((columns, SIDE), lambda n: (0, 0))],
        out_shape=[shaped(tall, columns), shaped(columns, SIDE)],
        compiler_params=params(LARGE),
        cost_estimate=cost(6 * tall * columns * order, 4 * vectors.size),
        name="lowered",
    )(where, own, other, vectors, side)


def slot_of(k, count):
    return (k + 10) % count if k < count - 2 else k + 2 - count


def joint_kernel(where_ref, reflect_ref, factor_ref, high_ref, low_ref, panel_ref, sems):
    count, kept, _ = factor_ref.shape
    order = reflect_ref.shape[1]
    steps = count // 2
    spare = order - kept
    copies = [None] * count
    for n in range(steps):
        for k in (n, n + steps):
            edge = (k + 1) * SIDE
            rows = pl.ds(0, min(edge, kept))
            copies[k] = [
                pltpu.make_async_copy(factor_ref.at[k, rows], panel_ref.at[k, rows], sems.at[0, k])
            ]
            if edge > kept:
                copies[k].append(
                    pltpu.make_async_copy(
                        factor_ref.at[slot_of(k, count), pl.ds(kept - spare, edge - kept)],
                        panel_ref.at[k, pl.ds(kept, edge - kept)],
                        sems.at[1, k],
                    )
                )
            for copy in copies[k]:
                copy.start()
    reflect = halves(reflect_ref[...])
    own = where_ref[1]
    zero = jnp.zeros((SIDE, SIDE), jnp.float32)
    for n in range(steps):
        far = n + steps
        for copy in copies[n] + copies[far]:
            copy.wait()
        edge, stop = (n + 1) * SIDE, (far + 1) * SIDE
        near_part, far_part = halves(panel_ref[n, 0:edge]), halves(panel_ref[far, 0:stop])
        shared = [jnp.concatenate([s, t[:edge]], axis=1) for s, t in zip(near_part, far_part)]
        both = stacked([r[:, :edge] for r in reflect], shared)
        rest = stacked([r[:, edge:stop] for r in reflect], [t[edge:] for t in far_part])
        for k, top in ((n, both[:, :SIDE]), (far, both[:, SIDE:] + rest)):
            mine = pl.ds(pl.multiple_of(jnp.minimum(own, k) * SIDE, SIDE), SIDE)
            bottom = jnp.where(own <= k, panel_ref[k, mine, :], zero)
            at = pl.ds(k * SIDE, SIDE)
            for ref, part in zip((high_ref, low_ref), zip(halves(top), halves(bottom))):
                ref[0:SIDE, at] = part[0]
                ref[SIDE:2 * SIDE, at] = part[1]


def joint_of(where, reflect, factor):
    block, order = reflect.shape
    count = factor.shape[0]
    return pl.pallas_call(
        joint_kernel,
        in_specs=[smem, vmem, pl.BlockSpec(memory_space=pltpu.HBM)],
        out_specs=[vmem] * 2,
        out_shape=[shaped(2 * block, order, dtype=jnp.bfloat16)] * 2,
        scratch_shapes=[
            pltpu.VMEM((count, order, SIDE), jnp.float32),
            pltpu.SemaphoreType.DMA((2, count)),
        ],
        compiler_params=params(LARGE),
        cost_estimate=cost(3 * block * order * order, 2 * factor.size),
        name="joint",
    )(where, reflect, factor)


def level_kernel(where_ref, upper_ref, lower_ref, high_ref, low_ref, keep_ref, give_ref):
    first = where_ref[0] == 0
    left = halves(jnp.concatenate([upper_ref[...], lower_ref[...]], axis=1))
    for n in range(keep_ref.shape[0]):
        at = pl.ds(2 * n * SIDE, 2 * SIDE)
        out = stacked(left, (high_ref[:, at], low_ref[:, at]))
        even, odd = out[:, :SIDE], out[:, SIDE:]
        keep_ref[n] = jnp.where(first, even, odd)
        give_ref[n] = jnp.where(first, odd, even)


def level_of(where, upper, lower, joint):
    columns = upper.shape[0]
    wide, order = joint[0].shape
    steps = order // (2 * SIDE)
    return pl.pallas_call(
        level_kernel,
        in_specs=[smem] + [vmem] * 4,
        out_specs=[vmem] * 2,
        out_shape=[shaped(steps, columns, SIDE)] * 2,
        compiler_params=params(),
        cost_estimate=cost(6 * columns * wide * order, 4 * wide * order),
        name="level",
    )(where, upper, lower, *joint)


def fold_kernel(pieces_ref, out_ref):
    count = pieces_ref.shape[0]
    for n in range(count // 2):
        far = count - 1 - n
        out_ref[n, 0:far] = pieces_ref[n, n + 1:count]
        out_ref[n, far] = pieces_ref[n, count]
        for k in range(far + 1, count):
            out_ref[n, k] = pieces_ref[far, k]
        out_ref[n, count] = pieces_ref[far, count]


def fold_of(pieces):
    count = pieces.shape[0]
    return pl.pallas_call(
        fold_kernel,
        in_specs=[vmem],
        out_specs=vmem,
        out_shape=shaped(count // 2, *pieces.shape[1:]),
        compiler_params=params(),
        name="fold",
    )(pieces)


def final_kernel(
    where_ref, own_ref, other_ref, summit_ref, back_ref, reflect_ref, rotated_ref, folded_ref,
    out_ref, solved_ref, coeffs_ref, whole_ref, top_ref, panel_ref, sems, out_sems,
):
    parity = where_ref[0]
    steps = own_ref.shape[0]
    count = 2 * steps
    copies = []
    for p in range(count // 4):
        copy = pltpu.make_async_copy(
            folded_ref.at[:, 2 * p:2 * p + 2], panel_ref.at[p], sems.at[p]
        )
        copy.start()
        copies.append(copy)
    rest = pl.ds(SIDE, rotated_ref.shape[0] - SIDE)
    rest_copy = pltpu.make_async_copy(rotated_ref.at[rest], out_ref.at[rest], out_sems.at[0])
    rest_copy.start()
    for n in range(steps):
        for k, value in enumerate(pick(parity, own_ref[n], other_ref[n])):
            at = pl.ds((2 * n + k) * SIDE, SIDE)
            coeffs_ref[at, :] = value[:SIDE]
            whole_ref[at, :] = value[SIDE:].T
    lowered = thrice(halves(reflect_ref[...]), halves(coeffs_ref[...]))
    lowered = jnp.where(where_ref[2] == 0, back_ref[...], summit_ref[...] - lowered.T)
    top_ref[...] = lowered.T
    top_copy = pltpu.make_async_copy(top_ref, out_ref.at[0:SIDE], out_sems.at[1])
    top_copy.start()

    def block_at(row, column):
        near = min(row, count - 1 - row)
        if row >= count // 2:
            at = column
        else:
            at = count - 1 - row if column == count else column - row - 1
        return panel_ref[near // 2, :, near % 2, at].reshape(SIDE, SIDE)

    zero = jnp.zeros((SIDE, SIDE), jnp.float32)

    def band_of(q, start, stop):
        bands = [
            jnp.concatenate([block_at(k, j) for j in range(start, stop)], axis=1)
            for k in (2 * q, 2 * q + 1)
        ]
        return halves(jnp.concatenate(bands, axis=0))

    last = count // 2 - 1
    solved = [None] * (last + 1)
    ready = whole_ref[pl.ds(2 * last * SIDE, 2 * SIDE), :]
    for q in reversed(range(last + 1)):
        a, b = 2 * q, 2 * q + 1
        if q == last:
            copies[0].wait()
            copies[1].wait()
        inverse = jnp.concatenate(
            [
                jnp.concatenate([block_at(a, count), -block_at(a, b)], axis=1),
                jnp.concatenate([zero, block_at(b, count)], axis=1),
            ],
            axis=0,
        )
        value = ready
        if q < last:
            value = value - thrice(band_of(q, b + 1, b + 3), solved[q + 1])
        value = thrice(halves(inverse), halves(value))
        whole_ref[pl.ds(a * SIDE, 2 * SIDE), :] = value
        solved[q] = halves(value)
        if q > 0:
            ready = whole_ref[pl.ds((a - 2) * SIDE, 2 * SIDE), :]
            if q < last:
                if q - 1 > last // 2:
                    copies[last - q + 1].wait()
                known = [
                    jnp.concatenate([pair[part] for pair in solved[q + 1:]], axis=0)
                    for part in range(2)
                ]
                ready = ready - thrice(band_of(q - 1, b + 1, count), known)
    mine = pl.ds(pl.multiple_of(where_ref[1] * SIDE, SIDE), SIDE)
    solved_ref[...] = whole_ref[mine, :]
    rest_copy.wait()
    top_copy.wait()


def final_of(where, own, other, summit, back, reflect, rotated, folded):
    columns = summit.shape[0]
    order = reflect.shape[1]
    rows, near, long = folded.shape[:3]
    narrow = own.shape[1] - SIDE
    hbm = pl.BlockSpec(memory_space=pltpu.HBM)
    return pl.pallas_call(
        final_kernel,
        in_specs=[smem] + [vmem] * 5 + [hbm] * 2,
        out_specs=[hbm, vmem],
        out_shape=[shaped(*rotated.shape), shaped(SIDE, narrow)],
        scratch_shapes=[
            pltpu.VMEM((order, columns), jnp.float32),
            pltpu.VMEM((order, narrow), jnp.float32),
            pltpu.VMEM((SIDE, columns), jnp.float32),
            pltpu.VMEM((near // 2, rows, 2, long) + folded.shape[3:], jnp.float32),
            pltpu.SemaphoreType.DMA((near // 2,)),
            pltpu.SemaphoreType.DMA((2,)),
        ],
        compiler_params=params(LARGE),
        cost_estimate=cost(8 * columns * order * order, 4 * folded.size),
        name="final",
    )(where, own, other, summit, back, reflect, rotated, folded)


def dot(left, right):
    return jnp.dot(left, right, precision=lax.Precision.HIGHEST, preferred_element_type=jnp.float32)


def moved(value, axis, pairs):
    return lax.ppermute(value, axis, pairs)


def per_device(
    right_side, reflectors, leaf_factor, node_reflect, node_factor, upper_blocks, block_inverse
):
    block = upper_blocks.shape[0]
    columns = right_side.shape[1]
    count = lax.axis_size("leaf")
    rows = lax.axis_size("rows")
    half = count // 2
    row_index = lax.axis_index("rows")
    leaf_index = lax.axis_index("leaf")
    where = jnp.stack([leaf_index % 2, leaf_index, row_index]).astype(jnp.int32)
    swap = [(i, i ^ 1) for i in range(count)]
    same = [list(range(k, count, 2)) for k in range(2)]

    def pair_sum(parts):
        keep, give = parts
        return keep + moved(give, "leaf", swap)

    def scatter_pair(pair):
        got = lax.all_to_all(pair, "leaf", 0, 0, axis_index_groups=same)
        return jnp.sum(got, axis=0)

    def copies(mine):
        return jnp.broadcast_to(mine[None], (half,) + mine.shape)

    def collect(spread):
        own = lax.all_to_all(spread, "leaf", 0, 0, axis_index_groups=same)
        return own, moved(own, "leaf", swap)

    kept = count * 3 // 4 * block
    spare = count * block - kept
    sources = range(count * 3 // 4, count)
    given = moved(node_factor[0, kept:], "leaf", [(k, slot_of(k, count)) for k in sources])
    keep, give = weights_of(where, right_side, reflectors)
    keep, given = lax.optimization_barrier((keep, given))
    factor_whole = lax.all_gather(
        jnp.concatenate(
            [node_factor[0, :kept - spare], node_factor[0, kept - spare:kept] + given], axis=0
        ),
        "leaf",
        axis=0,
    )
    weights_part = scatter_pair(pair_sum((keep, give)))
    spread = coeffs_of(where, *collect(copies(weights_part)), leaf_factor[0])
    rotated, top = lowered_of(where, *collect(spread), reflectors, right_side)

    upper_own, inverse_own = upper_blocks, block_inverse
    inverse_next = moved(inverse_own, "leaf", [(i + 1, i) for i in range(0, count, 2)])
    eighth = block // rows
    upper_slice = lax.dynamic_slice_in_dim(upper_own, row_index * eighth, eighth, 0)
    inverse_slice = lax.dynamic_slice_in_dim(inverse_own, row_index * eighth, eighth, 0)
    upper_slice = upper_slice.reshape(eighth, count, block).transpose(1, 0, 2)
    beside = lax.dynamic_slice_in_dim(
        upper_own, jnp.minimum(leaf_index + 1, count - 1) * block, block, 1
    )
    cross = dot(dot(inverse_slice, beside), inverse_next)
    at_cross = jnp.arange(count)[:, None, None] == leaf_index + 1
    at_cross = jnp.logical_and(at_cross, leaf_index % 2 == 0)
    upper_slice = jnp.where(at_cross, cross[None], upper_slice)
    upper_slice = jnp.concatenate([upper_slice, inverse_slice[None]], axis=0)
    upper_slice, top = lax.optimization_barrier((upper_slice, top))
    pieces = lax.all_gather(upper_slice, "leaf", axis=0)

    joint = joint_of(where, node_reflect[0], factor_whole)

    stride = 1
    upper = top
    lower = moved(top, "rows", [(i, i + 1) for i in range(0, rows, 2)])
    own_coeffs = jnp.zeros_like(top)
    own_top = top
    while stride < rows:
        if stride > 1:
            nodes = list(range(stride, rows, 2 * stride))
            upper = moved(lower, "rows", [(j + stride // 2, j) for j in nodes])
            lower = moved(lower, "rows", [(j - stride // 2, j) for j in nodes])
        share = scatter_pair(pair_sum(level_of(where, upper, lower, joint)))
        if stride == 2:
            share, pieces = lax.optimization_barrier((share, pieces))
            folded = lax.all_gather(fold_of(pieces), "rows", axis=0)
        lower = lower - share
        mine = row_index % (2 * stride) == stride
        own_coeffs = jnp.where(mine, share, own_coeffs)
        own_top = jnp.where(mine, upper, own_top)
        stride *= 2
    root = rows // 2

    back = moved(lower, "rows", [(root, 0)])
    pieces = lower.reshape(rows, columns // rows, block)
    arrived = lax.all_to_all(pieces, "rows", 0, 0)[root]
    own, other = collect(copies(jnp.concatenate([own_coeffs.T, arrived], axis=0)))
    return final_of(where, own, other, own_top, back, node_reflect[0], rotated, folded)


def solution(mesh):
    in_specs = (
        P(("rows", "leaf"), None),
        P(("rows", "leaf"), None),
        P("rows", None, "leaf"),
        P("rows", "leaf", None),
        P("rows", None, "leaf"),
        P("leaf", None),
        P("leaf", None),
    )
    out_specs = (P(("rows", "leaf"), None), P("leaf", "rows"))
    return jax.shard_map(
        per_device, mesh=mesh, in_specs=in_specs, out_specs=out_specs, check_vma=False
    )
```

time: 416 us -> 327 us (0.79)
  waiting for transfers between devices: 126 us -> 85.2 us
  blocking collectives: 156 us -> 135 us
  starting transfers between devices: 48.4 us -> 36 us
  local copies, waits for them, and re-layouts: 18.1 us -> 11.7 us
  Pallas kernels: 40.6 us -> 34.3 us
    all_gather x3, waiting for transfers between devices: 61.1 us -> 7.96 us  [the longest x1 7.92 us: per_device(): lax.all_gather(jnp.concatenate([node_factor[0, :kept - spare], node_facto...]
    all_to_all x2 -> x3, waiting for transfers between devices: 23.8 us -> 54.9 us  [the longest x2 35.1 us: scatter_pair(): got = lax.all_to_all(pair, 'leaf', 0, 0, axis_index_groups=same)]
    all_to_all x3 -> x2, blocking collectives: 69.3 us -> 42.2 us  [collect(): own = lax.all_to_all(spread, 'leaf', 0, 0, axis_index_groups=same)]
    ppermute x18, waiting for transfers between devices: 41.1 us -> 21.6 us  [moved(): return lax.ppermute(value, axis, pairs)]
    all_to_all x2 -> x3, starting transfers between devices: 24.8 us -> 11.2 us  [the longest x2 7.74 us: scatter_pair(): got = lax.all_to_all(pair, 'leaf', 0, 0, axis_index_groups=same)]
    pallas_call x1, Pallas kernels: 19.9 us -> 10.2 us  [final_of(): pl.pallas_call(final_kernel, in_specs=[smem] + [vmem] * 5 + [hbm] * 2, ou...]
    unnamed x34 -> x35, local copies, waits for them, and re-layouts: 15.4 us -> 7.87 us
    all_to_all x4, blocking collectives: 86.4 us -> 93.1 us  [the longest x3 68.6 us: scatter_pair(): got = lax.all_to_all(pair, 'leaf', 0, 0, axis_index_groups=same)]
  transfers between devices with their start and end apart: 23 -> 24, of which waited for: 14 -> 12; matrix products, arithmetic and copies ran while one was open for 3% -> 2% of each run, Pallas kernels for 8% -> 7%
where the time goes in v2:
time: 327 us; the launch traced here: 326 us
  blocking collectives  135 us (41%)
  waiting for transfers between devices  85.2 us (26%)
  starting transfers between devices  36 us (11%)
  Pallas kernels  34.3 us (10%)
  between operations  14.3 us (4%)
  local copies, waits for them, and re-layouts  11.7 us (4%)
  other arithmetic  8.01 us (2%)
    all_to_all x3, blocking collectives, scatter_pair(): got = lax.all_to_all(pair, 'leaf', 0, 0, axis_index_groups=same)  68.6 us
    all_to_all x2, blocking collectives, collect(): own = lax.all_to_all(spread, 'leaf', 0, 0, axis_index_groups=same)  42.2 us
    all_to_all x2, waiting for transfers between devices, scatter_pair(): got = lax.all_to_all(pair, 'leaf', 0, 0, axis_index_groups=same)  35.1 us
    ppermute x18, starting transfers between devices, moved(): return lax.ppermute(value, axis, pairs)  24.6 us
    all_to_all x1, blocking collectives, per_device(): arrived = lax.all_to_all(pieces, 'rows', 0, 0)[root]  24.6 us
    ppermute x18, waiting for transfers between devices, moved(): return lax.ppermute(value, axis, pairs)  21.6 us
    all_to_all x1, waiting for transfers between devices, collect(): own = lax.all_to_all(spread, 'leaf', 0, 0, axis_index_groups=same)  19.8 us
    pallas_call x1, Pallas kernels, final_of(): pl.pallas_call(final_kernel, in_specs=[smem] + [vmem] * 5 + [hbm] * 2, ou...  10.2 us
  transfers between devices with their start and end apart: 24, of which 12 were waited for; matrix products, arithmetic and copies ran while one was open for 2% of the time, Pallas kernels for 7%

profile of v2, /device:TPU:1, one launch (start us, length us, event | category | flops | bytes accessed | tf_op | source)
XLA Modules:
  0.0 325.9 jit_solution(17046919731152452166)
XLA Ops:
  7.2 1.1 slice_bitcast_fusion.1
  8.3 1.3 collective-permute-start.1
  10.3 3.8 %weights.1 = (f32[8,128,128]{2,1,0:T(8,128)}, f32[8,128,128]{2,1,0:T(8,128)}) custom-call(s32[3]{0:T(128)} %pad_add_fusion.where_ref, f32[512,128]{1,0:T(8,128)} %side_ref.3, f32[512,2048]{1,0:T(8,128)} %vectors_ref.3), custom_call_target="tpu_custom_call" | custom-call | flops 805306368 | bytes 4194304 | tf_op jit(solution)/shard_map/weights/pallas_call | solution.py:81
  14.0 1.1 slice_bitcast_fusion
  15.1 6.9 %collective-permute-done.1 = f32[512,128]{1,0:T(8,128)S(1)} collective-permute-done((f32[512,128]{1,0:T(8,128)S(1)}, f32[512,128]{1,0:T(8,128)S(1)}, u32[]{:S(2)}, u32[]{:S(2)}) %collective-permute-start.1) | collective-permute-done | bytes 262176 | tf_op jit(solution)/shard_map/ppermute | solution.py:388
  22.0 1.0 bitcast_add_fusion
  23.0 0.9 pad_maximum_fusion
  24.0 1.3 collective-permute-start.2
  25.3 1.7 collective-permute-done.2
  27.0 1.1 add.51
  28.1 26.0 %all_to_all.45 = f32[8,128,128]{2,1,0:T(8,128)S(1)} all-to-all(f32[8,128,128]{2,1,0:T(8,128)S(1)} %add.51), channel_id=1, replica_groups={{0,2,4,6,8,10,12,14},{1,3,5,7,9,11,13,15},{16,18,20,22,24,26,28,30},{17..., dimensions={0} | all-to-all | bytes 1048576 | tf_op jit(solution)/shard_map/all_to_all | solution.py:410
  54.2 24.8 %all_to_all.46.own_ref = f32[8,128,128]{2,1,0:T(8,128)S(1)} all-to-all(f32[8,128,128]{2,1,0:T(8,128)S(1)} %broadcast_in_dim.39), channel_id=1, replica_groups={{0,2,4,6,8,10,12,14},{1,3,5,7,9,11,13,15},{16,18,20,22,24,26,28,30},{17..., dimensions={0} | all-to-all | bytes 1048576 | tf_op jit(solution)/shard_map/all_to_all | solution.py:417
  79.0 2.9 collective-permute-start.3
  81.9 1.5 collective-permute-done.3.other_ref
  83.4 2.0 coeffs.1
  85.4 3.5 %all-to-all-start.2 = ((f32[8,128,128]{2,1,0:T(8,128)}), f32[8,128,128]{2,1,0:T(8,128)S(1)}, u32[]{:S(2)}, u32[]{:S(2)}) async-start(f32[8,128,128]{2,1,0:T(8,128)} %coeffs.1), calls=%async_computation.2 | async-start | bytes 1048576 | tf_op jit(solution)/shard_map/all_to_all | solution.py:417
  88.9 2.3 collective-permute-start
  91.2 1.0 fusion.1
  92.3 19.8 %all-to-all-done.2.own_ref = f32[8,128,128]{2,1,0:T(8,128)S(1)} async-done(((f32[8,128,128]{2,1,0:T(8,128)}), f32[8,128,128]{2,1,0:T(8,128)S(1)}, u32[]{:S(2)}, u32[]{:S(2)}) %all-to-all-start.2) | async-done | bytes 524320 | tf_op jit(solution)/shard_map/all_to_all | solution.py:417
  112.1 1.1 collective-permute-start.4
  113.4 0.9 fusion
  115.0 0.8 copy-done.13
  115.8 4.7 %lowered.1 = (f32[512,128]{1,0:T(8,128)}, f32[128,128]{1,0:T(8,128)}) custom-call(s32[3]{0:T(128)} %pad_add_fusion.where_ref, f32[8,128,128]{2,1,0:T(8,128)} %copy-done.11, f32[8,128,128]{2,1,0:T(8,128)} %copy-done.13, f32[512,2048]{1,0:T(8,128)} %vectors_ref.3, f32[512,128]{1,0:T(8,128)} %side_ref.3), custom_call_target="tpu_custom_call" | custom-call | flops 805306368 | bytes 4194304 | tf_op jit(solution)/shard_map/lowered/pallas_call | solution.py:147
  120.5 3.3 %collective-permute-start.5 = (f32[128,128]{1,0:T(8,128)}, f32[128,128]{1,0:T(8,128)S(1)}, u32[]{:S(2)}, u32[]{:S(2)}) collective-permute-start(f32[128,128]{1,0:T(8,128)} %get-tuple-element.26.upper_ref), channel_id=1, source_target_pairs={{0,16},{32,48},{64,80},{96,112},{128,144},{160,176},{192,208},{224... | collective-permute-start | bytes 196616 | tf_op jit(solution)/shard_map/ppermute | solution.py:388
  123.9 7.9 %all-gather.7.cloned.1.call-done = f32[24576,128]{1,0:T(8,128)} async-done(((f32[1536,128]{1,0:T(8,128)}), f32[24576,128]{1,0:T(8,128)}) %all-gather.7.cloned.1.call-update) | async-done | bytes 12582928 | tf_op jit(solution)/shard_map/all_gather | solution.py:426
  131.8 8.3 %joint.1 = (bf16[256,2048]{1,0:T(8,128)(2,1)}, bf16[256,2048]{1,0:T(8,128)(2,1)}) custom-call(s32[3]{0:T(128)} %pad_add_fusion.where_ref, f32[128,2048]{1,0:T(8,128)} %bitcast.31, f32[16,1536,128]{2,1,0:T(8,128)} %bitcast.30), custom_call_target="tpu_custom_call" | custom-call | flops 1610612736 | bytes 6291456 | tf_op jit(solution)/shard_map/joint/pallas_call | solution.py:212
  140.1 1.2 copy-done
  141.3 1.2 copy-done.3
  142.6 1.1 level.4
  144.0 1.7 collective-permute-done.6
  145.7 0.9 add.53
  146.6 4.2 %all-to-all-start.3 = ((f32[8,128,128]{2,1,0:T(8,128)}), f32[8,128,128]{2,1,0:T(8,128)S(1)}, u32[]{:S(2)}, u32[]{:S(2)}) async-start(f32[8,128,128]{2,1,0:T(8,128)} %add.53), calls=%async_computation.3 | async-start | bytes 1048576 | tf_op jit(solution)/shard_map/all_to_all | solution.py:410
  150.9 0.7 all-gather.9.cloned.1.call-update
  151.6 17.2 %all-to-all-done.3 = f32[8,128,128]{2,1,0:T(8,128)S(1)} async-done(((f32[8,128,128]{2,1,0:T(8,128)}), f32[8,128,128]{2,1,0:T(8,128)S(1)}, u32[]{:S(2)}, u32[]{:S(2)}) %all-to-all-start.3) | async-done | bytes 524320 | tf_op jit(solution)/shard_map/all_to_all | solution.py:410
  168.8 0.7 collective-permute-start.7
  169.5 0.7 collective-permute-start.8
  170.2 1.2 copy-done.1
  171.4 1.2 copy-done.4
  172.7 1.1 level.5
  174.4 1.5 collective-permute-done.9
  176.0 21.2 %all_to_all.47 = f32[8,128,128]{2,1,0:T(8,128)S(1)} all-to-all(f32[8,128,128]{2,1,0:T(8,128)S(1)} %add.54), channel_id=1, replica_groups={{0,2,4,6,8,10,12,14},{1,3,5,7,9,11,13,15},{16,18,20,22,24,26,28,30},{17..., dimensions={0} | all-to-all | bytes 1048576 | tf_op jit(solution)/shard_map/all_to_all | solution.py:410
  197.3 1.2 copy-done.6
  198.5 0.8 fold.1
  199.4 0.7 collective-permute-start.10
  200.1 0.7 collective-permute-start.11
  200.8 1.1 level.6
  201.9 1.0 collective-permute-start.12
  203.0 1.5 collective-permute-done.12
  204.5 21.3 %all_to_all.48 = f32[8,128,128]{2,1,0:T(8,128)S(1)} all-to-all(f32[8,128,128]{2,1,0:T(8,128)S(1)} %add.55), channel_id=1, replica_groups={{0,2,4,6,8,10,12,14},{1,3,5,7,9,11,13,15},{16,18,20,22,24,26,28,30},{17..., dimensions={0} | all-to-all | bytes 1048576 | tf_op jit(solution)/shard_map/all_to_all | solution.py:410
  225.9 0.7 collective-permute-start.13
  226.6 0.7 collective-permute-start.14
  227.3 1.1 level.7
  228.4 1.1 collective-permute-start.15
  229.5 1.5 collective-permute-done.15
  231.0 0.9 add.56
  231.9 3.5 %all-to-all-start.6 = ((f32[8,128,128]{2,1,0:T(8,128)}), f32[8,128,128]{2,1,0:T(8,128)S(1)}, u32[]{:S(2)}, u32[]{:S(2)}) async-start(f32[8,128,128]{2,1,0:T(8,128)} %add.56), calls=%async_computation.6 | async-start | bytes 1048576 | tf_op jit(solution)/shard_map/all_to_all | solution.py:410
  235.4 17.9 %all-to-all-done.6 = f32[8,128,128]{2,1,0:T(8,128)S(1)} async-done(((f32[8,128,128]{2,1,0:T(8,128)}), f32[8,128,128]{2,1,0:T(8,128)S(1)}, u32[]{:S(2)}, u32[]{:S(2)}) %all-to-all-start.6) | async-done | bytes 524320 | tf_op jit(solution)/shard_map/all_to_all | solution.py:410
  253.4 24.6 %all_to_all.49 = f32[16,8,128]{2,1,0:T(8,128)S(1)} all-to-all(f32[16,8,128]{2,1,0:T(8,128)S(1)} %bitcast.33), channel_id=1, replica_groups=mesh['rows'=16,'leaf'=16] {'rows'}, dimensions={0} | all-to-all | bytes 131072 | tf_op jit(solution)/shard_map/all_to_all | solution.py:479
  278.2 17.4 %all_to_all.50.own_ref = f32[8,136,128]{2,1,0:T(8,128)S(1)} all-to-all(f32[8,136,128]{2,1,0:T(8,128)S(1)} %broadcast_in_dim.41), channel_id=1, replica_groups={{0,2,4,6,8,10,12,14},{1,3,5,7,9,11,13,15},{16,18,20,22,24,26,28,30},{17..., dimensions={0} | all-to-all | bytes 1114112 | tf_op jit(solution)/shard_map/all_to_all | solution.py:417
  295.7 4.1 %collective-permute-start.16 = (f32[8,136,128]{2,1,0:T(8,128)S(1)}, f32[8,136,128]{2,1,0:T(8,128)S(1)}, u32[]{:S(2)}, u32[]{:S(2)}) collective-permute-start(f32[8,136,128]{2,1,0:T(8,128)S(1)} %all_to_all.50.own_ref), channel_id=1, source_target_pairs={{0,1},{1,0},{2,3},{3,2},{4,5},{5,4},{6,7},{7,6},{8,9},{9,8},{10,11... | collective-permute-start | bytes 1671176 | tf_op jit(solution)/shard_map/ppermute | solution.py:388
  299.8 1.3 collective-permute-start.17
  301.7 5.2 %collective-permute-done.17.back_ref = f32[128,128]{1,0:T(8,128)S(1)} collective-permute-done((f32[128,128]{1,0:T(8,128)S(1)}, f32[128,128]{1,0:T(8,128)S(1)}, u32[]{:S(2)}, u32[]{:S(2)}) %collective-permute-start.17) | collective-permute-done | bytes 65568 | tf_op jit(solution)/shard_map/ppermute | solution.py:388
  307.7 10.2 %final.1 = (f32[512,128]{1,0:T(8,128)}, f32[128,8]{1,0:T(8,128)}) custom-call(s32[3]{0:T(128)} %pad_add_fusion.where_ref, f32[8,136,128]{2,1,0:T(8,128)} %copy-done.12, f32[8,136,128]{2,1,0:T(8,128)} %copy-done.15, f32[128,128]{1,0:T(8,128)} %select_select_fusion.summit_ref, f32[128,128]{1,0:T(8,128)} %copy-done.16, f32[128,2048]{1,0:T(8,128)} %bitcast.32, ...), custom_call_target="tpu_custom_call" | custom-call | flops 4294967296 | bytes 8912896 | tf_op jit(solution)/shard_map/final/pallas_call | solution.py:364
  317.9 1.5 copy.14
  (70 shorter events, 4.7 us)
Async XLA Ops:
  7.2 76.2 %copy-start.7 = (f32[1,2048,128]{2,1,0:T(8,128)S(1)}, f32[1,2048,128]{2,1,0:T(8,128)}, u32[]{:S(2)}) copy-start(f32[1,2048,128]{2,1,0:T(8,128)} %param.9) | copy-start | bytes 3145732
  7.2 81.7 %copy-start.14 = (f32[128,128]{1,0:T(8,128)S(1)}, f32[128,128]{1,0:T(8,128)}, u32[]{:S(2)}) copy-start(f32[128,128]{1,0:T(8,128)} %param.13) | copy-start | bytes 196612
  7.2 124.6 %all-gather.7.cloned.1.call-start = ((), (), s32[]{:S(2)}) async-start(), calls=%async_computation.9 | async-start | bytes 13369344 | tf_op jit(solution)/shard_map/all_gather | solution.py:426
  8.3 13.7 %collective-permute-start.1 = (f32[512,128]{1,0:T(8,128)S(1)}, f32[512,128]{1,0:T(8,128)S(1)}, u32[]{:S(2)}, u32[]{:S(2)}) collective-permute-start(f32[512,128]{1,0:T(8,128)S(1)} %slice_bitcast_fusion.1), channel_id=1, source_target_pairs={{12,6},{13,7},{14,0},{15,1},{28,22},{29,23},{30,16},{31,17},{44,38... | collective-permute-start | bytes 786440 | tf_op jit(solution)/shard_map/ppermute | solution.py:388
  10.3 73.2 %copy-start.9 = (s32[3]{0:T(128)S(1)}, s32[3]{0:T(128)}, u32[]{:S(2)}) copy-start(s32[3]{0:T(128)} %pad_add_fusion.where_ref) | copy-start | bytes 40
  24.0 3.1 collective-permute-start.2
  79.0 4.4 %collective-permute-start.3 = (f32[8,128,128]{2,1,0:T(8,128)S(1)}, f32[8,128,128]{2,1,0:T(8,128)S(1)}, u32[]{:S(2)}, u32[]{:S(2)}) collective-permute-start(f32[8,128,128]{2,1,0:T(8,128)S(1)} %all_to_all.46.own_ref), channel_id=1, source_target_pairs={{0,1},{1,0},{2,3},{3,2},{4,5},{5,4},{6,7},{7,6},{8,9},{9,8},{10,11... | collective-permute-start | bytes 1572872 | tf_op jit(solution)/shard_map/ppermute | solution.py:388
  85.4 26.7 %all-to-all-start.2 = ((f32[8,128,128]{2,1,0:T(8,128)}), f32[8,128,128]{2,1,0:T(8,128)S(1)}, u32[]{:S(2)}, u32[]{:S(2)}) async-start(f32[8,128,128]{2,1,0:T(8,128)} %coeffs.1), calls=%async_computation.2 | async-start | bytes 1048576 | tf_op jit(solution)/shard_map/all_to_all | solution.py:417
  88.9 24.3 %collective-permute-start = (f32[128,128]{1,0:T(8,128)S(1)}, f32[128,128]{1,0:T(8,128)S(1)}, u32[]{:S(2)}, u32[]{:S(2)}) collective-permute-start(f32[128,128]{1,0:T(8,128)S(1)} %copy-done.14), channel_id=1, source_target_pairs={{1,0},{3,2},{5,4},{7,6},{9,8},{11,10},{13,12},{15,14},{17,16},{19,... | collective-permute-start | bytes 196616 | tf_op jit(solution)/shard_map/ppermute | solution.py:388
  112.1 2.9 copy-start.11
  112.1 2.9 collective-permute-start.4
  115.0 25.1 %copy-start.10 = (s32[3]{0:T(128)S(1)}, s32[3]{0:T(128)}, u32[]{:S(2)}) copy-start(s32[3]{0:T(128)} %pad_add_fusion.where_ref) | copy-start | bytes 40
  115.0 0.8 copy-start.13
  120.5 19.6 %copy-start.8 = (f32[128,128]{1,0:T(8,128)S(1)}, f32[128,128]{1,0:T(8,128)}, u32[]{:S(2)}) copy-start(f32[128,128]{1,0:T(8,128)} %get-tuple-element.26.upper_ref) | copy-start | bytes 196612
  120.5 19.6 %collective-permute-start.5 = (f32[128,128]{1,0:T(8,128)}, f32[128,128]{1,0:T(8,128)S(1)}, u32[]{:S(2)}, u32[]{:S(2)}) collective-permute-start(f32[128,128]{1,0:T(8,128)} %get-tuple-element.26.upper_ref), channel_id=1, source_target_pairs={{0,16},{32,48},{64,80},{96,112},{128,144},{160,176},{192,208},{224... | collective-permute-start | bytes 196616 | tf_op jit(solution)/shard_map/ppermute | solution.py:388
  140.1 1.2 copy-start
  141.3 1.2 copy-start.3
  142.6 58.2 %copy-start.2 = (bf16[256,2048]{1,0:T(8,128)(2,1)S(1)}, bf16[256,2048]{1,0:T(8,128)(2,1)}, u32[]{:S(2)}) copy-start(bf16[256,2048]{1,0:T(8,128)(2,1)} %get-tuple-element.28.high_ref) | copy-start | bytes 3145732
  142.6 58.2 %copy-start.5 = (bf16[256,2048]{1,0:T(8,128)(2,1)S(1)}, bf16[256,2048]{1,0:T(8,128)(2,1)}, u32[]{:S(2)}) copy-start(bf16[256,2048]{1,0:T(8,128)(2,1)} %get-tuple-element.29.low_ref) | copy-start | bytes 3145732
  143.7 2.0 collective-permute-start.6
  146.6 22.2 %all-to-all-start.3 = ((f32[8,128,128]{2,1,0:T(8,128)}), f32[8,128,128]{2,1,0:T(8,128)S(1)}, u32[]{:S(2)}, u32[]{:S(2)}) async-start(f32[8,128,128]{2,1,0:T(8,128)} %add.53), calls=%async_computation.3 | async-start | bytes 1048576 | tf_op jit(solution)/shard_map/all_to_all | solution.py:410
  150.8 46.5 %all-gather.9.cloned.1.call-start = ((), (), s32[]{:S(2)}) async-start(), calls=%async_computation.10 | async-start | bytes 1183744 | tf_op jit(solution)/shard_map/all_gather | solution.py:452
  151.6 155.3 %all-gather.11.cloned.1.call-start = ((), (), s32[]{:S(2)}) async-start(), calls=%async_computation.11 | async-start | bytes 9469952 | tf_op jit(solution)/shard_map/all_gather | solution.py:469
  168.8 1.3 collective-permute-start.7
  169.5 0.7 collective-permute-start.8
  170.2 1.2 copy-start.1
  171.4 1.2 copy-start.4
  173.8 2.1 collective-permute-start.9
  197.3 1.2 copy-start.6
  199.4 1.3 collective-permute-start.10
  200.1 0.7 collective-permute-start.11
  201.9 2.6 collective-permute-start.12
  225.9 1.3 collective-permute-start.13
  226.6 0.7 collective-permute-start.14
  228.4 2.6 collective-permute-start.15
  231.9 21.4 %all-to-all-start.6 = ((f32[8,128,128]{2,1,0:T(8,128)}), f32[8,128,128]{2,1,0:T(8,128)S(1)}, u32[]{:S(2)}, u32[]{:S(2)}) async-start(f32[8,128,128]{2,1,0:T(8,128)} %add.56), calls=%async_computation.6 | async-start | bytes 1048576 | tf_op jit(solution)/shard_map/all_to_all | solution.py:410
  295.7 11.2 %copy-start.12 = (f32[8,136,128]{2,1,0:T(8,128)}, f32[8,136,128]{2,1,0:T(8,128)S(1)}, u32[]{:S(2)}) copy-start(f32[8,136,128]{2,1,0:T(8,128)S(1)} %all_to_all.50.own_ref) | copy-start | bytes 1671172
  295.7 11.2 %collective-permute-start.16 = (f32[8,136,128]{2,1,0:T(8,128)S(1)}, f32[8,136,128]{2,1,0:T(8,128)S(1)}, u32[]{:S(2)}, u32[]{:S(2)}) collective-permute-start(f32[8,136,128]{2,1,0:T(8,128)S(1)} %all_to_all.50.own_ref), channel_id=1, source_target_pairs={{0,1},{1,0},{2,3},{3,2},{4,5},{5,4},{6,7},{7,6},{8,9},{9,8},{10,11... | collective-permute-start | bytes 1671176 | tf_op jit(solution)/shard_map/ppermute | solution.py:388
  299.8 7.1 %collective-permute-start.17 = (f32[128,128]{1,0:T(8,128)S(1)}, f32[128,128]{1,0:T(8,128)S(1)}, u32[]{:S(2)}, u32[]{:S(2)}) collective-permute-start(f32[128,128]{1,0:T(8,128)S(1)} %get-tuple-element.47), channel_id=1, source_target_pairs={{128,0},{129,1},{130,2},{131,3},{132,4},{133,5},{134,6},{135,7},{1... | collective-permute-start | bytes 196616 | tf_op jit(solution)/shard_map/ppermute | solution.py:388
  306.9 0.6 copy-start.16
  306.9 0.8 copy-start.15
Sparse Core Ops, SparseCore 0:
  24.1 107.6 all-gather.6
  154.1 42.3 all-gather.8
  199.5 81.0 all-gather.10

commit v3 on v2

--- a/solution.py
+++ b/solution.py
@@ -11,6 +11,7 @@
 GROUP = 4
 SPLIT = (((1,), (0,)), ((), ()))
 SMALL = 24 * 1024 * 1024
+MEDIUM = 52 * 1024 * 1024
 LARGE = 56 * 1024 * 1024
 
 
@@ -165,45 +166,40 @@
 def joint_kernel(where_ref, reflect_ref, factor_ref, high_ref, low_ref, panel_ref, sems):
     count, kept, _ = factor_ref.shape
     order = reflect_ref.shape[1]
-    steps = count // 2
     spare = order - kept
-    copies = [None] * count
-    for n in range(steps):
-        for k in (n, n + steps):
-            edge = (k + 1) * SIDE
-            rows = pl.ds(0, min(edge, kept))
-            copies[k] = [
-                pltpu.make_async_copy(factor_ref.at[k, rows], panel_ref.at[k, rows], sems.at[0, k])
-            ]
-            if edge > kept:
-                copies[k].append(
-                    pltpu.make_async_copy(
-                        factor_ref.at[slot_of(k, count), pl.ds(kept - spare, edge - kept)],
-                        panel_ref.at[k, pl.ds(kept, edge - kept)],
-                        sems.at[1, k],
-                    )
+    copies = []
+    for k in range(count):
+        edge = (k // 2 + 1) * 2 * SIDE
+        rows = pl.ds(0, min(edge, kept))
+        copies.append(
+            [pltpu.make_async_copy(factor_ref.at[k, rows], panel_ref.at[k, rows], sems.at[0, k])]
+        )
+        if edge > kept:
+            copies[k].append(
+                pltpu.make_async_copy(
+                    factor_ref.at[slot_of(k, count), pl.ds(kept - spare, edge - kept)],
+                    panel_ref.at[k, pl.ds(kept, edge - kept)],
+                    sems.at[1, k],
                 )
-            for copy in copies[k]:
-                copy.start()
+            )
+        for copy in copies[k]:
+            copy.start()
     reflect = halves(reflect_ref[...])
     own = where_ref[1]
     zero = jnp.zeros((SIDE, SIDE), jnp.float32)
-    for n in range(steps):
-        far = n + steps
-        for copy in copies[n] + copies[far]:
+    for k in range(0, count, 2):
+        for copy in copies[k] + copies[k + 1]:
             copy.wait()
-        edge, stop = (n + 1) * SIDE, (far + 1) * SIDE
-        near_part, far_part = halves(panel_ref[n, 0:edge]), halves(panel_ref[far, 0:stop])
-        shared = [jnp.concatenate([s, t[:edge]], axis=1) for s, t in zip(near_part, far_part)]
-        both = stacked([r[:, :edge] for r in reflect], shared)
-        rest = stacked([r[:, edge:stop] for r in reflect], [t[edge:] for t in far_part])
-        for k, top in ((n, both[:, :SIDE]), (far, both[:, SIDE:] + rest)):
-            mine = pl.ds(pl.multiple_of(jnp.minimum(own, k) * SIDE, SIDE), SIDE)
-            bottom = jnp.where(own <= k, panel_ref[k, mine, :], zero)
-            at = pl.ds(k * SIDE, SIDE)
-            for ref, part in zip((high_ref, low_ref), zip(halves(top), halves(bottom))):
-                ref[0:SIDE, at] = part[0]
-                ref[SIDE:2 * SIDE, at] = part[1]
+        edge = (k + 2) * SIDE
+        panel = jnp.concatenate([panel_ref[k, 0:edge], panel_ref[k + 1, 0:edge]], axis=1)
+        top = stacked([r[:, :edge] for r in reflect], halves(panel))
+        mine = pl.ds(pl.multiple_of(jnp.minimum(own, k + 1) * SIDE, SIDE), SIDE)
+        bottom = [jnp.where(own <= j, panel_ref[j, mine, :], zero) for j in (k, k + 1)]
+        bottom = jnp.concatenate(bottom, axis=1)
+        at = pl.ds(k * SIDE, 2 * SIDE)
+        for ref, first, second in zip((high_ref, low_ref), halves(top), halves(bottom)):
+            ref[0:SIDE, at] = first
+            ref[SIDE:2 * SIDE, at] = second
 
 
 def joint_of(where, reflect, factor):
@@ -218,7 +214,7 @@
             pltpu.VMEM((count, order, SIDE), jnp.float32),
             pltpu.SemaphoreType.DMA((2, count)),
         ],
-        compiler_params=params(LARGE),
+        compiler_params=params(MEDIUM),
         cost_estimate=cost(3 * block * order * order, 2 * factor.size),
         name="joint",
     )(where, reflect, factor)
@@ -350,7 +346,7 @@
                 ]
                 ready = ready - thrice(band_of(q - 1, b + 1, count), known)
     mine = pl.ds(pl.multiple_of(where_ref[1] * SIDE, SIDE), SIDE)
-    solved_ref[...] = whole_ref[mine, :]
+    solved_ref[...] = whole_ref[mine, :].T
     rest_copy.wait()
     top_copy.wait()
 
@@ -365,7 +361,7 @@
         final_kernel,
         in_specs=[smem] + [vmem] * 5 + [hbm] * 2,
         out_specs=[hbm, vmem],
-        out_shape=[shaped(*rotated.shape), shaped(SIDE, narrow)],
+        out_shape=[shaped(*rotated.shape), shaped(narrow, SIDE)],
         scratch_shapes=[
             pltpu.VMEM((order, columns), jnp.float32),
             pltpu.VMEM((order, narrow), jnp.float32),
@@ -477,8 +473,12 @@
     back = moved(lower, "rows", [(root, 0)])
     pieces = lower.reshape(rows, columns // rows, block)
     arrived = lax.all_to_all(pieces, "rows", 0, 0)[root]
+    arrived, back = lax.optimization_barrier((arrived, back))
     own, other = collect(copies(jnp.concatenate([own_coeffs.T, arrived], axis=0)))
-    return final_of(where, own, other, own_top, back, node_reflect[0], rotated, folded)
+    rotated, solved = final_of(
+        where, own, other, own_top, back, node_reflect[0], rotated, folded
+    )
+    return (rotated, solved.T)
 
 
 def solution(mesh):

time: 327 us -> 319 us (0.976)
  waiting for transfers between devices: 85.2 us -> 81.1 us
  local copies, waits for them, and re-layouts: 11.7 us -> 7.73 us
    ppermute x18, waiting for transfers between devices: 21.6 us -> 17.5 us  [moved(): return lax.ppermute(value, axis, pairs)]
    unnamed x35 -> x29, local copies, waits for them, and re-layouts: 7.87 us -> 5.43 us
where the time goes in v3:
time: 319 us; the launch traced here: 318 us
  blocking collectives  136 us (43%)
  waiting for transfers between devices  81.1 us (25%)
  starting transfers between devices  35.6 us (11%)
  Pallas kernels  34.3 us (11%)
  between operations  14.2 us (4%)
  other arithmetic  7.96 us (2%)
  local copies, waits for them, and re-layouts  7.73 us (2%)
    all_to_all x3, blocking collectives, scatter_pair(): got = lax.all_to_all(pair, 'leaf', 0, 0, axis_index_groups=same)  69.4 us
    all_to_all x2, blocking collectives, collect(): own = lax.all_to_all(spread, 'leaf', 0, 0, axis_index_groups=same)  42.3 us
    all_to_all x2, waiting for transfers between devices, scatter_pair(): got = lax.all_to_all(pair, 'leaf', 0, 0, axis_index_groups=same)  35.1 us
    ppermute x18, starting transfers between devices, moved(): return lax.ppermute(value, axis, pairs)  24.3 us
    all_to_all x1, blocking collectives, per_device(): arrived = lax.all_to_all(pieces, 'rows', 0, 0)[root]  24.3 us
    all_to_all x1, waiting for transfers between devices, collect(): own = lax.all_to_all(spread, 'leaf', 0, 0, axis_index_groups=same)  19.8 us
    ppermute x18, waiting for transfers between devices, moved(): return lax.ppermute(value, axis, pairs)  17.5 us
    pallas_call x1, Pallas kernels, final_of(): pl.pallas_call(final_kernel, in_specs=[smem] + [vmem] * 5 + [hbm] * 2, ou...  10.2 us
  transfers between devices with their start and end apart: 24, of which 12 were waited for; matrix products, arithmetic and copies ran while one was open for 2% of the time, Pallas kernels for 7%

profile of v3, /device:TPU:1, one launch (start us, length us, event | category | flops | bytes accessed | tf_op | source)
XLA Modules:
  0.0 318.0 jit_solution(8955193296433515229)
XLA Ops:
  7.2 1.1 slice_bitcast_fusion.1
  8.3 1.3 collective-permute-start.1
  10.2 3.8 %weights.1 = (f32[8,128,128]{2,1,0:T(8,128)}, f32[8,128,128]{2,1,0:T(8,128)}) custom-call(s32[3]{0:T(128)} %pad_add_fusion.where_ref, f32[512,128]{1,0:T(8,128)} %side_ref.3, f32[512,2048]{1,0:T(8,128)} %vectors_ref.3), custom_call_target="tpu_custom_call" | custom-call | flops 805306368 | bytes 4194304 | tf_op jit(solution)/shard_map/weights/pallas_call | solution.py:82
  13.9 1.1 slice_bitcast_fusion
  15.0 7.0 %collective-permute-done.1 = f32[512,128]{1,0:T(8,128)S(1)} collective-permute-done((f32[512,128]{1,0:T(8,128)S(1)}, f32[512,128]{1,0:T(8,128)S(1)}, u32[]{:S(2)}, u32[]{:S(2)}) %collective-permute-start.1) | collective-permute-done | bytes 262176 | tf_op jit(solution)/shard_map/ppermute | solution.py:384
  22.0 1.0 bitcast_add_fusion
  23.0 1.0 pad_maximum_fusion
  24.0 1.3 collective-permute-start.2
  25.3 1.7 collective-permute-done.2
  27.0 1.1 add.51
  28.1 26.0 %all_to_all.45 = f32[8,128,128]{2,1,0:T(8,128)S(1)} all-to-all(f32[8,128,128]{2,1,0:T(8,128)S(1)} %add.51), channel_id=1, replica_groups={{0,2,4,6,8,10,12,14},{1,3,5,7,9,11,13,15},{16,18,20,22,24,26,28,30},{17..., dimensions={0} | all-to-all | bytes 1048576 | tf_op jit(solution)/shard_map/all_to_all | solution.py:406
  54.2 24.8 %all_to_all.46.own_ref = f32[8,128,128]{2,1,0:T(8,128)S(1)} all-to-all(f32[8,128,128]{2,1,0:T(8,128)S(1)} %broadcast_in_dim.39), channel_id=1, replica_groups={{0,2,4,6,8,10,12,14},{1,3,5,7,9,11,13,15},{16,18,20,22,24,26,28,30},{17..., dimensions={0} | all-to-all | bytes 1048576 | tf_op jit(solution)/shard_map/all_to_all | solution.py:413
  79.0 2.9 collective-permute-start.3
  81.9 1.5 collective-permute-done.3.other_ref
  83.4 2.0 coeffs.1
  85.4 3.5 %all-to-all-start.2 = ((f32[8,128,128]{2,1,0:T(8,128)}), f32[8,128,128]{2,1,0:T(8,128)S(1)}, u32[]{:S(2)}, u32[]{:S(2)}) async-start(f32[8,128,128]{2,1,0:T(8,128)} %coeffs.1), calls=%async_computation.2 | async-start | bytes 1048576 | tf_op jit(solution)/shard_map/all_to_all | solution.py:413
  88.9 2.3 collective-permute-start
  91.3 1.0 fusion.1
  92.3 19.8 %all-to-all-done.2.own_ref = f32[8,128,128]{2,1,0:T(8,128)S(1)} async-done(((f32[8,128,128]{2,1,0:T(8,128)}), f32[8,128,128]{2,1,0:T(8,128)S(1)}, u32[]{:S(2)}, u32[]{:S(2)}) %all-to-all-start.2) | async-done | bytes 524320 | tf_op jit(solution)/shard_map/all_to_all | solution.py:413
  112.1 1.1 collective-permute-start.4
  113.4 0.9 fusion
  114.3 0.6 pad_maximum_fusion.2
  115.0 0.8 copy-done.10
  115.8 4.7 %lowered.1 = (f32[512,128]{1,0:T(8,128)}, f32[128,128]{1,0:T(8,128)}) custom-call(s32[3]{0:T(128)} %pad_add_fusion.where_ref, f32[8,128,128]{2,1,0:T(8,128)} %copy-done.8, f32[8,128,128]{2,1,0:T(8,128)} %copy-done.10, f32[512,2048]{1,0:T(8,128)} %vectors_ref.3, f32[512,128]{1,0:T(8,128)} %side_ref.3), custom_call_target="tpu_custom_call" | custom-call | flops 805306368 | bytes 4194304 | tf_op jit(solution)/shard_map/lowered/pallas_call | solution.py:148
  120.5 3.3 %collective-permute-start.5 = (f32[128,128]{1,0:T(8,128)}, f32[128,128]{1,0:T(8,128)S(1)}, u32[]{:S(2)}, u32[]{:S(2)}) collective-permute-start(f32[128,128]{1,0:T(8,128)} %get-tuple-element.30.upper_ref), channel_id=1, source_target_pairs={{0,16},{32,48},{64,80},{96,112},{128,144},{160,176},{192,208},{224... | collective-permute-start | bytes 196616 | tf_op jit(solution)/shard_map/ppermute | solution.py:384
  123.9 7.9 %all-gather.7.cloned.1.call-done = f32[24576,128]{1,0:T(8,128)} async-done(((f32[1536,128]{1,0:T(8,128)}), f32[24576,128]{1,0:T(8,128)}) %all-gather.7.cloned.1.call-update) | async-done | bytes 12582928 | tf_op jit(solution)/shard_map/all_gather | solution.py:422
  131.8 8.3 %joint.1 = (bf16[256,2048]{1,0:T(8,128)(2,1)S(1)}, bf16[256,2048]{1,0:T(8,128)(2,1)}) custom-call(s32[3]{0:T(128)S(1)} %copy-done.7, f32[128,2048]{1,0:T(8,128)} %bitcast.32, f32[16,1536,128]{2,1,0:T(8,128)} %bitcast.31), custom_call_target="tpu_custom_call" | custom-call | flops 1610612736 | bytes 6291456 | tf_op jit(solution)/shard_map/joint/pallas_call | solution.py:208
  140.1 1.2 copy-done
  141.3 1.1 level.4
  142.8 1.7 collective-permute-done.6
  144.5 0.9 add.53
  145.3 4.3 %all-to-all-start.3 = ((f32[8,128,128]{2,1,0:T(8,128)}), f32[8,128,128]{2,1,0:T(8,128)S(1)}, u32[]{:S(2)}, u32[]{:S(2)}) async-start(f32[8,128,128]{2,1,0:T(8,128)} %add.53), calls=%async_computation.3 | async-start | bytes 1048576 | tf_op jit(solution)/shard_map/all_to_all | solution.py:406
  149.6 0.7 all-gather.9.cloned.1.call-update
  150.4 17.2 %all-to-all-done.3 = f32[8,128,128]{2,1,0:T(8,128)S(1)} async-done(((f32[8,128,128]{2,1,0:T(8,128)}), f32[8,128,128]{2,1,0:T(8,128)S(1)}, u32[]{:S(2)}, u32[]{:S(2)}) %all-to-all-start.3) | async-done | bytes 524320 | tf_op jit(solution)/shard_map/all_to_all | solution.py:406
  167.6 0.7 collective-permute-start.7
  168.3 0.7 collective-permute-start.8
  169.0 1.2 copy-done.1
  170.2 1.1 level.5
  171.9 1.5 collective-permute-done.9
  173.5 21.4 %all_to_all.47 = f32[8,128,128]{2,1,0:T(8,128)S(1)} all-to-all(f32[8,128,128]{2,1,0:T(8,128)S(1)} %add.54), channel_id=1, replica_groups={{0,2,4,6,8,10,12,14},{1,3,5,7,9,11,13,15},{16,18,20,22,24,26,28,30},{17..., dimensions={0} | all-to-all | bytes 1048576 | tf_op jit(solution)/shard_map/all_to_all | solution.py:406
  194.9 1.2 copy-done.3
  196.2 0.9 fold.1
  197.1 0.7 collective-permute-start.10
  197.7 0.7 collective-permute-start.11
  198.5 1.1 level.6
  199.6 0.7 collective-permute-start.12
  200.3 1.5 collective-permute-done.12
  201.9 22.0 %all_to_all.48 = f32[8,128,128]{2,1,0:T(8,128)S(1)} all-to-all(f32[8,128,128]{2,1,0:T(8,128)S(1)} %add.55), channel_id=1, replica_groups={{0,2,4,6,8,10,12,14},{1,3,5,7,9,11,13,15},{16,18,20,22,24,26,28,30},{17..., dimensions={0} | all-to-all | bytes 1048576 | tf_op jit(solution)/shard_map/all_to_all | solution.py:406
  224.0 0.7 collective-permute-start.13
  224.6 0.7 collective-permute-start.14
  225.3 1.1 level.7
  226.4 1.1 collective-permute-start.15
  227.6 1.5 collective-permute-done.15
  229.1 0.9 add.56
  230.0 3.5 %all-to-all-start.6 = ((f32[8,128,128]{2,1,0:T(8,128)}), f32[8,128,128]{2,1,0:T(8,128)S(1)}, u32[]{:S(2)}, u32[]{:S(2)}) async-start(f32[8,128,128]{2,1,0:T(8,128)} %add.56), calls=%async_computation.6 | async-start | bytes 1048576 | tf_op jit(solution)/shard_map/all_to_all | solution.py:406
  233.5 17.9 %all-to-all-done.6 = f32[8,128,128]{2,1,0:T(8,128)S(1)} async-done(((f32[8,128,128]{2,1,0:T(8,128)}), f32[8,128,128]{2,1,0:T(8,128)S(1)}, u32[]{:S(2)}, u32[]{:S(2)}) %all-to-all-start.6) | async-done | bytes 524320 | tf_op jit(solution)/shard_map/all_to_all | solution.py:406
  251.5 1.3 collective-permute-start.16
  252.8 24.3 %all_to_all.49 = f32[16,8,128]{2,1,0:T(8,128)S(1)} all-to-all(f32[16,8,128]{2,1,0:T(8,128)S(1)} %bitcast.34), channel_id=1, replica_groups=mesh['rows'=16,'leaf'=16] {'rows'}, dimensions={0} | all-to-all | bytes 131072 | tf_op jit(solution)/shard_map/all_to_all | solution.py:475
  277.3 17.5 %all_to_all.50.own_ref = f32[8,136,128]{2,1,0:T(8,128)S(1)} all-to-all(f32[8,136,128]{2,1,0:T(8,128)S(1)} %broadcast_in_dim.41), channel_id=1, replica_groups={{0,2,4,6,8,10,12,14},{1,3,5,7,9,11,13,15},{16,18,20,22,24,26,28,30},{17..., dimensions={0} | all-to-all | bytes 1114112 | tf_op jit(solution)/shard_map/all_to_all | solution.py:413
  294.8 4.1 %collective-permute-start.17 = (f32[8,136,128]{2,1,0:T(8,128)S(1)}, f32[8,136,128]{2,1,0:T(8,128)S(1)}, u32[]{:S(2)}, u32[]{:S(2)}) collective-permute-start(f32[8,136,128]{2,1,0:T(8,128)S(1)} %all_to_all.50.own_ref), channel_id=1, source_target_pairs={{0,1},{1,0},{2,3},{3,2},{4,5},{5,4},{6,7},{7,6},{8,9},{9,8},{10,11... | collective-permute-start | bytes 1671176 | tf_op jit(solution)/shard_map/ppermute | solution.py:384
  298.9 0.6 select_select_fusion.summit_ref
  299.5 1.0 collective-permute-done.17.other_ref
  300.5 0.8 copy-done.12
  301.3 10.2 %final.1 = (f32[512,128]{1,0:T(8,128)}, f32[8,128]{1,0:T(8,128)}) custom-call(s32[3]{0:T(128)} %pad_add_fusion.where_ref, f32[8,136,128]{2,1,0:T(8,128)} %copy-done.9, f32[8,136,128]{2,1,0:T(8,128)} %copy-done.12, f32[128,128]{1,0:T(8,128)} %select_select_fusion.summit_ref, f32[128,128]{1,0:T(8,128)} %copy-done.13, f32[128,2048]{1,0:T(8,128)} %bitcast.33, ...), custom_call_target="tpu_custom_call" | custom-call | flops 4294967296 | bytes 8912896 | tf_op jit(solution)/shard_map/final/pallas_call | solution.py:360
  (63 shorter events, 2.6 us)
Async XLA Ops:
  7.2 76.3 %copy-start.4 = (f32[1,2048,128]{2,1,0:T(8,128)S(1)}, f32[1,2048,128]{2,1,0:T(8,128)}, u32[]{:S(2)}) copy-start(f32[1,2048,128]{2,1,0:T(8,128)} %param.9) | copy-start | bytes 3145732
  7.2 81.7 %copy-start.11 = (f32[128,128]{1,0:T(8,128)S(1)}, f32[128,128]{1,0:T(8,128)}, u32[]{:S(2)}) copy-start(f32[128,128]{1,0:T(8,128)} %param.13) | copy-start | bytes 196612
  7.2 124.6 %all-gather.7.cloned.1.call-start = ((), (), s32[]{:S(2)}) async-start(), calls=%async_computation.9 | async-start | bytes 13369344 | tf_op jit(solution)/shard_map/all_gather | solution.py:422
  8.3 13.7 %collective-permute-start.1 = (f32[512,128]{1,0:T(8,128)S(1)}, f32[512,128]{1,0:T(8,128)S(1)}, u32[]{:S(2)}, u32[]{:S(2)}) collective-permute-start(f32[512,128]{1,0:T(8,128)S(1)} %slice_bitcast_fusion.1), channel_id=1, source_target_pairs={{12,6},{13,7},{14,0},{15,1},{28,22},{29,23},{30,16},{31,17},{44,38... | collective-permute-start | bytes 786440 | tf_op jit(solution)/shard_map/ppermute | solution.py:384
  10.2 73.2 %copy-start.6 = (s32[3]{0:T(128)S(1)}, s32[3]{0:T(128)}, u32[]{:S(2)}) copy-start(s32[3]{0:T(128)} %pad_add_fusion.where_ref) | copy-start | bytes 40
  15.0 116.8 %copy-start.7 = (s32[3]{0:T(128)S(1)}, s32[3]{0:T(128)}, u32[]{:S(2)}) copy-start(s32[3]{0:T(128)} %pad_add_fusion.where_ref) | copy-start | bytes 40
  24.0 3.1 collective-permute-start.2
  79.0 4.4 %collective-permute-start.3 = (f32[8,128,128]{2,1,0:T(8,128)S(1)}, f32[8,128,128]{2,1,0:T(8,128)S(1)}, u32[]{:S(2)}, u32[]{:S(2)}) collective-permute-start(f32[8,128,128]{2,1,0:T(8,128)S(1)} %all_to_all.46.own_ref), channel_id=1, source_target_pairs={{0,1},{1,0},{2,3},{3,2},{4,5},{5,4},{6,7},{7,6},{8,9},{9,8},{10,11... | collective-permute-start | bytes 1572872 | tf_op jit(solution)/shard_map/ppermute | solution.py:384
  85.4 26.7 %all-to-all-start.2 = ((f32[8,128,128]{2,1,0:T(8,128)}), f32[8,128,128]{2,1,0:T(8,128)S(1)}, u32[]{:S(2)}, u32[]{:S(2)}) async-start(f32[8,128,128]{2,1,0:T(8,128)} %coeffs.1), calls=%async_computation.2 | async-start | bytes 1048576 | tf_op jit(solution)/shard_map/all_to_all | solution.py:413
  88.9 24.3 %collective-permute-start = (f32[128,128]{1,0:T(8,128)S(1)}, f32[128,128]{1,0:T(8,128)S(1)}, u32[]{:S(2)}, u32[]{:S(2)}) collective-permute-start(f32[128,128]{1,0:T(8,128)S(1)} %copy-done.11), channel_id=1, source_target_pairs={{1,0},{3,2},{5,4},{7,6},{9,8},{11,10},{13,12},{15,14},{17,16},{19,... | collective-permute-start | bytes 196616 | tf_op jit(solution)/shard_map/ppermute | solution.py:384
  112.1 2.9 copy-start.8
  112.1 2.8 collective-permute-start.4
  115.0 0.8 copy-start.10
  120.5 19.6 %copy-start.5 = (f32[128,128]{1,0:T(8,128)S(1)}, f32[128,128]{1,0:T(8,128)}, u32[]{:S(2)}) copy-start(f32[128,128]{1,0:T(8,128)} %get-tuple-element.30.upper_ref) | copy-start | bytes 196612
  120.5 19.6 %collective-permute-start.5 = (f32[128,128]{1,0:T(8,128)}, f32[128,128]{1,0:T(8,128)S(1)}, u32[]{:S(2)}, u32[]{:S(2)}) collective-permute-start(f32[128,128]{1,0:T(8,128)} %get-tuple-element.30.upper_ref), channel_id=1, source_target_pairs={{0,16},{32,48},{64,80},{96,112},{128,144},{160,176},{192,208},{224... | collective-permute-start | bytes 196616 | tf_op jit(solution)/shard_map/ppermute | solution.py:384
  140.1 1.2 copy-start
  141.3 57.1 %copy-start.2 = (bf16[256,2048]{1,0:T(8,128)(2,1)S(1)}, bf16[256,2048]{1,0:T(8,128)(2,1)}, u32[]{:S(2)}) copy-start(bf16[256,2048]{1,0:T(8,128)(2,1)} %get-tuple-element.33.low_ref) | copy-start | bytes 3145732
  142.5 2.0 collective-permute-start.6
  145.3 22.2 %all-to-all-start.3 = ((f32[8,128,128]{2,1,0:T(8,128)}), f32[8,128,128]{2,1,0:T(8,128)S(1)}, u32[]{:S(2)}, u32[]{:S(2)}) async-start(f32[8,128,128]{2,1,0:T(8,128)} %add.53), calls=%async_computation.3 | async-start | bytes 1048576 | tf_op jit(solution)/shard_map/all_to_all | solution.py:406
  149.6 45.3 %all-gather.9.cloned.1.call-start = ((), (), s32[]{:S(2)}) async-start(), calls=%async_computation.10 | async-start | bytes 1183744 | tf_op jit(solution)/shard_map/all_gather | solution.py:448
  150.3 150.1 %all-gather.11.cloned.1.call-start = ((), (), s32[]{:S(2)}) async-start(), calls=%async_computation.11 | async-start | bytes 9469952 | tf_op jit(solution)/shard_map/all_gather | solution.py:465
  167.6 1.3 collective-permute-start.7
  168.3 0.7 collective-permute-start.8
  169.0 1.2 copy-start.1
  171.3 2.1 collective-permute-start.9
  194.9 1.2 copy-start.3
  197.1 1.3 collective-permute-start.10
  197.7 0.7 collective-permute-start.11
  199.6 2.2 collective-permute-start.12
  224.0 1.3 collective-permute-start.13
  224.6 0.7 collective-permute-start.14
  226.4 2.6 collective-permute-start.15
  230.0 21.4 %all-to-all-start.6 = ((f32[8,128,128]{2,1,0:T(8,128)}), f32[8,128,128]{2,1,0:T(8,128)S(1)}, u32[]{:S(2)}, u32[]{:S(2)}) async-start(f32[8,128,128]{2,1,0:T(8,128)} %add.56), calls=%async_computation.6 | async-start | bytes 1048576 | tf_op jit(solution)/shard_map/all_to_all | solution.py:406
  251.5 25.7 %collective-permute-start.16 = (f32[128,128]{1,0:T(8,128)S(1)}, f32[128,128]{1,0:T(8,128)S(1)}, u32[]{:S(2)}, u32[]{:S(2)}) collective-permute-start(f32[128,128]{1,0:T(8,128)S(1)} %get-tuple-element.51), channel_id=1, source_target_pairs={{128,0},{129,1},{130,2},{131,3},{132,4},{133,5},{134,6},{135,7},{1... | collective-permute-start | bytes 196616 | tf_op jit(solution)/shard_map/ppermute | solution.py:384
  277.2 23.3 %copy-start.13 = (f32[128,128]{1,0:T(8,128)}, f32[128,128]{1,0:T(8,128)S(1)}, u32[]{:S(2)}) copy-start(f32[128,128]{1,0:T(8,128)S(1)} %collective-permute-done.16.back_ref) | copy-start | bytes 196612
  294.8 5.6 %copy-start.9 = (f32[8,136,128]{2,1,0:T(8,128)}, f32[8,136,128]{2,1,0:T(8,128)S(1)}, u32[]{:S(2)}) copy-start(f32[8,136,128]{2,1,0:T(8,128)S(1)} %all_to_all.50.own_ref) | copy-start | bytes 1671172
  294.8 5.6 %collective-permute-start.17 = (f32[8,136,128]{2,1,0:T(8,128)S(1)}, f32[8,136,128]{2,1,0:T(8,128)S(1)}, u32[]{:S(2)}, u32[]{:S(2)}) collective-permute-start(f32[8,136,128]{2,1,0:T(8,128)S(1)} %all_to_all.50.own_ref), channel_id=1, source_target_pairs={{0,1},{1,0},{2,3},{3,2},{4,5},{5,4},{6,7},{7,6},{8,9},{9,8},{10,11... | collective-permute-start | bytes 1671176 | tf_op jit(solution)/shard_map/ppermute | solution.py:384
  300.4 0.8 copy-start.12
Sparse Core Ops, SparseCore 0:
  24.1 107.6 all-gather.6
  152.8 41.8 all-gather.8
  197.2 82.4 all-gather.10

commit v4 on v3

--- a/solution.py
+++ b/solution.py
@@ -11,7 +11,7 @@
 GROUP = 4
 SPLIT = (((1,), (0,)), ((), ()))
 SMALL = 24 * 1024 * 1024
-MEDIUM = 52 * 1024 * 1024
+MEDIUM = 51 * 1024 * 1024
 LARGE = 56 * 1024 * 1024
 
 
@@ -23,6 +23,12 @@
 
 def once(left, right):
     return lax.dot_general(left, right, SPLIT, preferred_element_type=jnp.float32)
+
+
+def crossed(left, right):
+    return lax.dot_general(
+        left, right, (((1,), (1,)), ((), ())), preferred_element_type=jnp.float32
+    )
 
 
 def thrice(left, right):
@@ -159,25 +165,24 @@
     )(where, own, other, vectors, side)
 
 
-def slot_of(k, count):
-    return (k + 10) % count if k < count - 2 else k + 2 - count
+KEPT = 10
+ENDS = {10: (6, 8), 11: (7, 8), 12: (4, 6), 13: (5, 6), 14: (0, 4), 15: (1, 4)}
 
 
 def joint_kernel(where_ref, reflect_ref, factor_ref, high_ref, low_ref, panel_ref, sems):
     count, kept, _ = factor_ref.shape
-    order = reflect_ref.shape[1]
-    spare = order - kept
-    copies = []
-    for k in range(count):
+    copies = [None] * count
+    for k in reversed(range(count)):
         edge = (k // 2 + 1) * 2 * SIDE
         rows = pl.ds(0, min(edge, kept))
-        copies.append(
-            [pltpu.make_async_copy(factor_ref.at[k, rows], panel_ref.at[k, rows], sems.at[0, k])]
-        )
+        copies[k] = [
+            pltpu.make_async_copy(factor_ref.at[k, rows], panel_ref.at[k, rows], sems.at[0, k])
+        ]
         if edge > kept:
+            slot, first = ENDS[k]
             copies[k].append(
                 pltpu.make_async_copy(
-                    factor_ref.at[slot_of(k, count), pl.ds(kept - spare, edge - kept)],
+                    factor_ref.at[slot, pl.ds(first * SIDE, edge - kept)],
                     panel_ref.at[k, pl.ds(kept, edge - kept)],
                     sems.at[1, k],
                 )
@@ -187,7 +192,7 @@
     reflect = halves(reflect_ref[...])
     own = where_ref[1]
     zero = jnp.zeros((SIDE, SIDE), jnp.float32)
-    for k in range(0, count, 2):
+    for k in reversed(range(0, count, 2)):
         for copy in copies[k] + copies[k + 1]:
             copy.wait()
         edge = (k + 2) * SIDE
@@ -290,7 +295,7 @@
         for k, value in enumerate(pick(parity, own_ref[n], other_ref[n])):
             at = pl.ds((2 * n + k) * SIDE, SIDE)
             coeffs_ref[at, :] = value[:SIDE]
-            whole_ref[at, :] = value[SIDE:].T
+            whole_ref[:, at] = value[SIDE:]
     lowered = thrice(halves(reflect_ref[...]), halves(coeffs_ref[...]))
     lowered = jnp.where(where_ref[2] == 0, back_ref[...], summit_ref[...] - lowered.T)
     top_ref[...] = lowered.T
@@ -314,9 +319,18 @@
         ]
         return halves(jnp.concatenate(bands, axis=0))
 
+    def parts_of(value):
+        high = value.astype(jnp.bfloat16).astype(jnp.float32)
+        return jnp.concatenate([high, value - high], axis=0).astype(jnp.bfloat16)
+
+    def across(parts, right):
+        both = crossed(parts, right[0]) + crossed(parts, right[1])
+        size = both.shape[0] // 2
+        return both[:size] + both[size:]
+
     last = count // 2 - 1
-    solved = [None] * (last + 1)
-    ready = whole_ref[pl.ds(2 * last * SIDE, 2 * SIDE), :]
+    known = None
+    ready = whole_ref[:, pl.ds(2 * last * SIDE, 2 * SIDE)]
     for q in reversed(range(last + 1)):
         a, b = 2 * q, 2 * q + 1
         if q == last:
@@ -331,22 +345,19 @@
         )
         value = ready
         if q < last:
-            value = value - thrice(band_of(q, b + 1, b + 3), solved[q + 1])
-        value = thrice(halves(inverse), halves(value))
-        whole_ref[pl.ds(a * SIDE, 2 * SIDE), :] = value
-        solved[q] = halves(value)
+            value = value - across(newest, band_of(q, b + 1, b + 3))
+        value = across(parts_of(value), halves(inverse))
+        whole_ref[:, pl.ds(a * SIDE, 2 * SIDE)] = value
+        newest = parts_of(value)
+        known = newest if known is None else jnp.concatenate([newest, known], axis=1)
         if q > 0:
-            ready = whole_ref[pl.ds((a - 2) * SIDE, 2 * SIDE), :]
+            ready = whole_ref[:, pl.ds((a - 2) * SIDE, 2 * SIDE)]
             if q < last:
                 if q - 1 > last // 2:
                     copies[last - q + 1].wait()
-                known = [
-                    jnp.concatenate([pair[part] for pair in solved[q + 1:]], axis=0)
-                    for part in range(2)
-                ]
-                ready = ready - thrice(band_of(q - 1, b + 1, count), known)
+                ready = ready - across(known[:, 2 * SIDE:], band_of(q - 1, b + 1, count))
     mine = pl.ds(pl.multiple_of(where_ref[1] * SIDE, SIDE), SIDE)
-    solved_ref[...] = whole_ref[mine, :].T
+    solved_ref[...] = whole_ref[:, mine]
     rest_copy.wait()
     top_copy.wait()
 
@@ -364,7 +375,7 @@
         out_shape=[shaped(*rotated.shape), shaped(narrow, SIDE)],
         scratch_shapes=[
             pltpu.VMEM((order, columns), jnp.float32),
-            pltpu.VMEM((order, narrow), jnp.float32),
+            pltpu.VMEM((narrow, order), jnp.float32),
             pltpu.VMEM((SIDE, columns), jnp.float32),
             pltpu.VMEM((near // 2, rows, 2, long) + folded.shape[3:], jnp.float32),
             pltpu.SemaphoreType.DMA((near // 2,)),
@@ -413,18 +424,26 @@
         own = lax.all_to_all(spread, "leaf", 0, 0, axis_index_groups=same)
         return own, moved(own, "leaf", swap)
 
-    kept = count * 3 // 4 * block
-    spare = count * block - kept
-    sources = range(count * 3 // 4, count)
-    given = moved(node_factor[0, kept:], "leaf", [(k, slot_of(k, count)) for k in sources])
+    start = KEPT * block
+    longest = moved(
+        node_factor[0, start:], "leaf", [(k, ENDS[k][0]) for k in (14, 15)]
+    )
+    longer = moved(
+        node_factor[0, start:start + 4 * block], "leaf", [(k, ENDS[k][0]) for k in (10, 11, 12, 13)]
+    )
     keep, give = weights_of(where, right_side, reflectors)
-    keep, given = lax.optimization_barrier((keep, given))
+    keep, longest, longer = lax.optimization_barrier((keep, longest, longer))
+
+    def lowered_by(value, first):
+        return jnp.pad(value, ((first * block, start - first * block - value.shape[0]), (0, 0)))
+
+    longer = jnp.where(
+        leaf_index < ENDS[10][0],
+        lowered_by(longer, ENDS[12][1]),
+        lowered_by(longer[:2 * block], ENDS[10][1]),
+    )
     factor_whole = lax.all_gather(
-        jnp.concatenate(
-            [node_factor[0, :kept - spare], node_factor[0, kept - spare:kept] + given], axis=0
-        ),
-        "leaf",
-        axis=0,
+        node_factor[0, :start] + (lowered_by(longest, ENDS[14][1]) + longer), "leaf", axis=0
     )
     weights_part = scatter_pair(pair_sum((keep, give)))
     spread = coeffs_of(where, *collect(copies(weights_part)), leaf_factor[0])

time: 319 us -> 314 us (0.984)
    all_gather x1, waiting for transfers between devices: 7.94 us -> 0.02 us  [per_device(): lax.all_gather(node_factor[0, :start] + (lowered_by(longest, ENDS[14][1])...]
    ppermute x18 -> x19, waiting for transfers between devices: 17.5 us -> 25.3 us  [moved(): return lax.ppermute(value, axis, pairs)]
    ppermute x18 -> x19, starting transfers between devices: 24.3 us -> 23.8 us  [moved(): return lax.ppermute(value, axis, pairs)]
  transfers between devices with their start and end apart: 24 -> 25, of which waited for: 12 -> 12; matrix products, arithmetic and copies ran while one was open for 2% -> 2% of each run, Pallas kernels for 7% -> 7%
where the time goes in v4:
time: 314 us; the launch traced here: 313 us
  blocking collectives  134 us (43%)
  waiting for transfers between devices  82.8 us (26%)
  starting transfers between devices  34.4 us (11%)
  Pallas kernels  33.3 us (11%)
  between operations  14.2 us (5%)
  other arithmetic  8.11 us (3%)
  local copies, waits for them, and re-layouts  5.23 us (2%)
    all_to_all x3, blocking collectives, scatter_pair(): got = lax.all_to_all(pair, 'leaf', 0, 0, axis_index_groups=same)  67.8 us
    all_to_all x2, blocking collectives, collect(): own = lax.all_to_all(spread, 'leaf', 0, 0, axis_index_groups=same)  42.9 us
    all_to_all x2, waiting for transfers between devices, scatter_pair(): got = lax.all_to_all(pair, 'leaf', 0, 0, axis_index_groups=same)  35 us
    ppermute x19, waiting for transfers between devices, moved(): return lax.ppermute(value, axis, pairs)  25.3 us
    ppermute x19, starting transfers between devices, moved(): return lax.ppermute(value, axis, pairs)  23.8 us
    all_to_all x1, blocking collectives, per_device(): arrived = lax.all_to_all(pieces, 'rows', 0, 0)[root]  23.1 us
    all_to_all x1, waiting for transfers between devices, collect(): own = lax.all_to_all(spread, 'leaf', 0, 0, axis_index_groups=same)  19.9 us
    pallas_call x1, Pallas kernels, final_of(): pl.pallas_call(final_kernel, in_specs=[smem] + [vmem] * 5 + [hbm] * 2, ou...  9.49 us
  transfers between devices with their start and end apart: 25, of which 12 were waited for; matrix products, arithmetic and copies ran while one was open for 2% of the time, Pallas kernels for 7%

profile of v4, /device:TPU:1, one launch (start us, length us, event | category | flops | bytes accessed | tf_op | source)
XLA Modules:
  0.0 313.0 jit_solution(11084514976117770792)
XLA Ops:
  7.2 1.1 slice_bitcast_fusion
  8.3 1.3 collective-permute-start.1
  9.6 1.0 slice_bitcast_fusion.1
  10.6 0.7 collective-permute-start.2
  11.3 0.7 pad_add_fusion.where_ref
  12.0 3.7 %weights.1 = (f32[8,128,128]{2,1,0:T(8,128)}, f32[8,128,128]{2,1,0:T(8,128)}) custom-call(s32[3]{0:T(128)} %pad_add_fusion.where_ref, f32[512,128]{1,0:T(8,128)} %side_ref.3, f32[512,2048]{1,0:T(8,128)} %vectors_ref.3), custom_call_target="tpu_custom_call" | custom-call | flops 805306368 | bytes 4194304 | tf_op jit(solution)/shard_map/weights/pallas_call | solution.py:88
  15.7 14.7 %collective-permute-done.1 = f32[768,128]{1,0:T(8,128)S(1)} collective-permute-done((f32[768,128]{1,0:T(8,128)S(1)}, f32[768,128]{1,0:T(8,128)S(1)}, u32[]{:S(2)}, u32[]{:S(2)}) %collective-permute-start.1) | collective-permute-done | bytes 393248 | tf_op jit(solution)/shard_map/ppermute | solution.py:395
  30.5 2.0 bitcast_add_fusion
  32.5 1.3 collective-permute-start.3
  33.8 1.7 collective-permute-done.3
  35.6 1.1 add.60
  36.7 25.3 %all_to_all.45 = f32[8,128,128]{2,1,0:T(8,128)S(1)} all-to-all(f32[8,128,128]{2,1,0:T(8,128)S(1)} %add.60), channel_id=1, replica_groups={{0,2,4,6,8,10,12,14},{1,3,5,7,9,11,13,15},{16,18,20,22,24,26,28,30},{17..., dimensions={0} | all-to-all | bytes 1048576 | tf_op jit(solution)/shard_map/all_to_all | solution.py:417
  62.1 25.5 %all_to_all.46.own_ref = f32[8,128,128]{2,1,0:T(8,128)S(1)} all-to-all(f32[8,128,128]{2,1,0:T(8,128)S(1)} %broadcast_in_dim.39), channel_id=1, replica_groups={{0,2,4,6,8,10,12,14},{1,3,5,7,9,11,13,15},{16,18,20,22,24,26,28,30},{17..., dimensions={0} | all-to-all | bytes 1048576 | tf_op jit(solution)/shard_map/all_to_all | solution.py:424
  87.5 1.5 collective-permute-start.4
  89.1 1.5 collective-permute-done.4.other_ref
  90.6 2.0 coeffs.1
  92.6 3.5 %all-to-all-start.2 = ((f32[8,128,128]{2,1,0:T(8,128)}), f32[8,128,128]{2,1,0:T(8,128)S(1)}, u32[]{:S(2)}, u32[]{:S(2)}) async-start(f32[8,128,128]{2,1,0:T(8,128)} %coeffs.1), calls=%async_computation.2 | async-start | bytes 1048576 | tf_op jit(solution)/shard_map/all_to_all | solution.py:424
  96.1 2.3 collective-permute-start
  98.5 1.0 fusion.1
  99.5 19.9 %all-to-all-done.2.own_ref = f32[8,128,128]{2,1,0:T(8,128)S(1)} async-done(((f32[8,128,128]{2,1,0:T(8,128)}), f32[8,128,128]{2,1,0:T(8,128)S(1)}, u32[]{:S(2)}, u32[]{:S(2)}) %all-to-all-start.2) | async-done | bytes 524320 | tf_op jit(solution)/shard_map/all_to_all | solution.py:424
  119.3 1.1 collective-permute-start.5
  120.6 0.9 fusion
  121.5 0.6 pad_maximum_fusion.1
  122.2 0.8 copy-done.7
  123.0 4.7 %lowered.1 = (f32[512,128]{1,0:T(8,128)}, f32[128,128]{1,0:T(8,128)}) custom-call(s32[3]{0:T(128)} %pad_add_fusion.where_ref, f32[8,128,128]{2,1,0:T(8,128)} %copy-done.5, f32[8,128,128]{2,1,0:T(8,128)} %copy-done.7, f32[512,2048]{1,0:T(8,128)} %vectors_ref.3, f32[512,128]{1,0:T(8,128)} %side_ref.3), custom_call_target="tpu_custom_call" | custom-call | flops 805306368 | bytes 4194304 | tf_op jit(solution)/shard_map/lowered/pallas_call | solution.py:154
  127.7 3.5 %collective-permute-start.6 = (f32[128,128]{1,0:T(8,128)}, f32[128,128]{1,0:T(8,128)S(1)}, u32[]{:S(2)}, u32[]{:S(2)}) collective-permute-start(f32[128,128]{1,0:T(8,128)} %get-tuple-element.31.upper_ref), channel_id=1, source_target_pairs={{0,16},{32,48},{64,80},{96,112},{128,144},{160,176},{192,208},{224... | collective-permute-start | bytes 196616 | tf_op jit(solution)/shard_map/ppermute | solution.py:395
  131.2 8.0 %joint.1 = (bf16[256,2048]{1,0:T(8,128)(2,1)S(1)}, bf16[256,2048]{1,0:T(8,128)(2,1)S(1)}) custom-call(s32[3]{0:T(128)S(1)} %copy-done.4, f32[128,2048]{1,0:T(8,128)} %bitcast.32, f32[16,1280,128]{2,1,0:T(8,128)} %bitcast.31), custom_call_target="tpu_custom_call" | custom-call | flops 1610612736 | bytes 5242880 | tf_op jit(solution)/shard_map/joint/pallas_call | solution.py:213
  139.2 1.1 level.4
  140.3 0.6 collective-permute-start.7
  140.9 1.5 collective-permute-done.7
  142.5 0.9 add.63
  143.3 3.5 %all-to-all-start.3 = ((f32[8,128,128]{2,1,0:T(8,128)}), f32[8,128,128]{2,1,0:T(8,128)S(1)}, u32[]{:S(2)}, u32[]{:S(2)}) async-start(f32[8,128,128]{2,1,0:T(8,128)} %add.63), calls=%async_computation.3 | async-start | bytes 1048576 | tf_op jit(solution)/shard_map/all_to_all | solution.py:417
  146.9 0.7 all-gather.9.cloned.1.call-update
  147.6 17.1 %all-to-all-done.3 = f32[8,128,128]{2,1,0:T(8,128)S(1)} async-done(((f32[8,128,128]{2,1,0:T(8,128)}), f32[8,128,128]{2,1,0:T(8,128)S(1)}, u32[]{:S(2)}, u32[]{:S(2)}) %all-to-all-start.3) | async-done | bytes 524320 | tf_op jit(solution)/shard_map/all_to_all | solution.py:417
  164.8 0.7 collective-permute-start.8
  165.5 0.7 collective-permute-start.9
  166.2 1.1 level.5
  167.3 0.6 collective-permute-start.10
  167.9 1.5 collective-permute-done.10
  169.5 21.8 %all_to_all.47 = f32[8,128,128]{2,1,0:T(8,128)S(1)} all-to-all(f32[8,128,128]{2,1,0:T(8,128)S(1)} %add.64), channel_id=1, replica_groups={{0,2,4,6,8,10,12,14},{1,3,5,7,9,11,13,15},{16,18,20,22,24,26,28,30},{17..., dimensions={0} | all-to-all | bytes 1048576 | tf_op jit(solution)/shard_map/all_to_all | solution.py:417
  191.3 1.9 all-gather.9.cloned.1.call-done
  193.2 1.2 copy-done
  194.4 0.9 fold.1
  195.3 0.7 collective-permute-start.11
  196.0 0.8 collective-permute-start.12
  196.9 1.1 level.6
  198.3 1.7 collective-permute-done.13
  200.1 20.7 %all_to_all.48 = f32[8,128,128]{2,1,0:T(8,128)S(1)} all-to-all(f32[8,128,128]{2,1,0:T(8,128)S(1)} %add.65), channel_id=1, replica_groups={{0,2,4,6,8,10,12,14},{1,3,5,7,9,11,13,15},{16,18,20,22,24,26,28,30},{17..., dimensions={0} | all-to-all | bytes 1048576 | tf_op jit(solution)/shard_map/all_to_all | solution.py:417
  220.8 0.7 collective-permute-start.14
  221.5 0.7 collective-permute-start.15
  222.2 1.1 level.7
  223.3 1.1 collective-permute-start.16
  224.5 1.5 collective-permute-done.16
  226.0 0.9 add.66
  226.9 3.5 %all-to-all-start.6 = ((f32[8,128,128]{2,1,0:T(8,128)}), f32[8,128,128]{2,1,0:T(8,128)S(1)}, u32[]{:S(2)}, u32[]{:S(2)}) async-start(f32[8,128,128]{2,1,0:T(8,128)} %add.66), calls=%async_computation.6 | async-start | bytes 1048576 | tf_op jit(solution)/shard_map/all_to_all | solution.py:417
  230.4 17.9 %all-to-all-done.6 = f32[8,128,128]{2,1,0:T(8,128)S(1)} async-done(((f32[8,128,128]{2,1,0:T(8,128)}), f32[8,128,128]{2,1,0:T(8,128)S(1)}, u32[]{:S(2)}, u32[]{:S(2)}) %all-to-all-start.6) | async-done | bytes 524320 | tf_op jit(solution)/shard_map/all_to_all | solution.py:417
  248.4 1.3 collective-permute-start.17
  249.7 23.1 %all_to_all.49 = f32[16,8,128]{2,1,0:T(8,128)S(1)} all-to-all(f32[16,8,128]{2,1,0:T(8,128)S(1)} %bitcast.34), channel_id=1, replica_groups=mesh['rows'=16,'leaf'=16] {'rows'}, dimensions={0} | all-to-all | bytes 131072 | tf_op jit(solution)/shard_map/all_to_all | solution.py:494
  273.1 17.5 %all_to_all.50.own_ref = f32[8,136,128]{2,1,0:T(8,128)S(1)} all-to-all(f32[8,136,128]{2,1,0:T(8,128)S(1)} %broadcast_in_dim.41), channel_id=1, replica_groups={{0,2,4,6,8,10,12,14},{1,3,5,7,9,11,13,15},{16,18,20,22,24,26,28,30},{17..., dimensions={0} | all-to-all | bytes 1114112 | tf_op jit(solution)/shard_map/all_to_all | solution.py:424
  290.6 4.1 %collective-permute-start.18 = (f32[8,136,128]{2,1,0:T(8,128)S(1)}, f32[8,136,128]{2,1,0:T(8,128)S(1)}, u32[]{:S(2)}, u32[]{:S(2)}) collective-permute-start(f32[8,136,128]{2,1,0:T(8,128)S(1)} %all_to_all.50.own_ref), channel_id=1, source_target_pairs={{0,1},{1,0},{2,3},{3,2},{4,5},{5,4},{6,7},{7,6},{8,9},{9,8},{10,11... | collective-permute-start | bytes 1671176 | tf_op jit(solution)/shard_map/ppermute | solution.py:395
  294.6 0.6 select_select_fusion.summit_ref
  295.2 1.0 collective-permute-done.18.other_ref
  296.2 0.8 copy-done.9
  297.0 9.5 %final.1 = (f32[512,128]{1,0:T(8,128)}, f32[8,128]{1,0:T(8,128)}) custom-call(s32[3]{0:T(128)} %pad_add_fusion.where_ref, f32[8,136,128]{2,1,0:T(8,128)} %copy-done.6, f32[8,136,128]{2,1,0:T(8,128)} %copy-done.9, f32[128,128]{1,0:T(8,128)} %select_select_fusion.summit_ref, f32[128,128]{1,0:T(8,128)} %copy-done.10, f32[128,2048]{1,0:T(8,128)} %bitcast.33, ...), custom_call_target="tpu_custom_call" | custom-call | flops 4294967296 | bytes 8912896 | tf_op jit(solution)/shard_map/final/pallas_call | solution.py:371
  (59 shorter events, 1.4 us)
Async XLA Ops:
  7.2 83.5 %copy-start.1 = (f32[1,2048,128]{2,1,0:T(8,128)S(1)}, f32[1,2048,128]{2,1,0:T(8,128)}, u32[]{:S(2)}) copy-start(f32[1,2048,128]{2,1,0:T(8,128)} %param.9) | copy-start | bytes 3145732
  7.2 88.9 %copy-start.8 = (f32[128,128]{1,0:T(8,128)S(1)}, f32[128,128]{1,0:T(8,128)}, u32[]{:S(2)}) copy-start(f32[128,128]{1,0:T(8,128)} %param.13) | copy-start | bytes 196612
  7.2 124.0 %all-gather.7.cloned.1.call-start = ((), (), s32[]{:S(2)}) async-start(), calls=%async_computation.9 | async-start | bytes 11141120 | tf_op jit(solution)/shard_map/all_gather | solution.py:445
  8.3 22.1 %collective-permute-start.1 = (f32[768,128]{1,0:T(8,128)S(1)}, f32[768,128]{1,0:T(8,128)S(1)}, u32[]{:S(2)}, u32[]{:S(2)}) collective-permute-start(f32[768,128]{1,0:T(8,128)S(1)} %slice_bitcast_fusion), channel_id=1, source_target_pairs={{14,0},{15,1},{30,16},{31,17},{46,32},{47,33},{62,48},{63,49},{78,... | collective-permute-start | bytes 1179656 | tf_op jit(solution)/shard_map/ppermute | solution.py:395
  10.6 5.1 %collective-permute-start.2 = (f32[512,128]{1,0:T(8,128)S(1)}, f32[512,128]{1,0:T(8,128)S(1)}, u32[]{:S(2)}, u32[]{:S(2)}) collective-permute-start(f32[512,128]{1,0:T(8,128)S(1)} %slice_bitcast_fusion.1), channel_id=1, source_target_pairs={{10,6},{11,7},{12,4},{13,5},{26,22},{27,23},{28,20},{29,21},{42,38... | collective-permute-start | bytes 786440 | tf_op jit(solution)/shard_map/ppermute | solution.py:395
  12.0 78.6 %copy-start.3 = (s32[3]{0:T(128)S(1)}, s32[3]{0:T(128)}, u32[]{:S(2)}) copy-start(s32[3]{0:T(128)} %pad_add_fusion.where_ref) | copy-start | bytes 40
  15.7 115.5 %copy-start.4 = (s32[3]{0:T(128)S(1)}, s32[3]{0:T(128)}, u32[]{:S(2)}) copy-start(s32[3]{0:T(128)} %pad_add_fusion.where_ref) | copy-start | bytes 40
  32.5 3.1 collective-permute-start.3
  87.5 3.1 collective-permute-start.4
  92.6 26.7 %all-to-all-start.2 = ((f32[8,128,128]{2,1,0:T(8,128)}), f32[8,128,128]{2,1,0:T(8,128)S(1)}, u32[]{:S(2)}, u32[]{:S(2)}) async-start(f32[8,128,128]{2,1,0:T(8,128)} %coeffs.1), calls=%async_computation.2 | async-start | bytes 1048576 | tf_op jit(solution)/shard_map/all_to_all | solution.py:424
  96.1 24.3 %collective-permute-start = (f32[128,128]{1,0:T(8,128)S(1)}, f32[128,128]{1,0:T(8,128)S(1)}, u32[]{:S(2)}, u32[]{:S(2)}) collective-permute-start(f32[128,128]{1,0:T(8,128)S(1)} %copy-done.8), channel_id=1, source_target_pairs={{1,0},{3,2},{5,4},{7,6},{9,8},{11,10},{13,12},{15,14},{17,16},{19,... | collective-permute-start | bytes 196616 | tf_op jit(solution)/shard_map/ppermute | solution.py:395
  119.3 2.8 copy-start.5
  119.3 2.8 collective-permute-start.5
  122.2 0.8 copy-start.7
  127.7 11.5 %copy-start.2 = (f32[128,128]{1,0:T(8,128)S(1)}, f32[128,128]{1,0:T(8,128)}, u32[]{:S(2)}) copy-start(f32[128,128]{1,0:T(8,128)} %get-tuple-element.31.upper_ref) | copy-start | bytes 196612
  127.7 11.5 %collective-permute-start.6 = (f32[128,128]{1,0:T(8,128)}, f32[128,128]{1,0:T(8,128)S(1)}, u32[]{:S(2)}, u32[]{:S(2)}) collective-permute-start(f32[128,128]{1,0:T(8,128)} %get-tuple-element.31.upper_ref), channel_id=1, source_target_pairs={{0,16},{32,48},{64,80},{96,112},{128,144},{160,176},{192,208},{224... | collective-permute-start | bytes 196616 | tf_op jit(solution)/shard_map/ppermute | solution.py:395
  140.3 2.1 collective-permute-start.7
  143.3 21.4 %all-to-all-start.3 = ((f32[8,128,128]{2,1,0:T(8,128)}), f32[8,128,128]{2,1,0:T(8,128)S(1)}, u32[]{:S(2)}, u32[]{:S(2)}) async-start(f32[8,128,128]{2,1,0:T(8,128)} %add.63), calls=%async_computation.3 | async-start | bytes 1048576 | tf_op jit(solution)/shard_map/all_to_all | solution.py:417
  146.8 46.3 %all-gather.9.cloned.1.call-start = ((), (), s32[]{:S(2)}) async-start(), calls=%async_computation.10 | async-start | bytes 1183744 | tf_op jit(solution)/shard_map/all_gather | solution.py:467
  147.6 148.6 %all-gather.11.cloned.1.call-start = ((), (), s32[]{:S(2)}) async-start(), calls=%async_computation.11 | async-start | bytes 9469952 | tf_op jit(solution)/shard_map/all_gather | solution.py:484
  164.8 1.3 collective-permute-start.8
  165.5 0.7 collective-permute-start.9
  167.3 2.1 collective-permute-start.10
  193.2 1.2 copy-start
  195.3 1.5 collective-permute-start.11
  196.0 0.9 collective-permute-start.12
  198.0 2.0 collective-permute-start.13
  220.8 1.3 collective-permute-start.14
  221.5 0.7 collective-permute-start.15
  223.3 2.7 collective-permute-start.16
  226.9 21.4 %all-to-all-start.6 = ((f32[8,128,128]{2,1,0:T(8,128)}), f32[8,128,128]{2,1,0:T(8,128)S(1)}, u32[]{:S(2)}, u32[]{:S(2)}) async-start(f32[8,128,128]{2,1,0:T(8,128)} %add.66), calls=%async_computation.6 | async-start | bytes 1048576 | tf_op jit(solution)/shard_map/all_to_all | solution.py:417
  248.4 24.6 %collective-permute-start.17 = (f32[128,128]{1,0:T(8,128)S(1)}, f32[128,128]{1,0:T(8,128)S(1)}, u32[]{:S(2)}, u32[]{:S(2)}) collective-permute-start(f32[128,128]{1,0:T(8,128)S(1)} %get-tuple-element.53), channel_id=1, source_target_pairs={{128,0},{129,1},{130,2},{131,3},{132,4},{133,5},{134,6},{135,7},{1... | collective-permute-start | bytes 196616 | tf_op jit(solution)/shard_map/ppermute | solution.py:395
  272.9 23.3 %copy-start.10 = (f32[128,128]{1,0:T(8,128)}, f32[128,128]{1,0:T(8,128)S(1)}, u32[]{:S(2)}) copy-start(f32[128,128]{1,0:T(8,128)S(1)} %collective-permute-done.17.back_ref) | copy-start | bytes 196612
  290.6 5.7 %copy-start.6 = (f32[8,136,128]{2,1,0:T(8,128)}, f32[8,136,128]{2,1,0:T(8,128)S(1)}, u32[]{:S(2)}) copy-start(f32[8,136,128]{2,1,0:T(8,128)S(1)} %all_to_all.50.own_ref) | copy-start | bytes 1671172
  290.6 5.6 %collective-permute-start.18 = (f32[8,136,128]{2,1,0:T(8,128)S(1)}, f32[8,136,128]{2,1,0:T(8,128)S(1)}, u32[]{:S(2)}, u32[]{:S(2)}) collective-permute-start(f32[8,136,128]{2,1,0:T(8,128)S(1)} %all_to_all.50.own_ref), channel_id=1, source_target_pairs={{0,1},{1,0},{2,3},{3,2},{4,5},{5,4},{6,7},{7,6},{8,9},{9,8},{10,11... | collective-permute-start | bytes 1671176 | tf_op jit(solution)/shard_map/ppermute | solution.py:395
  296.2 0.8 copy-start.9
Sparse Core Ops, SparseCore 0:
  32.6 95.2 all-gather.6
  150.1 43.0 all-gather.8
  195.7 79.8 all-gather.10

commit v5 on v4

--- a/solution.py
+++ b/solution.py
@@ -251,7 +251,7 @@
     )(where, upper, lower, *joint)
 
 
-def fold_kernel(pieces_ref, out_ref):
+def fold_kernel(pieces_ref, after_ref, out_ref):
     count = pieces_ref.shape[0]
     for n in range(count // 2):
         far = count - 1 - n
@@ -262,16 +262,16 @@
         out_ref[n, count] = pieces_ref[far, count]
 
 
-def fold_of(pieces):
+def fold_of(pieces, after):
     count = pieces.shape[0]
     return pl.pallas_call(
         fold_kernel,
-        in_specs=[vmem],
+        in_specs=[vmem, vmem],
         out_specs=vmem,
         out_shape=shaped(count // 2, *pieces.shape[1:]),
         compiler_params=params(),
         name="fold",
-    )(pieces)
+    )(pieces, after)
 
 
 def final_kernel(
@@ -463,8 +463,6 @@
     at_cross = jnp.logical_and(at_cross, leaf_index % 2 == 0)
     upper_slice = jnp.where(at_cross, cross[None], upper_slice)
     upper_slice = jnp.concatenate([upper_slice, inverse_slice[None]], axis=0)
-    upper_slice, top = lax.optimization_barrier((upper_slice, top))
-    pieces = lax.all_gather(upper_slice, "leaf", axis=0)
 
     joint = joint_of(where, node_reflect[0], factor_whole)
 
@@ -478,10 +476,16 @@
             nodes = list(range(stride, rows, 2 * stride))
             upper = moved(lower, "rows", [(j + stride // 2, j) for j in nodes])
             lower = moved(lower, "rows", [(j - stride // 2, j) for j in nodes])
-        share = scatter_pair(pair_sum(level_of(where, upper, lower, joint)))
+        if stride == 4:
+            upper, lower, folded = lax.optimization_barrier((upper, lower, folded))
+            folded = lax.all_gather(folded, "rows", axis=0)
+        parts = level_of(where, upper, lower, joint)
+        if stride == 1:
+            upper_slice, parts = lax.optimization_barrier((upper_slice, parts))
+            pieces = lax.all_gather(upper_slice, "leaf", axis=0)
+        share = scatter_pair(pair_sum(parts))
         if stride == 2:
-            share, pieces = lax.optimization_barrier((share, pieces))
-            folded = lax.all_gather(fold_of(pieces), "rows", axis=0)
+            folded = fold_of(pieces, share)
         lower = lower - share
         mine = row_index % (2 * stride) == stride
         own_coeffs = jnp.where(mine, share, own_coeffs)

time: 314 us -> 312 us (level)
  no operation moved by 1% of the time
where the time goes in v5:
time: 312 us; the launch traced here: 310 us
  blocking collectives  133 us (43%)
  waiting for transfers between devices  81.2 us (26%)
  starting transfers between devices  34.4 us (11%)
  Pallas kernels  33.3 us (11%)
  between operations  14.2 us (5%)
  other arithmetic  8.11 us (3%)
  local copies, waits for them, and re-layouts  5.23 us (2%)
    all_to_all x3, blocking collectives, scatter_pair(): got = lax.all_to_all(pair, 'leaf', 0, 0, axis_index_groups=same)  67.8 us
    all_to_all x2, blocking collectives, collect(): own = lax.all_to_all(spread, 'leaf', 0, 0, axis_index_groups=same)  42.9 us
    all_to_all x2, waiting for transfers between devices, scatter_pair(): got = lax.all_to_all(pair, 'leaf', 0, 0, axis_index_groups=same)  35 us
    ppermute x19, waiting for transfers between devices, moved(): return lax.ppermute(value, axis, pairs)  25.3 us
    ppermute x19, starting transfers between devices, moved(): return lax.ppermute(value, axis, pairs)  23.8 us
    all_to_all x1, blocking collectives, per_device(): arrived = lax.all_to_all(pieces, 'rows', 0, 0)[root]  22.1 us
    all_to_all x1, waiting for transfers between devices, collect(): own = lax.all_to_all(spread, 'leaf', 0, 0, axis_index_groups=same)  19.9 us
    pallas_call x1, Pallas kernels, final_of(): pl.pallas_call(final_kernel, in_specs=[smem] + [vmem] * 5 + [hbm] * 2, ou...  9.49 us
  transfers between devices with their start and end apart: 25, of which 12 were waited for; matrix products, arithmetic and copies ran while one was open for 2% of the time, Pallas kernels for 7%

profile of v5, /device:TPU:1, one launch (start us, length us, event | category | flops | bytes accessed | tf_op | source)
XLA Modules:
  0.0 310.5 jit_solution(9132720750736331457)
XLA Ops:
  7.2 1.1 slice_bitcast_fusion
  8.3 1.3 collective-permute-start
  9.6 1.0 slice_bitcast_fusion.1
  10.6 0.7 collective-permute-start.1
  11.3 0.7 pad_add_fusion.where_ref
  12.0 3.7 %weights.1 = (f32[8,128,128]{2,1,0:T(8,128)}, f32[8,128,128]{2,1,0:T(8,128)}) custom-call(s32[3]{0:T(128)} %pad_add_fusion.where_ref, f32[512,128]{1,0:T(8,128)} %side_ref.3, f32[512,2048]{1,0:T(8,128)} %vectors_ref.3), custom_call_target="tpu_custom_call" | custom-call | flops 805306368 | bytes 4194304 | tf_op jit(solution)/shard_map/weights/pallas_call | solution.py:88
  15.7 14.7 %collective-permute-done = f32[768,128]{1,0:T(8,128)S(1)} collective-permute-done((f32[768,128]{1,0:T(8,128)S(1)}, f32[768,128]{1,0:T(8,128)S(1)}, u32[]{:S(2)}, u32[]{:S(2)}) %collective-permute-start) | collective-permute-done | bytes 393248 | tf_op jit(solution)/shard_map/ppermute | solution.py:395
  30.5 2.0 bitcast_add_fusion
  32.5 1.3 collective-permute-start.2
  33.8 1.7 collective-permute-done.2
  35.6 1.1 add.57
  36.7 25.3 %all_to_all.45 = f32[8,128,128]{2,1,0:T(8,128)S(1)} all-to-all(f32[8,128,128]{2,1,0:T(8,128)S(1)} %add.57), channel_id=1, replica_groups={{0,2,4,6,8,10,12,14},{1,3,5,7,9,11,13,15},{16,18,20,22,24,26,28,30},{17..., dimensions={0} | all-to-all | bytes 1048576 | tf_op jit(solution)/shard_map/all_to_all | solution.py:417
  62.1 25.5 %all_to_all.46.own_ref = f32[8,128,128]{2,1,0:T(8,128)S(1)} all-to-all(f32[8,128,128]{2,1,0:T(8,128)S(1)} %broadcast_in_dim.36), channel_id=1, replica_groups={{0,2,4,6,8,10,12,14},{1,3,5,7,9,11,13,15},{16,18,20,22,24,26,28,30},{17..., dimensions={0} | all-to-all | bytes 1048576 | tf_op jit(solution)/shard_map/all_to_all | solution.py:424
  87.5 1.5 collective-permute-start.3
  89.1 1.5 collective-permute-done.3.other_ref
  90.6 2.0 coeffs.1
  92.6 3.5 %all-to-all-start.2 = ((f32[8,128,128]{2,1,0:T(8,128)}), f32[8,128,128]{2,1,0:T(8,128)S(1)}, u32[]{:S(2)}, u32[]{:S(2)}) async-start(f32[8,128,128]{2,1,0:T(8,128)} %coeffs.1), calls=%async_computation.2 | async-start | bytes 1048576 | tf_op jit(solution)/shard_map/all_to_all | solution.py:424
  96.1 2.3 collective-permute-start.6
  98.5 1.0 fusion.1
  99.5 19.9 %all-to-all-done.2.own_ref = f32[8,128,128]{2,1,0:T(8,128)S(1)} async-done(((f32[8,128,128]{2,1,0:T(8,128)}), f32[8,128,128]{2,1,0:T(8,128)S(1)}, u32[]{:S(2)}, u32[]{:S(2)}) %all-to-all-start.2) | async-done | bytes 524320 | tf_op jit(solution)/shard_map/all_to_all | solution.py:424
  119.3 1.1 collective-permute-start.4
  120.6 0.9 fusion
  121.5 0.6 pad_maximum_fusion.1
  122.2 0.8 copy-done.7
  123.0 4.7 %lowered.1 = (f32[512,128]{1,0:T(8,128)}, f32[128,128]{1,0:T(8,128)}) custom-call(s32[3]{0:T(128)} %pad_add_fusion.where_ref, f32[8,128,128]{2,1,0:T(8,128)} %copy-done.5, f32[8,128,128]{2,1,0:T(8,128)} %copy-done.7, f32[512,2048]{1,0:T(8,128)} %vectors_ref.3, f32[512,128]{1,0:T(8,128)} %side_ref.3), custom_call_target="tpu_custom_call" | custom-call | flops 805306368 | bytes 4194304 | tf_op jit(solution)/shard_map/lowered/pallas_call | solution.py:154
  127.7 3.5 %collective-permute-start.5 = (f32[128,128]{1,0:T(8,128)}, f32[128,128]{1,0:T(8,128)S(1)}, u32[]{:S(2)}, u32[]{:S(2)}) collective-permute-start(f32[128,128]{1,0:T(8,128)} %get-tuple-element.32.upper_ref), channel_id=1, source_target_pairs={{0,16},{32,48},{64,80},{96,112},{128,144},{160,176},{192,208},{224... | collective-permute-start | bytes 196616 | tf_op jit(solution)/shard_map/ppermute | solution.py:395
  131.2 8.0 %joint.1 = (bf16[256,2048]{1,0:T(8,128)(2,1)S(1)}, bf16[256,2048]{1,0:T(8,128)(2,1)S(1)}) custom-call(s32[3]{0:T(128)S(1)} %copy-done.4, f32[128,2048]{1,0:T(8,128)} %bitcast.32, f32[16,1280,128]{2,1,0:T(8,128)} %bitcast.31), custom_call_target="tpu_custom_call" | custom-call | flops 1610612736 | bytes 5242880 | tf_op jit(solution)/shard_map/joint/pallas_call | solution.py:213
  139.2 1.1 level.4
  140.3 0.6 collective-permute-start.7
  140.9 1.5 collective-permute-done.7
  142.5 0.9 add.63
  143.3 3.5 %all-to-all-start.3 = ((f32[8,128,128]{2,1,0:T(8,128)}), f32[8,128,128]{2,1,0:T(8,128)S(1)}, u32[]{:S(2)}, u32[]{:S(2)}) async-start(f32[8,128,128]{2,1,0:T(8,128)} %add.63), calls=%async_computation.3 | async-start | bytes 1048576 | tf_op jit(solution)/shard_map/all_to_all | solution.py:417
  146.9 0.7 all-gather.9.cloned.1.call-update
  147.6 17.1 %all-to-all-done.3 = f32[8,128,128]{2,1,0:T(8,128)S(1)} async-done(((f32[8,128,128]{2,1,0:T(8,128)}), f32[8,128,128]{2,1,0:T(8,128)S(1)}, u32[]{:S(2)}, u32[]{:S(2)}) %all-to-all-start.3) | async-done | bytes 524320 | tf_op jit(solution)/shard_map/all_to_all | solution.py:417
  164.8 0.7 collective-permute-start.8
  165.5 0.7 collective-permute-start.9
  166.2 1.1 level.5
  167.3 0.6 collective-permute-start.10
  167.9 1.5 collective-permute-done.10
  169.5 21.8 %all_to_all.47 = f32[8,128,128]{2,1,0:T(8,128)S(1)} all-to-all(f32[8,128,128]{2,1,0:T(8,128)S(1)} %add.64), channel_id=1, replica_groups={{0,2,4,6,8,10,12,14},{1,3,5,7,9,11,13,15},{16,18,20,22,24,26,28,30},{17..., dimensions={0} | all-to-all | bytes 1048576 | tf_op jit(solution)/shard_map/all_to_all | solution.py:417
  191.3 0.7 collective-permute-start.11
  192.0 0.8 collective-permute-start.12
  193.2 1.2 copy-done
  194.4 0.9 fold.1
  195.3 1.1 level.6
  196.4 0.3 collective-permute-start.13
  196.8 1.7 collective-permute-done.13
  198.5 20.7 %all_to_all.48 = f32[8,128,128]{2,1,0:T(8,128)S(1)} all-to-all(f32[8,128,128]{2,1,0:T(8,128)S(1)} %add.65), channel_id=1, replica_groups={{0,2,4,6,8,10,12,14},{1,3,5,7,9,11,13,15},{16,18,20,22,24,26,28,30},{17..., dimensions={0} | all-to-all | bytes 1048576 | tf_op jit(solution)/shard_map/all_to_all | solution.py:417
  219.3 0.7 collective-permute-start.14
  220.0 0.7 collective-permute-start.15
  220.6 1.1 level.7
  221.8 1.1 collective-permute-start.16
  222.9 1.5 collective-permute-done.16
  224.4 0.9 add.66
  225.3 3.5 %all-to-all-start.6 = ((f32[8,128,128]{2,1,0:T(8,128)}), f32[8,128,128]{2,1,0:T(8,128)S(1)}, u32[]{:S(2)}, u32[]{:S(2)}) async-start(f32[8,128,128]{2,1,0:T(8,128)} %add.66), calls=%async_computation.6 | async-start | bytes 1048576 | tf_op jit(solution)/shard_map/all_to_all | solution.py:417
  228.8 17.9 %all-to-all-done.6 = f32[8,128,128]{2,1,0:T(8,128)S(1)} async-done(((f32[8,128,128]{2,1,0:T(8,128)}), f32[8,128,128]{2,1,0:T(8,128)S(1)}, u32[]{:S(2)}, u32[]{:S(2)}) %all-to-all-start.6) | async-done | bytes 524320 | tf_op jit(solution)/shard_map/all_to_all | solution.py:417
  246.8 1.3 collective-permute-start.17
  248.1 22.1 %all_to_all.49 = f32[16,8,128]{2,1,0:T(8,128)S(1)} all-to-all(f32[16,8,128]{2,1,0:T(8,128)S(1)} %bitcast.34), channel_id=1, replica_groups=mesh['rows'=16,'leaf'=16] {'rows'}, dimensions={0} | all-to-all | bytes 131072 | tf_op jit(solution)/shard_map/all_to_all | solution.py:498
  270.5 17.4 %all_to_all.50.own_ref = f32[8,136,128]{2,1,0:T(8,128)S(1)} all-to-all(f32[8,136,128]{2,1,0:T(8,128)S(1)} %broadcast_in_dim.41), channel_id=1, replica_groups={{0,2,4,6,8,10,12,14},{1,3,5,7,9,11,13,15},{16,18,20,22,24,26,28,30},{17..., dimensions={0} | all-to-all | bytes 1114112 | tf_op jit(solution)/shard_map/all_to_all | solution.py:424
  288.0 4.1 %collective-permute-start.18 = (f32[8,136,128]{2,1,0:T(8,128)S(1)}, f32[8,136,128]{2,1,0:T(8,128)S(1)}, u32[]{:S(2)}, u32[]{:S(2)}) collective-permute-start(f32[8,136,128]{2,1,0:T(8,128)S(1)} %all_to_all.50.own_ref), channel_id=1, source_target_pairs={{0,1},{1,0},{2,3},{3,2},{4,5},{5,4},{6,7},{7,6},{8,9},{9,8},{10,11... | collective-permute-start | bytes 1671176 | tf_op jit(solution)/shard_map/ppermute | solution.py:395
  292.0 0.6 select_select_fusion.summit_ref
  292.7 1.0 collective-permute-done.18.other_ref
  293.6 0.8 copy-done.9
  294.4 9.5 %final.1 = (f32[512,128]{1,0:T(8,128)}, f32[8,128]{1,0:T(8,128)}) custom-call(s32[3]{0:T(128)} %pad_add_fusion.where_ref, f32[8,136,128]{2,1,0:T(8,128)} %copy-done.6, f32[8,136,128]{2,1,0:T(8,128)} %copy-done.9, f32[128,128]{1,0:T(8,128)} %select_select_fusion.summit_ref, f32[128,128]{1,0:T(8,128)} %copy-done.10, f32[128,2048]{1,0:T(8,128)} %bitcast.33, ...), custom_call_target="tpu_custom_call" | custom-call | flops 4294967296 | bytes 8912896 | tf_op jit(solution)/shard_map/final/pallas_call | solution.py:371
  (59 shorter events, 1.4 us)
Async XLA Ops:
  7.2 83.5 %copy-start.1 = (f32[1,2048,128]{2,1,0:T(8,128)S(1)}, f32[1,2048,128]{2,1,0:T(8,128)}, u32[]{:S(2)}) copy-start(f32[1,2048,128]{2,1,0:T(8,128)} %param.9) | copy-start | bytes 3145732
  7.2 88.9 %copy-start.8 = (f32[128,128]{1,0:T(8,128)S(1)}, f32[128,128]{1,0:T(8,128)}, u32[]{:S(2)}) copy-start(f32[128,128]{1,0:T(8,128)} %param.13) | copy-start | bytes 196612
  7.2 124.0 %all-gather.7.cloned.1.call-start = ((), (), s32[]{:S(2)}) async-start(), calls=%async_computation.9 | async-start | bytes 11141120 | tf_op jit(solution)/shard_map/all_gather | solution.py:445
  8.3 22.1 %collective-permute-start = (f32[768,128]{1,0:T(8,128)S(1)}, f32[768,128]{1,0:T(8,128)S(1)}, u32[]{:S(2)}, u32[]{:S(2)}) collective-permute-start(f32[768,128]{1,0:T(8,128)S(1)} %slice_bitcast_fusion), channel_id=1, source_target_pairs={{14,0},{15,1},{30,16},{31,17},{46,32},{47,33},{62,48},{63,49},{78,... | collective-permute-start | bytes 1179656 | tf_op jit(solution)/shard_map/ppermute | solution.py:395
  10.6 5.1 %collective-permute-start.1 = (f32[512,128]{1,0:T(8,128)S(1)}, f32[512,128]{1,0:T(8,128)S(1)}, u32[]{:S(2)}, u32[]{:S(2)}) collective-permute-start(f32[512,128]{1,0:T(8,128)S(1)} %slice_bitcast_fusion.1), channel_id=1, source_target_pairs={{10,6},{11,7},{12,4},{13,5},{26,22},{27,23},{28,20},{29,21},{42,38... | collective-permute-start | bytes 786440 | tf_op jit(solution)/shard_map/ppermute | solution.py:395
  12.0 78.6 %copy-start.3 = (s32[3]{0:T(128)S(1)}, s32[3]{0:T(128)}, u32[]{:S(2)}) copy-start(s32[3]{0:T(128)} %pad_add_fusion.where_ref) | copy-start | bytes 40
  15.7 115.5 %copy-start.4 = (s32[3]{0:T(128)S(1)}, s32[3]{0:T(128)}, u32[]{:S(2)}) copy-start(s32[3]{0:T(128)} %pad_add_fusion.where_ref) | copy-start | bytes 40
  32.5 3.1 collective-permute-start.2
  87.5 3.1 collective-permute-start.3
  92.6 26.7 %all-to-all-start.2 = ((f32[8,128,128]{2,1,0:T(8,128)}), f32[8,128,128]{2,1,0:T(8,128)S(1)}, u32[]{:S(2)}, u32[]{:S(2)}) async-start(f32[8,128,128]{2,1,0:T(8,128)} %coeffs.1), calls=%async_computation.2 | async-start | bytes 1048576 | tf_op jit(solution)/shard_map/all_to_all | solution.py:424
  96.1 24.3 %collective-permute-start.6 = (f32[128,128]{1,0:T(8,128)S(1)}, f32[128,128]{1,0:T(8,128)S(1)}, u32[]{:S(2)}, u32[]{:S(2)}) collective-permute-start(f32[128,128]{1,0:T(8,128)S(1)} %copy-done.8), channel_id=1, source_target_pairs={{1,0},{3,2},{5,4},{7,6},{9,8},{11,10},{13,12},{15,14},{17,16},{19,... | collective-permute-start | bytes 196616 | tf_op jit(solution)/shard_map/ppermute | solution.py:395
  119.3 2.8 copy-start.5
  119.3 2.8 collective-permute-start.4
  122.2 0.8 copy-start.7
  127.7 11.5 %copy-start.2 = (f32[128,128]{1,0:T(8,128)S(1)}, f32[128,128]{1,0:T(8,128)}, u32[]{:S(2)}) copy-start(f32[128,128]{1,0:T(8,128)} %get-tuple-element.32.upper_ref) | copy-start | bytes 196612
  127.7 11.5 %collective-permute-start.5 = (f32[128,128]{1,0:T(8,128)}, f32[128,128]{1,0:T(8,128)S(1)}, u32[]{:S(2)}, u32[]{:S(2)}) collective-permute-start(f32[128,128]{1,0:T(8,128)} %get-tuple-element.32.upper_ref), channel_id=1, source_target_pairs={{0,16},{32,48},{64,80},{96,112},{128,144},{160,176},{192,208},{224... | collective-permute-start | bytes 196616 | tf_op jit(solution)/shard_map/ppermute | solution.py:395
  140.3 2.1 collective-permute-start.7
  143.3 21.4 %all-to-all-start.3 = ((f32[8,128,128]{2,1,0:T(8,128)}), f32[8,128,128]{2,1,0:T(8,128)S(1)}, u32[]{:S(2)}, u32[]{:S(2)}) async-start(f32[8,128,128]{2,1,0:T(8,128)} %add.63), calls=%async_computation.3 | async-start | bytes 1048576 | tf_op jit(solution)/shard_map/all_to_all | solution.py:417
  146.8 46.3 %all-gather.9.cloned.1.call-start = ((), (), s32[]{:S(2)}) async-start(), calls=%async_computation.10 | async-start | bytes 1183744 | tf_op jit(solution)/shard_map/all_gather | solution.py:485
  147.6 146.0 %all-gather.11.cloned.1.call-start = ((), (), s32[]{:S(2)}) async-start(), calls=%async_computation.11 | async-start | bytes 9469952 | tf_op jit(solution)/shard_map/all_gather | solution.py:481
  164.8 1.3 collective-permute-start.8
  165.5 0.7 collective-permute-start.9
  167.3 2.1 collective-permute-start.10
  191.3 4.0 %collective-permute-start.11 = (f32[128,128]{1,0:T(8,128)S(1)}, f32[128,128]{1,0:T(8,128)S(1)}, u32[]{:S(2)}, u32[]{:S(2)}) collective-permute-start(f32[128,128]{1,0:T(8,128)S(1)} %sub.13), channel_id=1, source_target_pairs={{96,64},{224,192},{97,65},{225,193},{98,66},{226,194},{99,67},{227... | collective-permute-start | bytes 196616 | tf_op jit(solution)/shard_map/ppermute | solution.py:395
  192.0 3.3 %collective-permute-start.12 = (f32[128,128]{1,0:T(8,128)S(1)}, f32[128,128]{1,0:T(8,128)S(1)}, u32[]{:S(2)}, u32[]{:S(2)}) collective-permute-start(f32[128,128]{1,0:T(8,128)S(1)} %sub.13), channel_id=1, source_target_pairs={{32,64},{160,192},{33,65},{161,193},{34,66},{162,194},{35,67},{163... | collective-permute-start | bytes 196616 | tf_op jit(solution)/shard_map/ppermute | solution.py:395
  193.2 1.2 copy-start
  196.4 2.0 collective-permute-start.13
  219.3 1.3 collective-permute-start.14
  220.0 0.7 collective-permute-start.15
  221.8 2.7 collective-permute-start.16
  225.3 21.4 %all-to-all-start.6 = ((f32[8,128,128]{2,1,0:T(8,128)}), f32[8,128,128]{2,1,0:T(8,128)S(1)}, u32[]{:S(2)}, u32[]{:S(2)}) async-start(f32[8,128,128]{2,1,0:T(8,128)} %add.66), calls=%async_computation.6 | async-start | bytes 1048576 | tf_op jit(solution)/shard_map/all_to_all | solution.py:417
  246.8 23.5 %collective-permute-start.17 = (f32[128,128]{1,0:T(8,128)S(1)}, f32[128,128]{1,0:T(8,128)S(1)}, u32[]{:S(2)}, u32[]{:S(2)}) collective-permute-start(f32[128,128]{1,0:T(8,128)S(1)} %get-tuple-element.57), channel_id=1, source_target_pairs={{128,0},{129,1},{130,2},{131,3},{132,4},{133,5},{134,6},{135,7},{1... | collective-permute-start | bytes 196616 | tf_op jit(solution)/shard_map/ppermute | solution.py:395
  270.3 23.3 %copy-start.10 = (f32[128,128]{1,0:T(8,128)}, f32[128,128]{1,0:T(8,128)S(1)}, u32[]{:S(2)}) copy-start(f32[128,128]{1,0:T(8,128)S(1)} %collective-permute-done.17.back_ref) | copy-start | bytes 196612
  288.0 5.7 %copy-start.6 = (f32[8,136,128]{2,1,0:T(8,128)}, f32[8,136,128]{2,1,0:T(8,128)S(1)}, u32[]{:S(2)}) copy-start(f32[8,136,128]{2,1,0:T(8,128)S(1)} %all_to_all.50.own_ref) | copy-start | bytes 1671172
  288.0 5.7 %collective-permute-start.18 = (f32[8,136,128]{2,1,0:T(8,128)S(1)}, f32[8,136,128]{2,1,0:T(8,128)S(1)}, u32[]{:S(2)}, u32[]{:S(2)}) collective-permute-start(f32[8,136,128]{2,1,0:T(8,128)S(1)} %all_to_all.50.own_ref), channel_id=1, source_target_pairs={{0,1},{1,0},{2,3},{3,2},{4,5},{5,4},{6,7},{7,6},{8,9},{9,8},{10,11... | collective-permute-start | bytes 1671176 | tf_op jit(solution)/shard_map/ppermute | solution.py:395
  293.6 0.8 copy-start.9
Sparse Core Ops, SparseCore 0:
  32.6 95.2 all-gather.6
  150.1 43.0 all-gather.8
  195.7 83.0 all-gather.10

commit v6 on v5

--- a/solution.py
+++ b/solution.py
@@ -126,42 +126,54 @@
     )(where, own, other, factor)
 
 
-def lowered_kernel(where_ref, own_ref, other_ref, vectors_ref, side_ref, out_ref, top_ref):
-    step = pl.program_id(0)
-
+def lowered_step(step, where_ref, own_ref, other_ref, vectors_ref, side_ref, sum_ref):
     @pl.when(step == 0)
     def _():
-        out_ref[...] = side_ref[...]
-
-    total = out_ref[...]
+        sum_ref[...] = side_ref[...]
+
+    total = sum_ref[...]
     for n in range(own_ref.shape[0]):
         right = jnp.concatenate(pick(where_ref[0], own_ref[n], other_ref[n]), axis=0)
         vectors = vectors_ref[:, 2 * n * SIDE:(2 * n + 2) * SIDE]
-        total = total - thrice(halves(vectors), halves(right))
-    out_ref[...] = total
-
-    @pl.when(step == pl.num_programs(0) - 1)
+        total = total - stacked(halves(vectors), halves(right))
+    sum_ref[...] = total
+
+
+def top_kernel(where_ref, own_ref, other_ref, vectors_ref, side_ref, top_ref, sum_ref):
+    step = pl.program_id(1)
+    lowered_step(step, where_ref, own_ref, other_ref, vectors_ref, side_ref, sum_ref)
+
+    @pl.when(step == pl.num_programs(1) - 1)
     def _():
-        top_ref[...] = out_ref[:SIDE, :].T
-
-
-def lowered_of(where, own, other, vectors, side):
-    tall, order = vectors.shape
+        top_ref[...] = sum_ref[...].T
+
+
+def rest_kernel(where_ref, own_ref, other_ref, vectors_ref, side_ref, out_ref):
+    step = pl.program_id(1)
+    lowered_step(step, where_ref, own_ref, other_ref, vectors_ref, side_ref, out_ref)
+
+
+def lowered_of(where, own, other, vectors, side, first, blocks):
+    order = vectors.shape[1]
     columns = side.shape[1]
     steps = order // (2 * SIDE)
-    block = pl.BlockSpec((GROUP, SIDE, columns), lambda n: (n, 0, 0))
-    whole = pl.BlockSpec((tall, columns), lambda n: (0, 0))
-    return pl.pallas_call(
-        lowered_kernel,
-        grid=(steps // GROUP,),
+    block = pl.BlockSpec((GROUP, SIDE, columns), lambda i, n: (n, 0, 0))
+    return pl.pallas_call(
+        rest_kernel if first else top_kernel,
+        grid=(blocks, steps // GROUP),
         in_specs=[
-            smem, block, block, pl.BlockSpec((tall, 2 * GROUP * SIDE), lambda n: (0, n)), whole,
+            smem,
+            block,
+            block,
+            pl.BlockSpec((SIDE, 2 * GROUP * SIDE), lambda i, n: (first + i, n)),
+            pl.BlockSpec((SIDE, columns), lambda i, n: (first + i, 0)),
         ],
-        out_specs=[whole, pl.BlockSpec((columns, SIDE), lambda n: (0, 0))],
-        out_shape=[shaped(tall, columns), shaped(columns, SIDE)],
+        out_specs=pl.BlockSpec((SIDE, columns), lambda i, n: (i, 0)),
+        out_shape=shaped(blocks * SIDE, columns),
+        scratch_shapes=[] if first else [pltpu.VMEM((SIDE, columns), jnp.float32)],
         compiler_params=params(LARGE),
-        cost_estimate=cost(6 * tall * columns * order, 4 * vectors.size),
-        name="lowered",
+        cost_estimate=cost(6 * blocks * SIDE * columns * order, 4 * blocks * SIDE * order),
+        name="lowered_rest" if first else "lowered_top",
     )(where, own, other, vectors, side)
 
 
@@ -288,8 +300,8 @@
         )
         copy.start()
         copies.append(copy)
-    rest = pl.ds(SIDE, rotated_ref.shape[0] - SIDE)
-    rest_copy = pltpu.make_async_copy(rotated_ref.at[rest], out_ref.at[rest], out_sems.at[0])
+    rest = pl.ds(SIDE, rotated_ref.shape[0])
+    rest_copy = pltpu.make_async_copy(rotated_ref, out_ref.at[rest], out_sems.at[0])
     rest_copy.start()
     for n in range(steps):
         for k, value in enumerate(pick(parity, own_ref[n], other_ref[n])):
@@ -372,7 +384,7 @@
         final_kernel,
         in_specs=[smem] + [vmem] * 5 + [hbm] * 2,
         out_specs=[hbm, vmem],
-        out_shape=[shaped(*rotated.shape), shaped(narrow, SIDE)],
+        out_shape=[shaped(rotated.shape[0] + SIDE, columns), shaped(narrow, SIDE)],
         scratch_shapes=[
             pltpu.VMEM((order, columns), jnp.float32),
             pltpu.VMEM((narrow, order), jnp.float32),
@@ -447,7 +459,9 @@
     )
     weights_part = scatter_pair(pair_sum((keep, give)))
     spread = coeffs_of(where, *collect(copies(weights_part)), leaf_factor[0])
-    rotated, top = lowered_of(where, *collect(spread), reflectors, right_side)
+    coeffs = collect(spread)
+    top = lowered_of(where, *coeffs, reflectors, right_side, 0, 1)
+    rest = lowered_of(where, *coeffs, reflectors, right_side, 1, right_side.shape[0] // block - 1)
 
     upper_own, inverse_own = upper_blocks, block_inverse
     inverse_next = moved(inverse_own, "leaf", [(i + 1, i) for i in range(0, count, 2)])
@@ -479,6 +493,8 @@
         if stride == 4:
             upper, lower, folded = lax.optimization_barrier((upper, lower, folded))
             folded = lax.all_gather(folded, "rows", axis=0)
+        if 2 * stride == rows:
+            upper, lower, rest = lax.optimization_barrier((upper, lower, rest))
         parts = level_of(where, upper, lower, joint)
         if stride == 1:
             upper_slice, parts = lax.optimization_barrier((upper_slice, parts))
@@ -499,7 +515,7 @@
     arrived, back = lax.optimization_barrier((arrived, back))
     own, other = collect(copies(jnp.concatenate([own_coeffs.T, arrived], axis=0)))
     rotated, solved = final_of(
-        where, own, other, own_top, back, node_reflect[0], rotated, folded
+        where, own, other, own_top, back, node_reflect[0], rest, folded
     )
     return (rotated, solved.T)
 

time: 312 us -> 313 us (level)
  Pallas kernels: 33.3 us -> 37.5 us
  blocking collectives: 133 us -> 129 us
    pallas_call x1 -> x2, Pallas kernels: 4.74 us -> 8.97 us  [lowered_of(): pl.pallas_call(rest_kernel if first else top_kernel, grid=(blocks, steps...]
    all_to_all x1, blocking collectives: 22.1 us -> 18.6 us  [per_device(): arrived = lax.all_to_all(pieces, 'rows', 0, 0)[root]]
  transfers between devices with their start and end apart: 25 -> 25, of which waited for: 12 -> 11; matrix products, arithmetic and copies ran while one was open for 2% -> 2% of each run, Pallas kernels for 7% -> 9%
where the time goes in v6:
time: 313 us; the launch traced here: 311 us
  blocking collectives  129 us (41%)
  waiting for transfers between devices  80.8 us (26%)
  Pallas kernels  37.5 us (12%)
  starting transfers between devices  34.7 us (11%)
  between operations  14.3 us (5%)
  other arithmetic  8.16 us (3%)
  local copies, waits for them, and re-layouts  5.24 us (2%)
    all_to_all x3, blocking collectives, scatter_pair(): got = lax.all_to_all(pair, 'leaf', 0, 0, axis_index_groups=same)  68 us
    all_to_all x2, blocking collectives, collect(): own = lax.all_to_all(spread, 'leaf', 0, 0, axis_index_groups=same)  42.9 us
    all_to_all x2, waiting for transfers between devices, scatter_pair(): got = lax.all_to_all(pair, 'leaf', 0, 0, axis_index_groups=same)  35 us
    ppermute x19, waiting for transfers between devices, moved(): return lax.ppermute(value, axis, pairs)  25.1 us
    ppermute x19, starting transfers between devices, moved(): return lax.ppermute(value, axis, pairs)  24.1 us
    all_to_all x1, waiting for transfers between devices, collect(): own = lax.all_to_all(spread, 'leaf', 0, 0, axis_index_groups=same)  19.9 us
    all_to_all x1, blocking collectives, per_device(): arrived = lax.all_to_all(pieces, 'rows', 0, 0)[root]  18.6 us
    pallas_call x1, Pallas kernels, final_of(): pl.pallas_call(final_kernel, in_specs=[smem] + [vmem] * 5 + [hbm] * 2, ou...  9.49 us
  transfers between devices with their start and end apart: 25, of which 11 were waited for; matrix products, arithmetic and copies ran while one was open for 2% of the time, Pallas kernels for 9%

profile of v6, /device:TPU:1, one launch (start us, length us, event | category | flops | bytes accessed | tf_op | source)
XLA Modules:
  0.0 311.3 jit_solution(4124579240767824081)
XLA Ops:
  7.2 1.1 slice_bitcast_fusion
  8.3 1.3 collective-permute-start
  9.6 1.0 slice_bitcast_fusion.1
  10.6 0.7 collective-permute-start.1
  11.3 0.7 pad_add_fusion.where_ref
  12.0 3.8 %weights.1 = (f32[8,128,128]{2,1,0:T(8,128)}, f32[8,128,128]{2,1,0:T(8,128)}) custom-call(s32[3]{0:T(128)} %pad_add_fusion.where_ref, f32[512,128]{1,0:T(8,128)} %side_ref.5, f32[512,2048]{1,0:T(8,128)} %vectors_ref.5), custom_call_target="tpu_custom_call" | custom-call | flops 805306368 | bytes 4194304 | tf_op jit(solution)/shard_map/weights/pallas_call | solution.py:88
  15.7 14.7 %collective-permute-done = f32[768,128]{1,0:T(8,128)S(1)} collective-permute-done((f32[768,128]{1,0:T(8,128)S(1)}, f32[768,128]{1,0:T(8,128)S(1)}, u32[]{:S(2)}, u32[]{:S(2)}) %collective-permute-start) | collective-permute-done | bytes 393248 | tf_op jit(solution)/shard_map/ppermute | solution.py:407
  30.5 2.0 bitcast_add_fusion
  32.5 1.3 collective-permute-start.2
  33.9 1.7 collective-permute-done.2
  35.6 1.1 add.57
  36.7 25.3 %all_to_all.45 = f32[8,128,128]{2,1,0:T(8,128)S(1)} all-to-all(f32[8,128,128]{2,1,0:T(8,128)S(1)} %add.57), channel_id=1, replica_groups={{0,2,4,6,8,10,12,14},{1,3,5,7,9,11,13,15},{16,18,20,22,24,26,28,30},{17..., dimensions={0} | all-to-all | bytes 1048576 | tf_op jit(solution)/shard_map/all_to_all | solution.py:429
  62.1 25.4 %all_to_all.46.own_ref = f32[8,128,128]{2,1,0:T(8,128)S(1)} all-to-all(f32[8,128,128]{2,1,0:T(8,128)S(1)} %broadcast_in_dim.36), channel_id=1, replica_groups={{0,2,4,6,8,10,12,14},{1,3,5,7,9,11,13,15},{16,18,20,22,24,26,28,30},{17..., dimensions={0} | all-to-all | bytes 1048576 | tf_op jit(solution)/shard_map/all_to_all | solution.py:436
  87.6 1.6 collective-permute-start.3
  89.1 1.5 collective-permute-done.3.other_ref
  90.7 2.0 coeffs.1
  92.7 3.5 %all-to-all-start.2 = ((f32[8,128,128]{2,1,0:T(8,128)}), f32[8,128,128]{2,1,0:T(8,128)S(1)}, u32[]{:S(2)}, u32[]{:S(2)}) async-start(f32[8,128,128]{2,1,0:T(8,128)} %coeffs.1), calls=%async_computation.2 | async-start | bytes 1048576 | tf_op jit(solution)/shard_map/all_to_all | solution.py:436
  96.2 2.3 collective-permute-start.6
  98.5 1.0 fusion.1
  99.5 19.9 %all-to-all-done.2.own_ref = f32[8,128,128]{2,1,0:T(8,128)S(1)} async-done(((f32[8,128,128]{2,1,0:T(8,128)}), f32[8,128,128]{2,1,0:T(8,128)S(1)}, u32[]{:S(2)}, u32[]{:S(2)}) %all-to-all-start.2) | async-done | bytes 524320 | tf_op jit(solution)/shard_map/all_to_all | solution.py:436
  119.4 1.1 collective-permute-start.4
  120.6 0.9 fusion
  121.6 0.6 pad_maximum_fusion.1
  122.2 0.8 copy-done.7
  123.0 2.8 lowered_top.1.upper_ref
  125.8 3.5 %collective-permute-start.5 = (f32[128,128]{1,0:T(8,128)}, f32[128,128]{1,0:T(8,128)S(1)}, u32[]{:S(2)}, u32[]{:S(2)}) collective-permute-start(f32[128,128]{1,0:T(8,128)} %lowered_top.1.upper_ref), channel_id=1, source_target_pairs={{0,16},{32,48},{64,80},{96,112},{128,144},{160,176},{192,208},{224... | collective-permute-start | bytes 196616 | tf_op jit(solution)/shard_map/ppermute | solution.py:407
  129.3 8.0 %joint.1 = (bf16[256,2048]{1,0:T(8,128)(2,1)S(1)}, bf16[256,2048]{1,0:T(8,128)(2,1)S(1)}) custom-call(s32[3]{0:T(128)S(1)} %copy-done.4, f32[128,2048]{1,0:T(8,128)} %bitcast.32, f32[16,1280,128]{2,1,0:T(8,128)} %bitcast.31), custom_call_target="tpu_custom_call" | custom-call | flops 1610612736 | bytes 5242880 | tf_op jit(solution)/shard_map/joint/pallas_call | solution.py:225
  137.3 1.1 level.4
  138.5 0.6 collective-permute-start.7
  139.1 1.5 collective-permute-done.7
  140.6 0.9 add.63
  141.5 3.5 %all-to-all-start.3 = ((f32[8,128,128]{2,1,0:T(8,128)}), f32[8,128,128]{2,1,0:T(8,128)S(1)}, u32[]{:S(2)}, u32[]{:S(2)}) async-start(f32[8,128,128]{2,1,0:T(8,128)} %add.63), calls=%async_computation.3 | async-start | bytes 1048576 | tf_op jit(solution)/shard_map/all_to_all | solution.py:429
  145.0 0.7 all-gather.9.cloned.1.call-update
  145.8 17.1 %all-to-all-done.3 = f32[8,128,128]{2,1,0:T(8,128)S(1)} async-done(((f32[8,128,128]{2,1,0:T(8,128)}), f32[8,128,128]{2,1,0:T(8,128)S(1)}, u32[]{:S(2)}, u32[]{:S(2)}) %all-to-all-start.3) | async-done | bytes 524320 | tf_op jit(solution)/shard_map/all_to_all | solution.py:429
  162.9 0.7 collective-permute-start.8
  163.6 0.7 collective-permute-start.9
  164.3 1.1 level.5
  166.0 1.5 collective-permute-done.10
  167.6 21.7 %all_to_all.47 = f32[8,128,128]{2,1,0:T(8,128)S(1)} all-to-all(f32[8,128,128]{2,1,0:T(8,128)S(1)} %add.64), channel_id=1, replica_groups={{0,2,4,6,8,10,12,14},{1,3,5,7,9,11,13,15},{16,18,20,22,24,26,28,30},{17..., dimensions={0} | all-to-all | bytes 1048576 | tf_op jit(solution)/shard_map/all_to_all | solution.py:429
  189.4 0.7 collective-permute-start.11
  190.1 0.7 collective-permute-start.12
  190.8 1.2 copy-done
  192.0 0.8 fold.1
  192.9 1.1 level.6
  194.0 0.9 collective-permute-start.13
  194.9 1.5 collective-permute-done.13
  196.5 21.0 %all_to_all.48 = f32[8,128,128]{2,1,0:T(8,128)S(1)} all-to-all(f32[8,128,128]{2,1,0:T(8,128)S(1)} %add.65), channel_id=1, replica_groups={{0,2,4,6,8,10,12,14},{1,3,5,7,9,11,13,15},{16,18,20,22,24,26,28,30},{17..., dimensions={0} | all-to-all | bytes 1048576 | tf_op jit(solution)/shard_map/all_to_all | solution.py:429
  217.6 0.7 collective-permute-start.14
  218.2 0.7 collective-permute-start.15
  218.9 6.2 %lowered_rest.1.rotated_ref = f32[384,128]{1,0:T(8,128)} custom-call(s32[3]{0:T(128)} %pad_add_fusion.where_ref, f32[8,128,128]{2,1,0:T(8,128)} %copy-done.6, f32[8,128,128]{2,1,0:T(8,128)} %copy-done.7, f32[512,2048]{1,0:T(8,128)} %vectors_ref.5, f32[512,128]{1,0:T(8,128)} %side_ref.5), custom_call_target="tpu_custom_call" | custom-call | flops 603979776 | bytes 3145728 | tf_op jit(solution)/shard_map/lowered_rest/pallas_call | solution.py:161
  225.1 1.1 level.7
  226.2 1.1 collective-permute-start.16
  227.3 1.5 collective-permute-done.16
  228.9 0.9 add.66
  229.7 3.5 %all-to-all-start.6 = ((f32[8,128,128]{2,1,0:T(8,128)}), f32[8,128,128]{2,1,0:T(8,128)S(1)}, u32[]{:S(2)}, u32[]{:S(2)}) async-start(f32[8,128,128]{2,1,0:T(8,128)} %add.66), calls=%async_computation.6 | async-start | bytes 1048576 | tf_op jit(solution)/shard_map/all_to_all | solution.py:429
  233.3 17.9 %all-to-all-done.6 = f32[8,128,128]{2,1,0:T(8,128)S(1)} async-done(((f32[8,128,128]{2,1,0:T(8,128)}), f32[8,128,128]{2,1,0:T(8,128)S(1)}, u32[]{:S(2)}, u32[]{:S(2)}) %all-to-all-start.6) | async-done | bytes 524320 | tf_op jit(solution)/shard_map/all_to_all | solution.py:429
  251.2 1.3 collective-permute-start.17
  252.5 18.6 %all_to_all.49 = f32[16,8,128]{2,1,0:T(8,128)S(1)} all-to-all(f32[16,8,128]{2,1,0:T(8,128)S(1)} %bitcast.34), channel_id=1, replica_groups=mesh['rows'=16,'leaf'=16] {'rows'}, dimensions={0} | all-to-all | bytes 131072 | tf_op jit(solution)/shard_map/all_to_all | solution.py:514
  271.4 17.5 %all_to_all.50.own_ref = f32[8,136,128]{2,1,0:T(8,128)S(1)} all-to-all(f32[8,136,128]{2,1,0:T(8,128)S(1)} %broadcast_in_dim.41), channel_id=1, replica_groups={{0,2,4,6,8,10,12,14},{1,3,5,7,9,11,13,15},{16,18,20,22,24,26,28,30},{17..., dimensions={0} | all-to-all | bytes 1114112 | tf_op jit(solution)/shard_map/all_to_all | solution.py:436
  288.8 4.1 %collective-permute-start.18 = (f32[8,136,128]{2,1,0:T(8,128)S(1)}, f32[8,136,128]{2,1,0:T(8,128)S(1)}, u32[]{:S(2)}, u32[]{:S(2)}) collective-permute-start(f32[8,136,128]{2,1,0:T(8,128)S(1)} %all_to_all.50.own_ref), channel_id=1, source_target_pairs={{0,1},{1,0},{2,3},{3,2},{4,5},{5,4},{6,7},{7,6},{8,9},{9,8},{10,11... | collective-permute-start | bytes 1671176 | tf_op jit(solution)/shard_map/ppermute | solution.py:407
  292.9 0.6 select_select_fusion.summit_ref
  293.5 0.9 collective-permute-done.18.other_ref
  294.5 0.8 copy-done.10
  295.3 9.5 %final.1 = (f32[512,128]{1,0:T(8,128)}, f32[8,128]{1,0:T(8,128)}) custom-call(s32[3]{0:T(128)} %pad_add_fusion.where_ref, f32[8,136,128]{2,1,0:T(8,128)} %copy-done.8, f32[8,136,128]{2,1,0:T(8,128)} %copy-done.10, f32[128,128]{1,0:T(8,128)} %select_select_fusion.summit_ref, f32[128,128]{1,0:T(8,128)} %copy-done.11, f32[128,2048]{1,0:T(8,128)} %bitcast.33, ...), custom_call_target="tpu_custom_call" | custom-call | flops 4294967296 | bytes 8912896 | tf_op jit(solution)/shard_map/final/pallas_call | solution.py:383
  (62 shorter events, 1.7 us)
Async XLA Ops:
  7.2 83.5 %copy-start.1 = (f32[1,2048,128]{2,1,0:T(8,128)S(1)}, f32[1,2048,128]{2,1,0:T(8,128)}, u32[]{:S(2)}) copy-start(f32[1,2048,128]{2,1,0:T(8,128)} %param.9) | copy-start | bytes 3145732
  7.2 89.0 %copy-start.9 = (f32[128,128]{1,0:T(8,128)S(1)}, f32[128,128]{1,0:T(8,128)}, u32[]{:S(2)}) copy-start(f32[128,128]{1,0:T(8,128)} %param.13) | copy-start | bytes 196612
  7.2 122.1 %all-gather.7.cloned.1.call-start = ((), (), s32[]{:S(2)}) async-start(), calls=%async_computation.9 | async-start | bytes 11141120 | tf_op jit(solution)/shard_map/all_gather | solution.py:457
  8.3 22.1 %collective-permute-start = (f32[768,128]{1,0:T(8,128)S(1)}, f32[768,128]{1,0:T(8,128)S(1)}, u32[]{:S(2)}, u32[]{:S(2)}) collective-permute-start(f32[768,128]{1,0:T(8,128)S(1)} %slice_bitcast_fusion), channel_id=1, source_target_pairs={{14,0},{15,1},{30,16},{31,17},{46,32},{47,33},{62,48},{63,49},{78,... | collective-permute-start | bytes 1179656 | tf_op jit(solution)/shard_map/ppermute | solution.py:407
  10.6 5.1 %collective-permute-start.1 = (f32[512,128]{1,0:T(8,128)S(1)}, f32[512,128]{1,0:T(8,128)S(1)}, u32[]{:S(2)}, u32[]{:S(2)}) collective-permute-start(f32[512,128]{1,0:T(8,128)S(1)} %slice_bitcast_fusion.1), channel_id=1, source_target_pairs={{10,6},{11,7},{12,4},{13,5},{26,22},{27,23},{28,20},{29,21},{42,38... | collective-permute-start | bytes 786440 | tf_op jit(solution)/shard_map/ppermute | solution.py:407
  12.0 78.7 %copy-start.3 = (s32[3]{0:T(128)S(1)}, s32[3]{0:T(128)}, u32[]{:S(2)}) copy-start(s32[3]{0:T(128)} %pad_add_fusion.where_ref) | copy-start | bytes 40
  15.7 113.6 %copy-start.4 = (s32[3]{0:T(128)S(1)}, s32[3]{0:T(128)}, u32[]{:S(2)}) copy-start(s32[3]{0:T(128)} %pad_add_fusion.where_ref) | copy-start | bytes 40
  32.5 3.1 collective-permute-start.2
  87.6 3.1 collective-permute-start.3
  92.7 26.7 %all-to-all-start.2 = ((f32[8,128,128]{2,1,0:T(8,128)}), f32[8,128,128]{2,1,0:T(8,128)S(1)}, u32[]{:S(2)}, u32[]{:S(2)}) async-start(f32[8,128,128]{2,1,0:T(8,128)} %coeffs.1), calls=%async_computation.2 | async-start | bytes 1048576 | tf_op jit(solution)/shard_map/all_to_all | solution.py:436
  96.2 24.3 %collective-permute-start.6 = (f32[128,128]{1,0:T(8,128)S(1)}, f32[128,128]{1,0:T(8,128)S(1)}, u32[]{:S(2)}, u32[]{:S(2)}) collective-permute-start(f32[128,128]{1,0:T(8,128)S(1)} %copy-done.9), channel_id=1, source_target_pairs={{1,0},{3,2},{5,4},{7,6},{9,8},{11,10},{13,12},{15,14},{17,16},{19,... | collective-permute-start | bytes 196616 | tf_op jit(solution)/shard_map/ppermute | solution.py:407
  119.4 2.8 copy-start.6
  119.4 2.8 collective-permute-start.4
  122.2 0.8 copy-start.7
  125.8 11.5 %copy-start.2 = (f32[128,128]{1,0:T(8,128)S(1)}, f32[128,128]{1,0:T(8,128)}, u32[]{:S(2)}) copy-start(f32[128,128]{1,0:T(8,128)} %lowered_top.1.upper_ref) | copy-start | bytes 196612
  125.8 11.5 %collective-permute-start.5 = (f32[128,128]{1,0:T(8,128)}, f32[128,128]{1,0:T(8,128)S(1)}, u32[]{:S(2)}, u32[]{:S(2)}) collective-permute-start(f32[128,128]{1,0:T(8,128)} %lowered_top.1.upper_ref), channel_id=1, source_target_pairs={{0,16},{32,48},{64,80},{96,112},{128,144},{160,176},{192,208},{224... | collective-permute-start | bytes 196616 | tf_op jit(solution)/shard_map/ppermute | solution.py:407
  138.5 2.1 collective-permute-start.7
  141.5 21.4 %all-to-all-start.3 = ((f32[8,128,128]{2,1,0:T(8,128)}), f32[8,128,128]{2,1,0:T(8,128)S(1)}, u32[]{:S(2)}, u32[]{:S(2)}) async-start(f32[8,128,128]{2,1,0:T(8,128)} %add.63), calls=%async_computation.3 | async-start | bytes 1048576 | tf_op jit(solution)/shard_map/all_to_all | solution.py:429
  145.0 45.8 %all-gather.9.cloned.1.call-start = ((), (), s32[]{:S(2)}) async-start(), calls=%async_computation.10 | async-start | bytes 1183744 | tf_op jit(solution)/shard_map/all_gather | solution.py:501
  145.7 148.8 %all-gather.11.cloned.1.call-start = ((), (), s32[]{:S(2)}) async-start(), calls=%async_computation.11 | async-start | bytes 9469952 | tf_op jit(solution)/shard_map/all_gather | solution.py:495
  162.9 1.3 collective-permute-start.8
  163.6 0.7 collective-permute-start.9
  165.4 59.7 %copy-start.5 = (s32[3]{0:T(128)S(1)}, s32[3]{0:T(128)}, u32[]{:S(2)}) copy-start(s32[3]{0:T(128)} %pad_add_fusion.where_ref) | copy-start | bytes 40
  165.5 2.1 collective-permute-start.10
  189.4 3.5 %collective-permute-start.11 = (f32[128,128]{1,0:T(8,128)S(1)}, f32[128,128]{1,0:T(8,128)S(1)}, u32[]{:S(2)}, u32[]{:S(2)}) collective-permute-start(f32[128,128]{1,0:T(8,128)S(1)} %sub.13), channel_id=1, source_target_pairs={{96,64},{224,192},{97,65},{225,193},{98,66},{226,194},{99,67},{227... | collective-permute-start | bytes 196616 | tf_op jit(solution)/shard_map/ppermute | solution.py:407
  190.1 2.8 collective-permute-start.12
  190.8 1.2 copy-start
  194.0 2.4 collective-permute-start.13
  217.6 7.5 %collective-permute-start.14 = (f32[128,128]{1,0:T(8,128)S(1)}, f32[128,128]{1,0:T(8,128)S(1)}, u32[]{:S(2)}, u32[]{:S(2)}) collective-permute-start(f32[128,128]{1,0:T(8,128)S(1)} %sub.14), channel_id=1, source_target_pairs={{192,128},{193,129},{194,130},{195,131},{196,132},{197,133},{198,1... | collective-permute-start | bytes 196616 | tf_op jit(solution)/shard_map/ppermute | solution.py:407
  218.2 6.9 %collective-permute-start.15 = (f32[128,128]{1,0:T(8,128)S(1)}, f32[128,128]{1,0:T(8,128)S(1)}, u32[]{:S(2)}, u32[]{:S(2)}) collective-permute-start(f32[128,128]{1,0:T(8,128)S(1)} %sub.14), channel_id=1, source_target_pairs={{64,128},{65,129},{66,130},{67,131},{68,132},{69,133},{70,134},{71... | collective-permute-start | bytes 196616 | tf_op jit(solution)/shard_map/ppermute | solution.py:407
  226.2 2.6 collective-permute-start.16
  229.7 21.4 %all-to-all-start.6 = ((f32[8,128,128]{2,1,0:T(8,128)}), f32[8,128,128]{2,1,0:T(8,128)S(1)}, u32[]{:S(2)}, u32[]{:S(2)}) async-start(f32[8,128,128]{2,1,0:T(8,128)} %add.66), calls=%async_computation.6 | async-start | bytes 1048576 | tf_op jit(solution)/shard_map/all_to_all | solution.py:429
  251.2 20.0 %collective-permute-start.17 = (f32[128,128]{1,0:T(8,128)S(1)}, f32[128,128]{1,0:T(8,128)S(1)}, u32[]{:S(2)}, u32[]{:S(2)}) collective-permute-start(f32[128,128]{1,0:T(8,128)S(1)} %get-tuple-element.59), channel_id=1, source_target_pairs={{128,0},{129,1},{130,2},{131,3},{132,4},{133,5},{134,6},{135,7},{1... | collective-permute-start | bytes 196616 | tf_op jit(solution)/shard_map/ppermute | solution.py:407
  271.2 23.3 %copy-start.11 = (f32[128,128]{1,0:T(8,128)}, f32[128,128]{1,0:T(8,128)S(1)}, u32[]{:S(2)}) copy-start(f32[128,128]{1,0:T(8,128)S(1)} %collective-permute-done.17.back_ref) | copy-start | bytes 196612
  288.8 5.7 %copy-start.8 = (f32[8,136,128]{2,1,0:T(8,128)}, f32[8,136,128]{2,1,0:T(8,128)S(1)}, u32[]{:S(2)}) copy-start(f32[8,136,128]{2,1,0:T(8,128)S(1)} %all_to_all.50.own_ref) | copy-start | bytes 1671172
  288.8 5.6 %collective-permute-start.18 = (f32[8,136,128]{2,1,0:T(8,128)S(1)}, f32[8,136,128]{2,1,0:T(8,128)S(1)}, u32[]{:S(2)}, u32[]{:S(2)}) collective-permute-start(f32[8,136,128]{2,1,0:T(8,128)S(1)} %all_to_all.50.own_ref), channel_id=1, source_target_pairs={{0,1},{1,0},{2,3},{3,2},{4,5},{5,4},{6,7},{7,6},{8,9},{9,8},{10,11... | collective-permute-start | bytes 1671176 | tf_op jit(solution)/shard_map/ppermute | solution.py:407
  294.5 0.8 copy-start.10
Sparse Core Ops, SparseCore 0:
  32.7 95.3 all-gather.6
  148.2 41.9 all-gather.8
  193.0 83.9 all-gather.10
